TPU v7x, 32 devices: a whole 2x2x4 slice. The times are simulated.
32 devices in a mesh: dp: 8 (over y, x, core), tensor: 4 (over z).
Axes of the slice: x: 2, y: 2, z: 4, core: 2. Of those that a mesh axis runs over, the one named last changes fastest.
Arguments:
- tokens: bfloat16 [8, 1024, 2048], P('dp', None, 'tensor'), may hold values from -6 to 6
- cotangent: bfloat16 [8, 1024, 2048], P('dp', None, 'tensor'), may hold values from -6 to 6
- norm_gains: bfloat16 [2, 2048], replicated, may hold values from 0.5 to 1.5
- query_key_value_matrix: bfloat16 [3, 2048, 2048], P(None, None, 'tensor'), may hold values from -0.125 to 0.125
- output_matrix: bfloat16 [2048, 2048], P('tensor'), may hold values from -0.375 to 0.375
- gate_up_matrix: bfloat16 [2, 2048, 8192], P(None, None, 'tensor'), may hold values from -0.125 to 0.125
- down_matrix: bfloat16 [8192, 2048], P('tensor'), may hold values from -0.0625 to 0.0625
- lead_factors: bfloat16 [5, 4, 2048, 16], replicated, may hold values from -0.125 to 0.125
- head_factors: bfloat16 [3, 4, 16, 2048], P(None, None, None, 'tensor'), may hold values from -0.375 to 0.375
- unit_factors: bfloat16 [2, 4, 16, 8192], P(None, None, None, 'tensor'), may hold values from -0.375 to 0.375
- merge_factors: bfloat16 [4, 2048, 16], P(None, 'tensor'), may hold values from -0.375 to 0.375
- down_factors: bfloat16 [4, 8192, 16], P(None, 'tensor'), may hold values from -0.0625 to 0.0625
- tail_factors: bfloat16 [2, 4, 16, 2048], replicated, may hold values from -0.375 to 0.375
- doc_ids: int32 [8, 1024], P('dp'), may hold values from 0 to 127, never falling along the last dimension, each value on 1 to 512 neighbouring positions
- keep_mask: int32 [8, 1024], P('dp'), may hold values 0 or 1
- adapter_pick: int32 [8, 1], P('dp'), may hold values from 0 to 3
Outputs:
- block_output: bfloat16 [8, 1024, 2048], P('dp', None, 'tensor')
- tokens_grad: bfloat16 [8, 1024, 2048], P('dp', None, 'tensor')
- lead_grad: float32 [5, 4, 2048, 16], replicated
- head_grad: float32 [3, 4, 16, 2048], P(None, None, None, 'tensor')
- unit_grad: float32 [2, 4, 16, 8192], P(None, None, None, 'tensor')
- merge_grad: float32 [4, 2048, 16], P(None, 'tensor')
- down_grad: float32 [4, 8192, 16], P(None, 'tensor')
- tail_grad: float32 [2, 4, 16, 2048], replicated
Inputs may be any that keep to these rules, and one draw needn't show every extreme that they name: `doc_ids`: ids never fall along a sequence; one document holds at most 512 tokens. `adapter_pick`: every adapter is picked by some sequence.
All inputs are finite; a program needn't handle non-finite values. No bound on the sum of `keep_mask` on one device may be relied on, other than what follows from the above.
Results may differ from a plain program's by a relative error of at most 0.017.
Values may be sent and summed in bfloat16 or wider, within the bound.
No kernel may reach another device: no remote copies, remote signals or barrier semaphores. Data moves between devices by JAX's collectives and lax.ppermute only.
A program may use at most 320 MiB of HBM per device.

v0:
```python
import math

import jax
import jax.numpy as jnp
from jax import lax
from jax.sharding import PartitionSpec as P

HEAD_DIM = 64


EPSILON = 1e-05
ROPE_BASE = 130000.0
ADAPTER_SCALING = 2.0
MASKED = -1000000000.0


def tables(length):
    half_width = HEAD_DIM // 2
    frequency = ROPE_BASE ** (-jnp.arange(half_width, dtype=jnp.float32) * (2.0 / HEAD_DIM))
    angles = jnp.arange(length, dtype=jnp.float32)[:, None] * frequency[None, :]
    return (jnp.cos(angles)[:, None, :], jnp.sin(angles)[:, None, :])


def rotate(value_rows, cosine_table, sine_table):
    half_width = value_rows.shape[-1] // 2
    first_half = value_rows[..., :half_width]
    second_half = value_rows[..., half_width:]
    return jnp.concatenate(
        [
            first_half * cosine_table - second_half * sine_table,
            second_half * cosine_table + first_half * sine_table,
        ],
        axis=-1,
    )


def unrotate(value_rows, cosine_table, sine_table):
    half_width = value_rows.shape[-1] // 2
    first_half = value_rows[..., :half_width]
    second_half = value_rows[..., half_width:]
    return jnp.concatenate(
        [
            first_half * cosine_table + second_half * sine_table,
            second_half * cosine_table - first_half * sine_table,
        ],
        axis=-1,
    )


def permit(segments, kept_keys, first_row, last_row):
    rows_at = jnp.arange(first_row, last_row)[:, None]
    keys_at = jnp.arange(last_row)[None, :]
    same_doc = segments[first_row:last_row][:, None] == segments[:last_row][None, :]
    live_key = (kept_keys[:last_row][None, :] == 1) | (rows_at == keys_at)
    return (keys_at <= rows_at) & same_doc & live_key


def block_scores(query_rot, key_rot, segments, kept_keys, first_row, last_row, inverse_root):
    scores = (
        jnp.einsum(
            "qhe,khe->hqk",
            query_rot[first_row:last_row],
            key_rot[:last_row],
            preferred_element_type=jnp.float32,
        )
        * inverse_root
    )
    allowed = permit(segments, kept_keys, first_row, last_row)
    return jnp.where(allowed[None], scores, MASKED)


def norm_back(stream, scale, norm_gain, gradient):
    scaled = norm_gain * gradient
    return scale * (
        scaled - stream * scale * scale * jnp.mean(scaled * stream, axis=1, keepdims=True)
    )


def place_slot(gradient, slots, axis):
    shape = [1] * (gradient.ndim + 1)
    shape[axis] = slots.shape[0]
    return jnp.expand_dims(gradient, axis) * slots.reshape(shape)


def on_device(
    tokens,
    cotangent,
    norm_gains,
    query_key_value_matrix,
    output_matrix,
    gate_up_matrix,
    down_matrix,
    lead_factors,
    head_factors,
    unit_factors,
    merge_factors,
    down_factors,
    tail_factors,
    doc_ids,
    keep_mask,
    adapter_pick,
):
    tensor_index = lax.axis_index("tensor")
    slab_width = tokens.shape[2]
    gathered = lax.all_gather(tokens[0], "tensor", axis=1, tiled=True)
    stream = gathered.astype(jnp.float32)
    length, full_width = stream.shape
    norm_gain = norm_gains.astype(jnp.float32)
    chosen = adapter_pick[0, 0]
    leading_selection = lax.dynamic_index_in_dim(lead_factors, chosen, 1, keepdims=False)
    head_selection = lax.dynamic_index_in_dim(head_factors, chosen, 1, keepdims=False)
    unit_selection = lax.dynamic_index_in_dim(unit_factors, chosen, 1, keepdims=False)
    merged_selection = lax.dynamic_index_in_dim(merge_factors, chosen, 0, keepdims=False)
    shrinking_selection = lax.dynamic_index_in_dim(down_factors, chosen, 0, keepdims=False)
    trailing_selection = lax.dynamic_index_in_dim(tail_factors, chosen, 1, keepdims=False)
    scale_one = lax.rsqrt(jnp.mean(stream * stream, axis=1, keepdims=True) + EPSILON)
    first_normalized = (stream * scale_one * norm_gain[0]).astype(jnp.bfloat16)
    mids_attention = jnp.einsum(
        "td,kdr->ktr", first_normalized, leading_selection[0:3], preferred_element_type=jnp.float32
    ).astype(jnp.bfloat16)
    projection_result = jnp.einsum(
        "td,kdf->ktf", first_normalized, query_key_value_matrix, preferred_element_type=jnp.float32
    )
    projection_result = projection_result + ADAPTER_SCALING * jnp.einsum(
        "ktr,krf->ktf", mids_attention, head_selection, preferred_element_type=jnp.float32
    )
    cosine_table, sine_table = tables(length)
    query_rot = rotate(
        projection_result[0].reshape(length, -1, HEAD_DIM), cosine_table, sine_table
    ).astype(jnp.bfloat16)
    key_rot = rotate(
        projection_result[1].reshape(length, -1, HEAD_DIM), cosine_table, sine_table
    ).astype(jnp.bfloat16)
    valued = projection_result[2].reshape(length, -1, HEAD_DIM).astype(jnp.bfloat16)
    segments = doc_ids[0]
    kept_keys = keep_mask[0]
    block_rows = min(512, length)
    inverse_root = 1.0 / math.sqrt(HEAD_DIM)
    pieces = []
    log_sums = []
    for first_row in range(0, length, block_rows):
        last_row = first_row + block_rows
        scores = block_scores(
            query_rot, key_rot, segments, kept_keys, first_row, last_row, inverse_root
        )
        largest = jnp.max(scores, axis=2, keepdims=True)
        raised = jnp.exp(scores - largest)
        totals = jnp.sum(raised, axis=2, keepdims=True)
        weights = (raised / totals).astype(jnp.bfloat16)
        pieces.append(
            jnp.einsum(
                "hqk,khe->qhe", weights, valued[:last_row], preferred_element_type=jnp.float32
            )
        )
        log_sums.append(largest + jnp.log(totals))
    attention_result = jnp.concatenate(pieces, axis=0).reshape(length, -1).astype(jnp.bfloat16)
    merge_mid = jnp.dot(
        attention_result, merged_selection, preferred_element_type=jnp.float32
    ).astype(jnp.bfloat16)
    branch_portion = jnp.dot(attention_result, output_matrix, preferred_element_type=jnp.float32)
    branch_portion = branch_portion + ADAPTER_SCALING * jnp.dot(
        merge_mid, trailing_selection[0], preferred_element_type=jnp.float32
    )
    first_hidden = stream + lax.psum(branch_portion, "tensor")
    scale_two = lax.rsqrt(jnp.mean(first_hidden * first_hidden, axis=1, keepdims=True) + EPSILON)
    second_normalized = (first_hidden * scale_two * norm_gain[1]).astype(jnp.bfloat16)
    own_hidden_one = lax.dynamic_slice_in_dim(
        first_hidden, tensor_index * slab_width, slab_width, 1
    )
    mids_unit = jnp.einsum(
        "td,kdr->ktr", second_normalized, leading_selection[3:5], preferred_element_type=jnp.float32
    ).astype(jnp.bfloat16)
    gated_product = jnp.einsum(
        "td,kdf->ktf", second_normalized, gate_up_matrix, preferred_element_type=jnp.float32
    )
    gated_product = gated_product + ADAPTER_SCALING * jnp.einsum(
        "ktr,krf->ktf", mids_unit, unit_selection, preferred_element_type=jnp.float32
    )
    gate_activation = gated_product[0]
    up_activation = gated_product[1]
    sigmoid_gate = jax.nn.sigmoid(gate_activation)
    activated = gate_activation * sigmoid_gate
    hidden_state = (activated * up_activation).astype(jnp.bfloat16)
    down_mid = jnp.dot(
        hidden_state, shrinking_selection, preferred_element_type=jnp.float32
    ).astype(jnp.bfloat16)
    feedforward_portion = jnp.dot(hidden_state, down_matrix, preferred_element_type=jnp.float32)
    feedforward_portion = feedforward_portion + ADAPTER_SCALING * jnp.dot(
        down_mid, trailing_selection[1], preferred_element_type=jnp.float32
    )
    whole_feed = lax.psum(feedforward_portion, "tensor")
    layer_out = own_hidden_one + lax.dynamic_slice_in_dim(
        whole_feed, tensor_index * slab_width, slab_width, 1
    )
    upstream = lax.all_gather(cotangent[0], "tensor", axis=1, tiled=True)
    down_back = (
        ADAPTER_SCALING
        * jnp.einsum(
            "td,rd->tr", upstream, trailing_selection[1], preferred_element_type=jnp.float32
        )
    ).astype(jnp.bfloat16)
    trailing_down = ADAPTER_SCALING * jnp.einsum(
        "tr,td->rd", down_mid, upstream, preferred_element_type=jnp.float32
    )
    down_local = jnp.einsum(
        "tf,tr->fr", hidden_state, down_back, preferred_element_type=jnp.float32
    )
    hidden_grad = jnp.einsum("td,fd->tf", upstream, down_matrix, preferred_element_type=jnp.float32)
    hidden_grad = hidden_grad + jnp.einsum(
        "tr,fr->tf", down_back, shrinking_selection, preferred_element_type=jnp.float32
    )
    gate_grad = (
        hidden_grad * up_activation * sigmoid_gate * (1.0 + gate_activation * (1.0 - sigmoid_gate))
    )
    up_grad = hidden_grad * activated
    gated_grad = jnp.stack([gate_grad, up_grad]).astype(jnp.bfloat16)
    unit_back = (
        ADAPTER_SCALING
        * jnp.einsum("ktf,krf->ktr", gated_grad, unit_selection, preferred_element_type=jnp.float32)
    ).astype(jnp.bfloat16)
    local_unit = ADAPTER_SCALING * jnp.einsum(
        "ktr,ktf->krf", mids_unit, gated_grad, preferred_element_type=jnp.float32
    )
    lead_unit = jnp.einsum(
        "td,ktr->kdr", second_normalized, unit_back, preferred_element_type=jnp.float32
    )
    normed_two_part = jnp.einsum(
        "ktf,kdf->td", gated_grad, gate_up_matrix, preferred_element_type=jnp.float32
    )
    normed_two_part = normed_two_part + jnp.einsum(
        "ktr,kdr->td", unit_back, leading_selection[3:5], preferred_element_type=jnp.float32
    )
    normed_two_grad = lax.psum(normed_two_part, "tensor")
    hidden_one_grad = upstream.astype(jnp.float32) + norm_back(
        first_hidden, scale_two, norm_gain[1], normed_two_grad
    )
    branch_grad = hidden_one_grad.astype(jnp.bfloat16)
    own_hidden_grad = lax.dynamic_slice_in_dim(
        hidden_one_grad, tensor_index * slab_width, slab_width, 1
    )
    merge_back = (
        ADAPTER_SCALING
        * jnp.einsum(
            "td,rd->tr", branch_grad, trailing_selection[0], preferred_element_type=jnp.float32
        )
    ).astype(jnp.bfloat16)
    trailing_attention = ADAPTER_SCALING * jnp.einsum(
        "tr,td->rd", merge_mid, branch_grad, preferred_element_type=jnp.float32
    )
    merge_local = jnp.einsum(
        "tf,tr->fr", attention_result, merge_back, preferred_element_type=jnp.float32
    )
    attended_grad = jnp.einsum(
        "td,fd->tf", branch_grad, output_matrix, preferred_element_type=jnp.float32
    )
    attended_grad = attended_grad + jnp.einsum(
        "tr,fr->tf", merge_back, merged_selection, preferred_element_type=jnp.float32
    )
    attended_grad = attended_grad.astype(jnp.bfloat16).reshape(length, -1, HEAD_DIM)
    query_parts = []
    key_grad = jnp.zeros(key_rot.shape, jnp.float32)
    value_grad = jnp.zeros(valued.shape, jnp.float32)
    for block_index, first_row in enumerate(range(0, length, block_rows)):
        last_row = first_row + block_rows
        scores = block_scores(
            query_rot, key_rot, segments, kept_keys, first_row, last_row, inverse_root
        )
        probs = jnp.exp(scores - log_sums[block_index])
        prob_grad = jnp.einsum(
            "qhe,khe->hqk",
            attended_grad[first_row:last_row],
            valued[:last_row],
            preferred_element_type=jnp.float32,
        )
        inner = jnp.sum(probs * prob_grad, axis=2, keepdims=True)
        score_grad = (probs * (prob_grad - inner)).astype(jnp.bfloat16)
        query_parts.append(
            jnp.einsum(
                "hqk,khe->qhe", score_grad, key_rot[:last_row], preferred_element_type=jnp.float32
            )
            * inverse_root
        )
        key_grad = key_grad.at[:last_row].add(
            jnp.einsum(
                "hqk,qhe->khe",
                score_grad,
                query_rot[first_row:last_row],
                preferred_element_type=jnp.float32,
            )
            * inverse_root
        )
        value_grad = value_grad.at[:last_row].add(
            jnp.einsum(
                "hqk,qhe->khe",
                probs.astype(jnp.bfloat16),
                attended_grad[first_row:last_row],
                preferred_element_type=jnp.float32,
            )
        )
    query_grad = unrotate(jnp.concatenate(query_parts, axis=0), cosine_table, sine_table)
    key_grad = unrotate(key_grad, cosine_table, sine_table)
    projected_grad = jnp.stack(
        [
            query_grad.reshape(length, -1),
            key_grad.reshape(length, -1),
            value_grad.reshape(length, -1),
        ]
    ).astype(jnp.bfloat16)
    head_back = (
        ADAPTER_SCALING
        * jnp.einsum(
            "ktf,krf->ktr", projected_grad, head_selection, preferred_element_type=jnp.float32
        )
    ).astype(jnp.bfloat16)
    local_head = ADAPTER_SCALING * jnp.einsum(
        "ktr,ktf->krf", mids_attention, projected_grad, preferred_element_type=jnp.float32
    )
    lead_attention = jnp.einsum(
        "td,ktr->kdr", first_normalized, head_back, preferred_element_type=jnp.float32
    )
    normed_one_part = jnp.einsum(
        "ktf,kdf->td", projected_grad, query_key_value_matrix, preferred_element_type=jnp.float32
    )
    normed_one_part = normed_one_part + jnp.einsum(
        "ktr,kdr->td", head_back, leading_selection[0:3], preferred_element_type=jnp.float32
    )
    whole_grad = lax.psum(normed_one_part, "tensor")
    full_norm_grad = norm_back(stream, scale_one, norm_gain[0], whole_grad)
    tokens_grad = own_hidden_grad + lax.dynamic_slice_in_dim(
        full_norm_grad, tensor_index * slab_width, slab_width, 1
    )
    slots = (jnp.arange(lead_factors.shape[1]) == chosen).astype(jnp.float32)
    lead_local = place_slot(jnp.concatenate([lead_attention, lead_unit], axis=0), slots, 1)
    tail_local = place_slot(jnp.stack([trailing_attention, trailing_down]), slots, 1)
    head_sum, unit_sum, merge_sum, down_sum = lax.psum(
        (
            place_slot(local_head, slots, 1),
            place_slot(local_unit, slots, 1),
            place_slot(merge_local, slots, 0),
            place_slot(down_local, slots, 0),
        ),
        "dp",
    )
    lead_sum, tail_sum = lax.psum((lead_local, tail_local), ("dp", "tensor"))
    return (
        layer_out.astype(jnp.bfloat16)[None],
        tokens_grad.astype(jnp.bfloat16)[None],
        lead_sum,
        head_sum,
        unit_sum,
        merge_sum,
        down_sum,
        tail_sum,
    )


def solution(mesh):
    return jax.shard_map(
        on_device,
        mesh=mesh,
        in_specs=(
            P("dp", None, "tensor"),
            P("dp", None, "tensor"),
            P(),
            P(None, None, "tensor"),
            P("tensor", None),
            P(None, None, "tensor"),
            P("tensor", None),
            P(),
            P(None, None, None, "tensor"),
            P(None, None, None, "tensor"),
            P(None, "tensor", None),
            P(None, "tensor", None),
            P(),
            P("dp", None),
            P("dp", None),
            P("dp", None),
        ),
        out_specs=(
            P("dp", None, "tensor"),
            P("dp", None, "tensor"),
            P(),
            P(None, None, None, "tensor"),
            P(None, None, None, "tensor"),
            P(None, "tensor", None),
            P(None, "tensor", None),
            P(),
        ),
        check_vma=False,
    )
```

profile of v0, /device:TPU:0, one launch (start us, length us, event | category | flops | bytes accessed | tf_op | source)
XLA Modules:
  0.0 1740.5 jit_solution(509260375009268421)
XLA Ops:
  14.7 78.4 %all-gather.5.cloned.1.call-done = bf16[1,1024,2048]{2,1,0:T(8,128)(2,1)} async-done(((bf16[1,1024,512]{2,1,0:T(8,128)(2,1)}), bf16[1,1024,2048]{2,1,0:T(8,128)(2,1)}) %all-gather.5.cloned.1.call-update) | async-done | bytes 4194320 | tf_op jit(solution)/shard_map/all_gather | solution.py:105
  102.0 11.9 fusion.145
  133.1 5.7 copy-done.3
  154.2 19.8 %all-gather.7.cloned.1.call-done = bf16[1,1024,2048]{2,1,0:T(8,128)(2,1)} async-done(((bf16[1,1024,512]{2,1,0:T(8,128)(2,1)}), bf16[1,1024,2048]{2,1,0:T(8,128)(2,1)}) %all-gather.7.cloned.1.call-update) | async-done | bytes 4194320 | tf_op jit(solution)/shard_map/all_gather | solution.py:195
  177.4 15.8 fusion.27
  193.2 272.7 %all-reduce.11.cloned.1.call-done = f32[1024,2048]{1,0:T(8,128)} async-done(((f32[1024,2048]{1,0:T(8,128)}), f32[1024,2048]{1,0:T(8,128)}) %all-reduce.11.cloned.1.call-update) | async-done | bytes 8388624 | tf_op jit(solution)/shard_map/psum | solution.py:164
  465.9 5.8 multiply_reduce_fusion.3
  474.9 23.2 %fusion.151 = f32[1024,2,2048]{2,0,1:T(8,128)} fusion(bf16[1024,2048,1]{1,0,2:T(8,128)(2,1)S(1)} %fusion.21, bf16[2,2048,2048]{2,1,0:T(8,128)(2,1)} %param.33), kind=kOutput, calls=%fused_computation.231 | convolution fusion | flops 17179869184 | bytes 37748736 | tf_op jit(solution)/shard_map/td,kdf->ktf/dot_general | solution.py:173
  498.1 14.0 bitcast_add_fusion
  512.1 13.4 fusion.33
  531.0 21.6 %fusion.36 = f32[1024,2048,1]{1,0,2:T(8,128)S(1)} fusion(bf16[2,2048,2048]{2,1,0:T(8,128)(2,1)} %param.33, bf16[1,1024,2048]{2,1,0:T(8,128)(2,1)} %get-tuple-element.85, bf16[1,1024,2048]{2,1,0:T(8,128)(2,1)S(1)} %get-tuple-element.84), kind=kOutput, calls=%fused_computation.72 | convolution fusion | flops 17184063488 | bytes 33554432 | tf_op jit(solution)/shard_map/ktf,kdf->td/dot_general | solution.py:227
  559.0 8.2 fusion.73
  567.3 11.2 fusion.152
  583.9 264.3 %all-reduce.13.cloned.1.call-done = f32[1024,2048]{1,0:T(8,128)} async-done(((f32[1024,2048]{1,0:T(8,128)}), f32[1024,2048]{1,0:T(8,128)}) %all-reduce.13.cloned.1.call-update) | async-done | bytes 8388624 | tf_op jit(solution)/shard_map/psum | solution.py:233
  848.3 6.8 multiply_reduce_fusion.2
  855.2 7.6 multiply_add_fusion
  878.0 5.9 multiply_convert_fusion.1
  893.4 10.0 multiply_reduce_fusion
  910.6 11.9 multiply_convert_fusion
  935.3 8.9 fusion.137
  972.5 539.7 %all-reduce.19.cloned.1.call-done = (f32[1024,2048]{1,0:T(8,128)}, f32[1024,2048]{1,0:T(8,128)}) async-done(((f32[1024,2048]{1,0:T(8,128)}, f32[1024,2048]{1,0:T(8,128)}), (f32[1024,2048]{1,0:T(8,128)}, f32[1024,2048]{1,0:T(8,128)})) %all-reduce.19.cloned.1.call-update) | async-done | bytes 16777232 | tf_op jit(solution)/shard_map/psum | solution.py:191
  1515.8 5.9 fusion.5
  1524.7 52.5 %all-reduce.17.cloned.1.call-done = (f32[3,4,16,512]{3,2,1,0:T(8,128)}, f32[2,4,16,2048]{3,2,1,0:T(8,128)}, f32[4,512,16]{1,2,0:T(8,128)}, f32[4,2048,16]{1,2,0:T(8,128)}) async-done(((f32[3,4,16,512]{3,2,1,0:T(8,128)}, f32[2,4,16,2048]{3,2,1,0:T(8,128)}, f32[4,512,16]{1,2,0:T(8,128)}, f32[4,2048,16]{1,2,0:T(8,128)}), (f32[3,4,16,512]{3,2,1,0:T(8,128)}, f32[2,4,16,2048]{3,2,1,0:T(8,128)}, ...) | async-done | bytes 2097168 | tf_op jit(solution)/shard_map/psum | solution.py:335
  1577.2 145.2 %all-reduce.15.cloned.1.call-done = (f32[5,4,2048,16]{2,3,1,0:T(8,128)}, f32[2,4,16,2048]{3,2,1,0:T(8,128)}) async-done(((f32[5,4,2048,16]{2,3,1,0:T(8,128)}, f32[2,4,16,2048]{3,2,1,0:T(8,128)}), (f32[5,4,2048,16]{2,3,1,0:T(8,128)}, f32[2,4,16,2048]{3,2,1,0:T(8,128)})) %all-reduce.15.cloned.1.call-update) | async-done | bytes 3670032 | tf_op jit(solution)/shard_map/psum | solution.py:344
  (262 shorter events, 164.1 us)
Async XLA Ops:
  7.2 139.1 %copy-start = (bf16[512,2048]{1,0:T(8,128)(2,1)S(1)}, bf16[512,2048]{1,0:T(8,128)(2,1)}, u32[]{:S(2)}) copy-start(bf16[512,2048]{1,0:T(8,128)(2,1)} %param.32) | copy-start | bytes 6291460
  7.2 85.9 %all-gather.5.cloned.1.call-start = ((), (), s32[]{:S(2)}) async-start(), calls=%async_computation.2 | async-start | bytes 5242880 | tf_op jit(solution)/shard_map/all_gather | solution.py:105
  7.9 166.1 %all-gather.7.cloned.1.call-start = ((), (), s32[]{:S(2)}) async-start(), calls=%async_computation.3 | async-start | bytes 5242880 | tf_op jit(solution)/shard_map/all_gather | solution.py:195
  8.7 457.2 %all-reduce.11.cloned.1.call-start = ((), (), s32[]{:S(2)}) async-start(), calls=%async_computation | async-start | bytes 16777216 | tf_op jit(solution)/shard_map/psum | solution.py:164
  12.3 89.7 %copy-start.69 = (f32[1,2048]{1,0:T(1,128)}, f32[1,2048]{1,0:T(1,128)S(1)}, u32[]{:S(2)}) copy-start(f32[1,2048]{1,0:T(1,128)S(1)} %get-tuple-element.105) | copy-start | bytes 24580
  12.8 106.5 %copy-start.29 = (f32[1024,32]{0,1:T(8,128)}, f32[1024,32]{0,1:T(8,128)S(1)}, u32[]{:S(2)}) copy-start(f32[1024,32]{0,1:T(8,128)S(1)} %get-tuple-element.110) | copy-start | bytes 393220
  12.9 106.5 %copy-start.31 = (f32[1024,32]{0,1:T(8,128)}, f32[1024,32]{0,1:T(8,128)S(1)}, u32[]{:S(2)}) copy-start(f32[1024,32]{0,1:T(8,128)S(1)} %get-tuple-element.111) | copy-start | bytes 393220
  115.0 18.1 %copy-start.27 = (bf16[1,512,512]{1,2,0:T(8,128)(2,1)}, bf16[1,512,512]{1,2,0:T(8,128)(2,1)S(1)}, u32[]{:S(2)}) copy-start(bf16[1,512,512]{1,2,0:T(8,128)(2,1)S(1)} %slice.240) | copy-start | bytes 1572868
  116.5 23.9 %copy-start.21 = (bf16[1,1024,512]{1,2,0:T(8,128)(2,1)}, bf16[1,1024,512]{1,2,0:T(8,128)(2,1)S(1)}, u32[]{:S(2)}) copy-start(bf16[1,1024,512]{1,2,0:T(8,128)(2,1)S(1)} %slice.249) | copy-start | bytes 3145732
  154.2 694.1 %all-reduce.13.cloned.1.call-start = ((), (), s32[]{:S(2)}) async-start(), calls=%async_computation.1 | async-start | bytes 16777216 | tf_op jit(solution)/shard_map/psum | solution.py:233
  177.4 334.7 %copy-start.52 = (bf16[16,1024]{1,0:T(8,128)(2,1)}, bf16[16,1024]{1,0:T(8,128)(2,1)S(1)}, u32[]{:S(2)}) copy-start(bf16[16,1024]{1,0:T(8,128)(2,1)S(1)} %fusion.70) | copy-start | bytes 98308
  472.4 25.7 %copy-start.6 = (bf16[1024,2048,1]{1,0,2:T(8,128)(2,1)}, bf16[1024,2048,1]{1,0,2:T(8,128)(2,1)S(1)}, u32[]{:S(2)}) copy-start(bf16[1024,2048,1]{1,0,2:T(8,128)(2,1)S(1)} %fusion.21) | copy-start | bytes 12582916
  474.9 23.2 %copy-start.44 = (bf16[2,16,1024]{2,1,0:T(8,128)(2,1)}, bf16[2,16,1024]{2,1,0:T(8,128)(2,1)S(1)}, u32[]{:S(2)}) copy-start(bf16[2,16,1024]{2,1,0:T(8,128)(2,1)S(1)} %convolution_convert_fusion.1) | copy-start | bytes 196612
  474.9 23.2 %copy-start.68 = (bf16[2,4,16,2048]{3,2,1,0:T(8,128)(2,1)S(1)}, bf16[2,4,16,2048]{3,2,1,0:T(8,128)(2,1)}, u32[]{:S(2)}) copy-start(bf16[2,4,16,2048]{3,2,1,0:T(8,128)(2,1)} %param.37) | copy-start | bytes 1572868
  525.5 27.2 %copy-start.72 = (bf16[1,1024,2048]{2,1,0:T(8,128)(2,1)}, bf16[1,1024,2048]{2,1,0:T(8,128)(2,1)S(1)}, u32[]{:S(2)}) copy-start(bf16[1,1024,2048]{2,1,0:T(8,128)(2,1)S(1)} %get-tuple-element.84) | copy-start | bytes 12582916
  531.0 21.7 %copy-start.40 = (bf16[2,1024,16]{1,2,0:T(8,128)(2,1)}, bf16[2,1024,16]{1,2,0:T(8,128)(2,1)S(1)}, u32[]{:S(2)}) copy-start(bf16[2,1024,16]{1,2,0:T(8,128)(2,1)S(1)} %fusion.65) | copy-start | bytes 196612
  558.3 954.0 %all-reduce.19.cloned.1.call-start = ((), (), s32[]{:S(2)}) async-start(), calls=%async_computation.6 | async-start | bytes 33554432 | tf_op jit(solution)/shard_map/psum | solution.py:191
  583.9 271.1 %copy-start.65 = (f32[1024]{0:T(1024)S(1)}, f32[1024]{0:T(1024)}, u32[]{:S(2)}) copy-start(f32[1024]{0:T(1024)} %copy-done.64) | copy-start | bytes 12292
  878.0 15.3 slice-start
  878.0 15.3 slice-start.1
  878.0 15.3 slice-start.2
  949.9 627.3 %all-reduce.17.cloned.1.call-start = ((), (), s32[]{:S(2)}) async-start(), calls=%async_computation.5 | async-start | bytes 4194304 | tf_op jit(solution)/shard_map/psum | solution.py:335
  967.0 755.4 %all-reduce.15.cloned.1.call-start = ((), (), s32[]{:S(2)}) async-start(), calls=%async_computation.4 | async-start | bytes 7340032 | tf_op jit(solution)/shard_map/psum | solution.py:344
  1577.2 154.5 %copy-start.39 = (f32[4,2048,16]{1,2,0:T(8,128)S(1)}, f32[4,2048,16]{1,2,0:T(8,128)}, u32[]{:S(2)}) copy-start(f32[4,2048,16]{1,2,0:T(8,128)} %get-tuple-element.130) | copy-start | bytes 1572868
  (66 other events, 378.7 us)
Sparse Core Ops, SparseCore 0:
  9.6 83.4 all-gather.4
  94.7 79.2 all-gather.6
  176.5 289.3 all-reduce.10
  558.4 289.8 all-reduce.12
  950.0 562.2 all-reduce.18
  1516.2 60.9 all-reduce.16
  1583.4 138.9 all-reduce.14
where the time goes:
time: 1750 us; the launch traced here: 1740 us
  waiting for transfers between devices  1370 us (78%)
  matrix products  242 us (14%)
  other arithmetic  71.8 us (4%)
  local copies, waits for them, and re-layouts  36.4 us (2%)
    psum x1, waiting for transfers between devices, on_device(): whole_feed = lax.psum(feedforward_portion, 'tensor')  540 us
    psum x1, waiting for transfers between devices, on_device(): first_hidden = stream + lax.psum(branch_portion, 'tensor')  273 us
    psum x1, waiting for transfers between devices, on_device(): normed_two_grad = lax.psum(normed_two_part, 'tensor')  264 us
    psum x1, waiting for transfers between devices, on_device(): lead_sum, tail_sum = lax.psum((lead_local, tail_local), ('dp', 'tensor'))  145 us
    all_gather x1, waiting for transfers between devices, on_device(): gathered = lax.all_gather(tokens[0], 'tensor', axis=1, tiled=True)  78.4 us
    psum x1, waiting for transfers between devices, on_device(): lax.psum((place_slot(local_head, slots, 1), place_slot(local_unit, slots,...  52.5 us
  transfers between devices with their start and end apart: 7, of which 7 were waited for; matrix products, arithmetic and copies ran while one was open for 8% of the time, Pallas kernels for 0%

commit v1 on v0

v1 whole, which is shorter than its diff:
```python
import functools
import math

import jax
import jax.numpy as jnp
from jax import lax
from jax.experimental import pallas as pl
from jax.experimental.pallas import tpu as pltpu
from jax.sharding import PartitionSpec as P

HEAD_DIM = 64
EPSILON = 1e-05
ROPE_BASE = 130000.0
SCALING = 2.0
MASKED = -1000000000.0
LONGEST_DOC = 512
CHUNKS = 2
MODES = {
    "tok": ("stack", "stack"),
    "cot": ("pair", "pair"),
    "branch": ("stack", "pair"),
    "hidden": ("stack", "stack"),
    "feed": ("pair", "pair"),
    "back": ("stack", "pair"),
    "grad": ("stack", "stack"),
    "last": ("pair", "stack"),
}
SUB_ROWS = 256
VMEM_LIMIT = 60 * 1024 * 1024

BESIDE = [(0, 1), (1, 0), (2, 3), (3, 2)]
MIDDLE = [(1, 2), (2, 1)]
OVER = [(0, 2), (3, 1)]
ACROSS = [(1, 3), (2, 0)]
OUTWARD = [(1, 0), (2, 3)]
INWARD = [(0, 1), (3, 2)]

F32 = jnp.float32
BF16 = jnp.bfloat16


def dot(a, b):
    return jnp.dot(a, b, preferred_element_type=F32)


def dot_nt(a, b):
    return lax.dot_general(a, b, (((1,), (1,)), ((), ())), preferred_element_type=F32)


def dot_tn(a, b):
    return lax.dot_general(a, b, (((0,), (0,)), ((), ())), preferred_element_type=F32)


def whole(array):
    rank = len(array.shape)
    return pl.BlockSpec(array.shape, lambda *_: (0,) * rank, pipeline_mode=pl.Buffered(1))


ANY = pl.BlockSpec(memory_space=pl.ANY)


def out_whole(shape):
    rank = len(shape)
    return pl.BlockSpec(shape, lambda *_: (0,) * rank)


def spread(own, mode):
    if mode == "stack":
        return [lax.all_gather(own, "tensor", axis=0, tiled=False)]
    beside = lax.ppermute(own, "tensor", BESIDE)
    near = lax.ppermute(own, "tensor", MIDDLE)
    far = lax.ppermute(own, "tensor", OVER)
    return [
        own,
        beside,
        near,
        far,
        lax.ppermute(near, "tensor", OUTWARD),
        lax.ppermute(far, "tensor", OUTWARD),
    ]


def slab_columns(slab, width):
    return pl.ds(pl.multiple_of(slab * width, width), width)


def slab_copies(state, parts, target, sems):
    width = parts[0].shape[-1]
    if len(parts) == 1:
        return [
            (None, pltpu.make_async_copy(
                parts[0].at[j], target.at[:, j * width : (j + 1) * width], sems.at[j]
            ))
            for j in range(parts[0].shape[0])
        ]
    me, inner, near, far = places(state)
    copies = []
    for sem, (condition, part, slab) in enumerate((
        (None, parts[0], me),
        (None, parts[1], beside_of(me)),
        (inner, parts[2], near),
        (inner, parts[3], far),
        (jnp.logical_not(inner), parts[4], near),
        (jnp.logical_not(inner), parts[5], far),
    )):
        copies.append((condition, pltpu.make_async_copy(
            part, target.at[:, slab_columns(slab, width)], sems.at[sem % 4 + 2 * (sem // 4)]
        )))
    return copies


def beside_of(me):
    return me + 1 - 2 * lax.rem(me, 2)


def places(state):
    me = state[0]
    upper = me >= 2
    return me, (me == 1) | (me == 2), jnp.where(upper, 1, 2), jnp.where(upper, 0, 3)


def each_copy(copies, act):
    for condition, copy in copies:
        if condition is None:
            act(copy)
        else:
            pl.when(condition)(functools.partial(act, copy))


def start_copies(copies):
    each_copy(copies, lambda copy: copy.start())


def wait_copies(copies):
    each_copy(copies, lambda copy: copy.wait())


def write_slabs(state, outs, term):
    width = outs[0].shape[-1]
    if len(outs) == 1:
        for slab in range(outs[0].shape[0]):
            outs[0][slab] = term(slab_columns(slab, width)).astype(BF16)
        return
    me, _, near, far = places(state)
    for target, slab in (
        (outs[0].at[0], near),
        (outs[0].at[1], far),
        (outs[1], beside_of(me)),
        (outs[2], me),
    ):
        target[...] = term(slab_columns(slab, width)).astype(BF16)


def slab_outs(mode, count, rows, width):
    if mode == "stack":
        shapes = ((count, rows, width),)
    else:
        shapes = ((2, rows, width), (rows, width), (rows, width))
    return (
        tuple(jax.ShapeDtypeStruct(shape, BF16) for shape in shapes),
        tuple(out_whole(shape) for shape in shapes),
    )


def add_kernel(state, far, received, beside, near_out, far_out, beside_out):
    near_out[...] = (far[0].astype(F32) + received[0].astype(F32)).astype(BF16)
    far_out[...] = (far[1].astype(F32) + received[1].astype(F32)).astype(BF16)
    beside_out[...] = beside[...]


def sum_kernel(state, *refs):
    terms, (exact, rounded) = refs[:-2], refs[-2:]
    total = terms[0][...].astype(F32)
    for term in terms[1:]:
        total += term[...].astype(F32)
    exact[...] = total
    rounded[...] = total.astype(BF16)


def sum_after_kernel(count, state, first, *refs):
    terms, joined = refs[:-1], refs[-1]
    step = pl.program_id(0)

    @pl.when(step < count)
    def _():
        joined[...] = first[...]

    @pl.when(step >= count)
    def _():
        total = terms[0][...].astype(F32)
        for term in terms[1:]:
            total += term[...].astype(F32)
        joined[...] = total.astype(BF16)


def relay_kernel(state, *refs):
    count = len(refs) // 2
    for source, target in zip(refs[:count], refs[count:]):
        target[...] = source[...]


def relay(line, parts):
    return line.call(
        relay_kernel,
        "relay",
        (1,),
        parts,
        [whole(x) for x in parts],
        tuple(jax.ShapeDtypeStruct(x.shape, x.dtype) for x in parts),
        tuple(out_whole(x.shape) for x in parts),
    )


class SlabSum:
    def __init__(self, line, parts):
        self.line, self.parts = line, parts
        if len(parts) == 1:
            self.terms = [
                lax.psum_scatter(parts[0], "tensor", scatter_dimension=0, tiled=False)
            ]
        else:
            self.received = lax.ppermute(parts[0], "tensor", INWARD)

    def cross(self, after=()):
        far, beside, own = self.parts
        rows, width = own.shape
        step = min(256, rows)
        flat = pl.BlockSpec((step, width), lambda i, s: (i, 0))
        both = pl.BlockSpec((2, step, width), lambda i, s: (0, i, 0))
        near, far, beside = self.line.call(
            add_kernel,
            "add",
            (rows // step,),
            (far, self.received, beside),
            [both, both, flat],
            (jax.ShapeDtypeStruct((rows, width), BF16),) * 3,
            (flat,) * 3,
            after=after,
        )
        near = lax.ppermute(near, "tensor", MIDDLE)
        far = lax.ppermute(far, "tensor", ACROSS)
        beside = lax.ppermute(beside, "tensor", BESIDE)
        self.terms = [own, beside, near, far]

    def finish(self, base, after=()):
        rows, width = base.shape
        step = min(256, rows)
        flat = pl.BlockSpec((step, width), lambda i, s: (i, 0))
        return self.line.call(
            sum_kernel,
            "sum",
            (rows // step,),
            (base, *self.terms),
            [flat] * (1 + len(self.terms)),
            (jax.ShapeDtypeStruct((rows, width), F32), jax.ShapeDtypeStruct((rows, width), BF16)),
            (flat, flat),
            after=after,
        )


    def finish_after(self, base, first):
        rows, width = base.shape
        step = min(256, rows)
        count = rows // step
        flat = pl.BlockSpec((step, width), lambda i, s: (jnp.maximum(i - count, 0), 0))
        return self.line.call(
            functools.partial(sum_after_kernel, count),
            "sum_after",
            (2 * count,),
            (first, base, *self.terms),
            [pl.BlockSpec((step, width), lambda i, s: (jnp.minimum(i, count - 1), 0))]
            + [flat] * (1 + len(self.terms)),
            jax.ShapeDtypeStruct((2 * rows, width), BF16),
            pl.BlockSpec((step, width), lambda i, s: (i, 0)),
        )


def params(grid_rank=1):
    return pltpu.CompilerParams(
        dimension_semantics=("arbitrary",) * grid_rank, vmem_limit_bytes=VMEM_LIMIT
    )


class Line:
    def __init__(self, state):
        self.state, self.last = state, ()

    def call(self, kernel, name, grid, ins, in_specs, outs, out_specs, scratch=(), after=()):
        after = (*self.last, *after)
        n_used = 1 + len(ins)

        def body(*refs):
            kernel(*refs[:n_used], *refs[n_used + len(after) :])

        results = pl.pallas_call(
            body,
            name=name,
            grid_spec=pltpu.PrefetchScalarGridSpec(
                num_scalar_prefetch=1,
                grid=grid,
                in_specs=list(in_specs) + [ANY] * len(after),
                out_specs=out_specs,
                scratch_shapes=list(scratch),
            ),
            out_shape=outs,
            compiler_params=params(len(grid)),
            cost_estimate=pl.CostEstimate(flops=1, bytes_accessed=1, transcendentals=0),
        )(self.state, *ins, *after)
        self.last = (jax.tree.leaves(results)[-1],)
        return results


def swap_halves(values):
    width = values.shape[-1]
    half = HEAD_DIM // 2
    lane = lax.broadcasted_iota(jnp.int32, values.shape, values.ndim - 1) % HEAD_DIM
    return jnp.where(
        lane < half,
        pltpu.roll(values, width - half, values.ndim - 1),
        pltpu.roll(values, half, values.ndim - 1),
    )


def rope_groups(values, cosine, sine, sign):
    groups = []
    for first in range(0, values.shape[-1], 128):
        group = values[:, first : first + 128]
        groups.append(group * cosine + (sign * swap_halves(group)) * sine)
    return jnp.concatenate(groups, axis=-1)


def project_kernel(n_parts, state, *refs):
    parts, refs = refs[:n_parts], refs[n_parts:]
    gain, lead, weight, head, cosine, sine, qkv, normed, mid, scale, stream, sems = refs
    step = pl.program_id(0)
    rank = lead.shape[2]

    @pl.when(step == 0)
    def _():
        copies = slab_copies(state, parts, stream, sems)
        start_copies(copies)
        wait_copies(copies)
        for first in range(0, stream.shape[0], SUB_ROWS):
            here = pl.ds(first, SUB_ROWS)
            rows = stream[here, :].astype(F32)
            r1 = lax.rsqrt(jnp.mean(rows * rows, axis=1, keepdims=True) + EPSILON)
            scale[here, :] = r1
            values = (rows * r1 * gain[0:1, :]).astype(BF16)
            normed[here, :] = values
            mids = dot_nt(values, lead[:3, 0].reshape(3 * rank, -1))
            for j in range(3):
                mid[j, here, :] = mids[:, j * rank : (j + 1) * rank].astype(BF16)

    for first in range(0, stream.shape[0], SUB_ROWS):
        here = pl.ds(first, SUB_ROWS)
        projected = dot(normed[here, :], weight[0]) + SCALING * dot(mid[step, here, :], head[0, 0])

        @pl.when(step < 2)
        def _():
            qkv[0, here, :] = rope_groups(projected, cosine[here, :], sine[here, :], 1.0).astype(BF16)

        @pl.when(step == 2)
        def _():
            qkv[0, here, :] = projected.astype(BF16)


def project(line, parts, gains, lead, weight, head, cosine, sine, after=()):
    rows = parts[0].shape[-2]
    full, width = weight.shape[1:]
    rank = lead.shape[2]
    slabs = full // parts[0].shape[-1]
    return line.call(
        functools.partial(project_kernel, len(parts)),
        "project",
        (3,),
        (*parts, gains, lead, weight, head, cosine, sine),
        [ANY] * len(parts)
        + [
            whole(gains),
            pl.BlockSpec(
                (lead.shape[0], 1, rank, full),
                lambda j, s: (0, s[1], 0, 0),
                pipeline_mode=pl.Buffered(1),
            ),
            pl.BlockSpec((1, full, width), lambda j, s: (j, 0, 0)),
            pl.BlockSpec((1, 1, rank, width), lambda j, s: (j, s[1], 0, 0)),
            whole(cosine),
            whole(sine),
        ],
        (
            jax.ShapeDtypeStruct((3, rows, width), BF16),
            jax.ShapeDtypeStruct((rows, full), BF16),
            jax.ShapeDtypeStruct((3, rows, rank), BF16),
            jax.ShapeDtypeStruct((rows, 1), F32),
        ),
        (
            pl.BlockSpec((1, rows, width), lambda j, s: (j, 0, 0)),
            out_whole((rows, full)),
            out_whole((3, rows, rank)),
            out_whole((rows, 1)),
        ),
        [pltpu.VMEM((rows, full), BF16), pltpu.SemaphoreType.DMA((slabs,))],
        after,
    )


def head_mask(shape, half):
    lane = lax.broadcasted_iota(jnp.int32, shape, len(shape) - 1)
    return (lane >= HEAD_DIM) if half else (lane < HEAD_DIM)


def key_span(first_row, block):
    low = max(0, first_row - LONGEST_DOC + 1)
    return (low // 128) * 128, first_row + block


def key_bias(doc_rows, doc_keys, keep_keys, first_row, low, high, block):
    rows_at = first_row + lax.broadcasted_iota(jnp.int32, (block, high - low), 0)
    keys_at = low + lax.broadcasted_iota(jnp.int32, (block, high - low), 1)
    same = doc_rows == doc_keys[:, low:high]
    live = (keep_keys[:, low:high] == 1) | (rows_at == keys_at)
    return jnp.where((keys_at <= rows_at) & same & live, 0.0, MASKED)


def attend_kernel(first_row, block, n_chunks, n_outs, state, *refs):
    chunks, refs = refs[: 2 * n_chunks], refs[2 * n_chunks :]
    query, doc_rows, doc_keys, keep, weight, merge, tail = refs[:7]
    attended, refs = refs[7], refs[8:]
    branch, (keys, values, bias, held) = refs[:n_outs], refs[n_outs:]
    step = pl.program_id(0)
    rows = query.shape[1]
    for c in range(n_chunks):
        keys[c * rows : (c + 1) * rows, :] = chunks[2 * c][0]
        values[c * rows : (c + 1) * rows, :] = chunks[2 * c + 1][0]
    for sub in range(rows // block):
        start = first_row + sub * block
        low, high = key_span(start, block)
        here = pl.ds(sub * block, block)

        @pl.when(step == 0)
        def _():
            bias[sub, :, : high - low] = key_bias(
                doc_rows[here, :], doc_keys[...], keep[...], start, low, high, block
            )

        outs = []
        for half in range(2):
            mask = head_mask((block, 128), half)
            q = jnp.where(mask, query[0, here, :] * (HEAD_DIM**-0.5), 0.0).astype(BF16)
            scores = dot_nt(q, keys[low:high, :]) + bias[sub, :, : high - low]
            raised = jnp.exp(scores - jnp.max(scores, axis=1, keepdims=True))
            total = jnp.sum(raised, axis=1, keepdims=True)
            weights = (raised * (1.0 / total)).astype(BF16)
            outs.append(dot(weights, values[low:high, :]))
        columns = pl.ds(pl.multiple_of(step * 128, 128), 128)
        held[here, columns] = jnp.where(head_mask((block, 128), 0), outs[0], outs[1]).astype(BF16)

    @pl.when(step == pl.num_programs(0) - 1)
    def _():
        result = held[...]
        attended[...] = result
        mid = dot_nt(result, merge[0]).astype(BF16)
        write_slabs(
            state,
            branch,
            lambda columns: dot(result, weight[:, columns])
            + SCALING * dot(mid, tail[0, 0, :, columns]),
        )


def attend(line, qkvs, chunk, doc_column, doc_row, keep_row, weight, merge, tail, slabs, mode, after=()):
    rows, width = qkvs[0].shape[1:]
    first_row = chunk * rows
    block = min(256, rows)
    n_chunks = chunk + 1
    rank, full = merge.shape[1], weight.shape[1]
    ins, specs = [], []
    for c in range(n_chunks):
        for j in (1, 2):
            ins.append(qkvs[c])
            specs.append(pl.BlockSpec((1, rows, 128), lambda i, s, j=j: (j, 0, i)))
    ins += [qkvs[chunk], doc_column, doc_row, keep_row, weight, merge, tail]
    specs += [
        pl.BlockSpec((1, rows, 128), lambda i, s: (0, 0, i)),
        pl.BlockSpec((rows, 1), lambda i, s: (chunk, 0), pipeline_mode=pl.Buffered(1)),
        whole(doc_row),
        whole(keep_row),
        whole(weight),
        pl.BlockSpec((1, rank, width), lambda i, s: (s[1], 0, 0), pipeline_mode=pl.Buffered(1)),
        pl.BlockSpec(
            (1, 1, rank, full), lambda i, s: (0, s[1], 0, 0), pipeline_mode=pl.Buffered(1)
        ),
    ]
    n_keys = first_row + rows
    shapes, out_specs = slab_outs(mode, slabs, rows, full // slabs)
    outs = line.call(
        functools.partial(attend_kernel, first_row, block, n_chunks, len(shapes)),
        "attend",
        (width // 128,),
        ins,
        specs,
        (jax.ShapeDtypeStruct((rows, width), BF16),) + shapes,
        (out_whole((rows, width)),) + out_specs,
        [
            pltpu.VMEM((n_keys, 128), BF16),
            pltpu.VMEM((n_keys, 128), BF16),
            pltpu.VMEM((rows // block, block, min(n_keys, LONGEST_DOC + block)), F32),
            pltpu.VMEM((rows, width), BF16),
        ],
        after,
    )
    return outs


def feed_kernel(n_parts, n_cots, n_feed, n_back, state, *refs):
    parts, refs = refs[:n_parts], refs[n_parts:]
    cot_parts, refs = refs[:n_cots], refs[n_cots:]
    gain, lead, gate_w, up_w, down_w, unit, down, tail = refs[:8]
    refs = refs[8:]
    feed, refs = refs[:n_feed], refs[n_feed:]
    back, refs = refs[:n_back], refs[n_back:]
    unit_grad, down_grad, lead_grad, tail_grad = refs[:4]
    stream, upstream, normed, mid, down_back, scale = refs[4:10]
    feed_sum, back_sum, down_mid, unit_back, sems, cot_sems = refs[10:]
    step = pl.program_id(0)
    rank = lead.shape[2]
    firsts = range(0, stream.shape[0], SUB_ROWS)

    @pl.when(step == 0)
    def _():
        copies = slab_copies(state, parts, stream, sems)
        cot_copies = slab_copies(state, cot_parts, upstream, cot_sems)
        start_copies(copies)
        start_copies(cot_copies)
        wait_copies(copies)
        for first in firsts:
            here = pl.ds(first, SUB_ROWS)
            rows = stream[here, :].astype(F32)
            r2 = lax.rsqrt(jnp.mean(rows * rows, axis=1, keepdims=True) + EPSILON)
            scale[here, :] = r2
            values = (rows * r2 * gain[1:2, :]).astype(BF16)
            normed[here, :] = values
            mids = dot_nt(values, lead[3:5, 0].reshape(2 * rank, -1))
            for j in range(2):
                mid[j, here, :] = mids[:, j * rank : (j + 1) * rank].astype(BF16)
        wait_copies(cot_copies)
        down_back[...] = (SCALING * dot_nt(upstream[...], tail[0, 0])).astype(BF16)
        feed_sum[...] = jnp.zeros_like(feed_sum)
        back_sum[...] = jnp.zeros_like(back_sum)
        down_mid[...] = jnp.zeros_like(down_mid)
        unit_back[...] = jnp.zeros_like(unit_back)

    unit_terms = [0.0, 0.0]
    down_term = 0.0
    for first in firsts:
        here = pl.ds(first, SUB_ROWS)
        gate = dot(normed[here, :], gate_w[0]) + SCALING * dot(mid[0, here, :], unit[0, 0])
        up = dot(normed[here, :], up_w[0]) + SCALING * dot(mid[1, here, :], unit[1, 0])
        hidden_grad = dot_nt(upstream[here, :], down_w[...]) + dot(down_back[here, :], down[0])
        sigma = 1.0 / (1.0 + jnp.exp(-gate))
        active = gate * sigma
        hidden = (active * up).astype(BF16)
        up_grad = (hidden_grad * active).astype(BF16)
        gate_grad = (hidden_grad * up * (sigma + active * (1.0 - sigma))).astype(BF16)
        feed_sum[here, :] += dot(hidden, down_w[...])
        back_sum[here, :] += dot_nt(gate_grad, gate_w[0]) + dot_nt(up_grad, up_w[0])
        down_mid[here, :] += dot_nt(hidden, down[0])
        unit_back[0, here, :] += dot_nt(gate_grad, unit[0, 0])
        unit_back[1, here, :] += dot_nt(up_grad, unit[1, 0])
        unit_terms[0] += dot_tn(mid[0, here, :], gate_grad)
        unit_terms[1] += dot_tn(mid[1, here, :], up_grad)
        down_term += dot_tn(down_back[here, :], hidden)
    unit_grad[0] = SCALING * unit_terms[0]
    unit_grad[1] = SCALING * unit_terms[1]
    down_grad[...] = down_term

    @pl.when(step == pl.num_programs(0) - 1)
    def _():
        values = normed[...]
        mid_down = down_mid[...].astype(BF16)
        tail_grad[...] = SCALING * dot_tn(mid_down, upstream[...])
        unit_backs = [(SCALING * unit_back[j]).astype(BF16) for j in range(2)]
        for j in range(2):
            lead_grad[j] = dot_tn(unit_backs[j], values)
        write_slabs(
            state,
            feed,
            lambda columns: feed_sum[:, columns] + SCALING * dot(mid_down, tail[0, 0, :, columns]),
        )
        for first in firsts:
            here = pl.ds(first, SUB_ROWS)
            there = slice(first, first + SUB_ROWS)
            r2 = scale[here, :]
            total = back_sum[here, :]
            for j in range(2):
                total += dot(unit_backs[j][there], lead[3 + j, 0])
            inner = jnp.mean(total * normed[here, :].astype(F32), axis=1, keepdims=True)
            back_sum[here, :] = r2 * (
                gain[1:2, :] * total - stream[here, :].astype(F32) * (r2 * inner)
            )
        write_slabs(state, back, lambda columns: back_sum[:, columns])


def feed_forward(
    line, parts, cot_parts, gains, lead, gate_up, down_w, unit, down, tail, modes, after=()
):
    feed_mode, back_mode = modes
    rows, slab_width = parts[0].shape[-2:]
    full, units = gate_up.shape[1:]
    rank = lead.shape[2]
    slabs = full // slab_width
    block = min(512, units)
    feed_shapes, feed_specs = slab_outs(feed_mode, slabs, rows, slab_width)
    back_shapes, back_specs = slab_outs(back_mode, slabs, rows, slab_width)
    outs = line.call(
        functools.partial(
            feed_kernel, len(parts), len(cot_parts), len(feed_shapes), len(back_shapes)
        ),
        "feed_forward",
        (units // block,),
        (*parts, *cot_parts, gains, lead, gate_up, gate_up, down_w, unit, down, tail),
        [ANY] * (len(parts) + len(cot_parts))
        + [
            whole(gains),
            pl.BlockSpec(
                (lead.shape[0], 1, rank, full),
                lambda i, s: (0, s[1], 0, 0),
                pipeline_mode=pl.Buffered(1),
            ),
            pl.BlockSpec((1, full, block), lambda i, s: (0, 0, i)),
            pl.BlockSpec((1, full, block), lambda i, s: (1, 0, i)),
            pl.BlockSpec((block, full), lambda i, s: (i, 0)),
            pl.BlockSpec((2, 1, rank, block), lambda i, s: (0, s[1], 0, i)),
            pl.BlockSpec((1, rank, block), lambda i, s: (s[1], 0, i)),
            pl.BlockSpec(
                (1, 1, rank, full), lambda i, s: (1, s[1], 0, 0), pipeline_mode=pl.Buffered(1)
            ),
        ],
        feed_shapes
        + back_shapes
        + (
            jax.ShapeDtypeStruct((2, rank, units), F32),
            jax.ShapeDtypeStruct((rank, units), F32),
            jax.ShapeDtypeStruct((2, rank, full), F32),
            jax.ShapeDtypeStruct((rank, full), F32),
        ),
        feed_specs
        + back_specs
        + (
            pl.BlockSpec((2, rank, block), lambda i, s: (0, 0, i)),
            pl.BlockSpec((rank, block), lambda i, s: (0, i)),
            out_whole((2, rank, full)),
            out_whole((rank, full)),
        ),
        [
            pltpu.VMEM((rows, full), BF16),
            pltpu.VMEM((rows, full), BF16),
            pltpu.VMEM((rows, full), BF16),
            pltpu.VMEM((2, rows, rank), BF16),
            pltpu.VMEM((rows, rank), BF16),
            pltpu.VMEM((rows, 1), F32),
            pltpu.VMEM((rows, full), F32),
            pltpu.VMEM((rows, full), F32),
            pltpu.VMEM((rows, rank), F32),
            pltpu.VMEM((2, rows, rank), F32),
            pltpu.SemaphoreType.DMA((slabs,)),
            pltpu.SemaphoreType.DMA((slabs,)),
        ],
        after,
    )
    n_feed, n_both = len(feed_shapes), len(feed_shapes) + len(back_shapes)
    return list(outs[:n_feed]), list(outs[n_feed:n_both]), outs[n_both:]


def attend_back_kernel(first_row, block, n_chunks, n_parts, state, *refs):
    parts, refs = refs[:n_parts], refs[n_parts:]
    chunks, refs = refs[: 2 * n_chunks], refs[2 * n_chunks :]
    query, doc_rows, doc_keys, keep, attended, weight, merge, tail = refs[:8]
    query_grad, key_grad, value_grad, merge_grad, tail_grad = refs[8:13]
    keys, values, bias, branch, out_grad, sems = refs[13:]
    step = pl.program_id(0)
    rows = query.shape[1]
    inverse_root = HEAD_DIM**-0.5

    @pl.when(step == 0)
    def _():
        copies = slab_copies(state, parts, branch, sems)
        start_copies(copies)
        wait_copies(copies)
        gradient = branch[...]
        result = attended[...]
        merge_back = (SCALING * dot_nt(gradient, tail[0, 0])).astype(BF16)
        merge_mid = dot_nt(result, merge[0]).astype(BF16)
        merge_grad[...] = dot_tn(merge_back, result)
        tail_grad[...] = SCALING * dot_tn(merge_mid, gradient)
        whole_grad = (dot_nt(gradient, weight[...]) + dot(merge_back, merge[0])).astype(BF16)
        for pair in range(out_grad.shape[0]):
            out_grad[pair] = whole_grad[:, pair * 128 : (pair + 1) * 128]

    for c in range(n_chunks):
        keys[c * rows : (c + 1) * rows, :] = chunks[2 * c][0]
        values[c * rows : (c + 1) * rows, :] = chunks[2 * c + 1][0]
    key_grad[...] = jnp.zeros_like(key_grad)
    value_grad[...] = jnp.zeros_like(value_grad)
    for sub in range(rows // block):
        start = first_row + sub * block
        low, high = key_span(start, block)
        here = pl.ds(sub * block, block)

        @pl.when(step == 0)
        def _():
            bias[sub, :, : high - low] = key_bias(
                doc_rows[here, :], doc_keys[...], keep[...], start, low, high, block
            )

        outs = []
        key_term = value_term = 0.0
        for half in range(2):
            mask = head_mask((block, 128), half)
            q = jnp.where(mask, query[0, here, :] * inverse_root, 0.0).astype(BF16)
            grad = jnp.where(mask, out_grad[step, here, :], 0.0).astype(BF16)
            scores = dot_nt(q, keys[low:high, :]) + bias[sub, :, : high - low]
            raised = jnp.exp(scores - jnp.max(scores, axis=1, keepdims=True))
            probs = raised * (1.0 / jnp.sum(raised, axis=1, keepdims=True))
            prob_grad = dot_nt(grad, values[low:high, :])
            inner = jnp.sum(probs * prob_grad, axis=1, keepdims=True)
            score_grad = (probs * (prob_grad - inner)).astype(BF16)
            outs.append(dot(score_grad, keys[low:high, :]))
            key_term += dot_tn(score_grad, q)
            value_term += dot_tn(probs.astype(BF16), grad)
        mixed = jnp.where(head_mask((block, 128), 0), outs[0], outs[1])
        query_grad[here, :] = mixed * inverse_root
        key_grad[low:high, :] += key_term
        value_grad[low:high, :] += value_term


def attend_back(line, parts, qkvs, chunk, doc_column, doc_row, keep_row, attended, weight, merge, tail, after=()):
    rows, width = qkvs[0].shape[1:]
    first_row = chunk * rows
    block = min(256, rows)
    n_chunks = chunk + 1
    rank, full = merge.shape[1], weight.shape[1]
    slabs = full // parts[0].shape[-1]
    ins, specs = list(parts), [ANY] * len(parts)
    for c in range(n_chunks):
        for j in (1, 2):
            ins.append(qkvs[c])
            specs.append(pl.BlockSpec((1, rows, 128), lambda i, s, j=j: (j, 0, i)))
    ins += [qkvs[chunk], doc_column, doc_row, keep_row, attended, weight, merge, tail]
    specs += [
        pl.BlockSpec((1, rows, 128), lambda i, s: (0, 0, i)),
        pl.BlockSpec((rows, 1), lambda i, s: (chunk, 0), pipeline_mode=pl.Buffered(1)),
        whole(doc_row),
        whole(keep_row),
        whole(attended),
        whole(weight),
        pl.BlockSpec((1, rank, width), lambda i, s: (s[1], 0, 0), pipeline_mode=pl.Buffered(1)),
        pl.BlockSpec(
            (1, 1, rank, full), lambda i, s: (0, s[1], 0, 0), pipeline_mode=pl.Buffered(1)
        ),
    ]
    n_keys = first_row + rows
    return line.call(
        functools.partial(attend_back_kernel, first_row, block, n_chunks, len(parts)),
        "attend_back",
        (width // 128,),
        ins,
        specs,
        (
            jax.ShapeDtypeStruct((rows, width), F32),
            jax.ShapeDtypeStruct((n_keys, width), F32),
            jax.ShapeDtypeStruct((n_keys, width), F32),
            jax.ShapeDtypeStruct((rank, width), F32),
            jax.ShapeDtypeStruct((rank, full), F32),
        ),
        (
            pl.BlockSpec((rows, 128), lambda i, s: (0, i)),
            pl.BlockSpec((n_keys, 128), lambda i, s: (0, i)),
            pl.BlockSpec((n_keys, 128), lambda i, s: (0, i)),
            out_whole((rank, width)),
            out_whole((rank, full)),
        ),
        [
            pltpu.VMEM((n_keys, 128), BF16),
            pltpu.VMEM((n_keys, 128), BF16),
            pltpu.VMEM((rows // block, block, min(n_keys, LONGEST_DOC + block)), F32),
            pltpu.VMEM((rows, full), BF16),
            pltpu.VMEM((width // 128, rows, 128), BF16),
            pltpu.SemaphoreType.DMA((slabs,)),
        ],
        after,
    )


def project_back_kernel(n_later, n_outs, state, *refs):
    query_grad, refs = refs[0], refs[1:]
    later, refs = refs[: 2 * n_later], refs[2 * n_later :]
    weight, head, lead, gain, normed, mid, scale, cosine, sine = refs[:9]
    outs, refs = refs[9 : 9 + n_outs], refs[9 + n_outs :]
    head_grad, lead_grad, total, held = refs
    step = pl.program_id(0)

    @pl.when(step == 0)
    def _():
        total[...] = jnp.zeros_like(total)
        held[...] = rope_groups(query_grad[...], cosine[...], sine[...], -1.0).astype(BF16)

    def added(which):
        gradient = later[which][...]
        for other in range(1, n_later):
            gradient += later[2 * other + which][...]
        return gradient

    @pl.when(step == 1)
    def _():
        held[...] = rope_groups(added(0), cosine[...], sine[...], -1.0).astype(BF16)

    @pl.when(step == 2)
    def _():
        held[...] = added(1).astype(BF16)

    gradient = held[...]
    values = normed[...]
    back = (SCALING * dot_nt(gradient, head[0, 0])).astype(BF16)
    head_grad[0] = SCALING * dot_tn(mid[0], gradient)
    lead_grad[0] = dot_tn(back, values)
    total[...] += dot_nt(gradient, weight[0]) + dot(back, lead[0, 0])

    @pl.when(step == pl.num_programs(0) - 1)
    def _():
        r1 = scale[...]
        rows = values.astype(F32)
        inner = jnp.mean(total[...] * rows, axis=1, keepdims=True)
        total[...] = r1 * (gain[0:1, :] * total[...] - rows / gain[0:1, :] * inner)
        write_slabs(state, outs, lambda columns: total[:, columns])


def project_back(line, query_grad, later, chunk, weight, head, lead, gains, normed, mid, scale, cosine, sine, slabs, mode, after=()):
    rows, width = query_grad.shape
    full = weight.shape[1]
    rank = lead.shape[2]
    ins, specs = [query_grad], [whole(query_grad)]
    for array in later:
        ins.append(array)
        specs.append(
            pl.BlockSpec((rows, width), lambda j, s: (chunk, 0), pipeline_mode=pl.Buffered(1))
        )
    ins += [weight, head, lead, gains, normed, mid, scale, cosine, sine]
    specs += [
        pl.BlockSpec((1, full, width), lambda j, s: (j, 0, 0)),
        pl.BlockSpec((1, 1, rank, width), lambda j, s: (j, s[1], 0, 0)),
        pl.BlockSpec((1, 1, rank, full), lambda j, s: (j, s[1], 0, 0)),
        whole(gains),
        whole(normed),
        pl.BlockSpec((1, rows, rank), lambda j, s: (j, 0, 0)),
        whole(scale),
        whole(cosine),
        whole(sine),
    ]
    shapes, out_specs = slab_outs(mode, slabs, rows, full // slabs)
    outs = line.call(
        functools.partial(project_back_kernel, len(later) // 2, len(shapes)),
        "project_back",
        (3,),
        ins,
        specs,
        shapes
        + (
            jax.ShapeDtypeStruct((3, rank, width), F32),
            jax.ShapeDtypeStruct((3, rank, full), F32),
        ),
        out_specs
        + (
            pl.BlockSpec((1, rank, width), lambda j, s: (j, 0, 0)),
            pl.BlockSpec((1, rank, full), lambda j, s: (j, 0, 0)),
        ),
        [pltpu.VMEM((rows, full), F32), pltpu.VMEM((rows, width), BF16)],
        after,
    )
    return list(outs[:-2]), outs[-2], outs[-1]


def rope_tables(length):
    half = HEAD_DIM // 2
    frequency = ROPE_BASE ** (-jnp.arange(half, dtype=F32) * (2.0 / HEAD_DIM))
    angles = jnp.arange(length, dtype=F32)[:, None] * frequency[None, :]
    cosine, sine = jnp.cos(angles), jnp.sin(angles)
    return (
        jnp.concatenate([cosine] * 4, axis=1),
        jnp.concatenate([-sine, sine] * 2, axis=1),
    )


def wire_kernel(n_shared, n_pairs, state, *refs):
    pairs, (far, beside, own, split, shared) = refs[: 2 * n_pairs], refs[2 * n_pairs :]
    shared_at = split_at = 0
    for p in range(n_pairs):
        total = (pairs[2 * p][...] + pairs[2 * p + 1][...]).astype(BF16)
        total = total.reshape(-1, total.shape[-1])
        rows = total.shape[0]
        if p < n_shared:
            shared[shared_at : shared_at + rows, :] = total
            shared_at += rows
            continue
        width = split.shape[1]
        for first in range(0, total.shape[1], width):
            split[split_at : split_at + rows, :] = total[:, first : first + width]
            split_at += rows
    write_slabs(state, (far, beside, own), lambda columns: shared[:, columns])
    picked = jnp.full((split.shape[0] - split_at, split.shape[1]), state[1].astype(F32))
    split[split_at:, :] = picked.astype(BF16)


def join_kernel(state, own, beside, near, far, split, joined):
    rows = own.shape[0]
    total = own[...].astype(F32) + beside[...].astype(F32)
    joined[:rows, :] = (total + near[...].astype(F32) + far[...].astype(F32)).astype(BF16)
    joined[rows:, :] = split[...]


def combine_kernel(n_shared, adapters, state, everyone, shared, *split):
    count, rows, width = everyone.shape
    for a in range(adapters):
        total = jnp.zeros((rows - 16, width), F32)
        for d in range(count):
            here = everyone[d, rows - 16 :, :].astype(F32)[:1] == float(a)
            total += jnp.where(here, everyone[d, : rows - 16, :].astype(F32), 0.0)
        shared[a] = total[:n_shared].astype(BF16)
        at = n_shared
        for target in split:
            height, full = target.shape[1:]
            for first in range(0, full, width):
                target[a, :, first : first + width] = total[at : at + height]
                at += height


def whole_width_kernel(state, *refs):
    early, late, (lead, tail) = refs[:6], refs[6:12], refs[12:14]
    early_whole, late_whole, early_sems, late_sems = refs[14:]
    rank, adapters = lead.shape[2], lead.shape[1]
    early_copies = slab_copies(state, early, early_whole, early_sems)
    late_copies = slab_copies(state, late, late_whole, late_sems)
    start_copies(early_copies)
    start_copies(late_copies)
    wait_copies(early_copies)
    wait_copies(late_copies)
    for held, leads, tails in ((late_whole, (0, 1, 2), 0), (early_whole, (3, 4), 1)):
        height = held.shape[0] // adapters
        for a in range(adapters):
            rows = held[a * height : (a + 1) * height, :].astype(F32)
            for i, j in enumerate(leads):
                lead[j, a] = rows[i * rank : (i + 1) * rank]
            tail[tails, a] = rows[len(leads) * rank :]


def whole_width(line, early, late, adapters, rank):
    width = early[0].shape[1]
    full = 4 * width
    return line.call(
        whole_width_kernel,
        "whole_width",
        (1,),
        (*early, *late),
        [ANY] * 12,
        (
            jax.ShapeDtypeStruct((5, adapters, rank, full), F32),
            jax.ShapeDtypeStruct((2, adapters, rank, full), F32),
        ),
        (out_whole((5, adapters, rank, full)), out_whole((2, adapters, rank, full))),
        [
            pltpu.VMEM((early[0].shape[0], full), BF16),
            pltpu.VMEM((late[0].shape[0], full), BF16),
            pltpu.SemaphoreType.DMA((4,)),
            pltpu.SemaphoreType.DMA((4,)),
        ],
    )


class AdapterSums:
    def __init__(self, line, split, shared, adapters, slabs):
        full = shared[0][0].shape[-1]
        width = full // slabs
        self.line, self.split = line, split
        self.adapters, self.width = adapters, width
        self.n_shared = sum(x.size // full for x, _ in shared)
        n_split = sum(x.size // width for x, _ in split) + 16
        arrays = [x for pair in shared + split for x in pair]
        slab = (self.n_shared, width)
        far, beside, self.own, self.sent = line.call(
            functools.partial(wire_kernel, len(shared), len(shared) + len(split)),
            "wire",
            (1,),
            arrays,
            [whole(x) for x in arrays],
            tuple(
                jax.ShapeDtypeStruct(shape, BF16)
                for shape in ((2, *slab), slab, slab, (n_split, width))
            ),
            tuple(out_whole(shape) for shape in ((2, *slab), slab, slab, (n_split, width))),
            [pltpu.VMEM((self.n_shared, full), BF16)],
        )
        self.slab_sum = SlabSum(line, (far, beside, self.own))

    def cross(self):
        self.slab_sum.cross()

    def join(self):
        rows = self.own.shape[0] + self.sent.shape[0]
        ins = (*self.slab_sum.terms, self.sent)
        sent = self.line.call(
            join_kernel,
            "join",
            (1,),
            ins,
            [whole(x) for x in ins],
            jax.ShapeDtypeStruct((rows, self.width), BF16),
            out_whole((rows, self.width)),
        )
        self.everyone = lax.all_gather(sent, "dp", axis=0, tiled=False)

    def combine(self):
        shapes = [(self.adapters, x.size // x.shape[-1], x.shape[-1]) for x, _ in self.split]
        shared = (self.adapters, self.n_shared, self.width)
        shared, *split = self.line.call(
            functools.partial(combine_kernel, self.n_shared, self.adapters),
            "combine",
            (1,),
            (self.everyone,),
            [whole(self.everyone)],
            (
                jax.ShapeDtypeStruct(shared, BF16),
                *(jax.ShapeDtypeStruct(shape, F32) for shape in shapes),
            ),
            (out_whole(shared), *(out_whole(shape) for shape in shapes)),
        )
        self.parts = spread(shared.reshape(-1, self.width), "pair")
        return split


def on_device(
    slabs,
    tokens,
    cotangent,
    norm_gains,
    query_key_value_matrix,
    output_matrix,
    gate_up_matrix,
    down_matrix,
    lead_factors,
    head_factors,
    unit_factors,
    merge_factors,
    down_factors,
    tail_factors,
    doc_ids,
    keep_mask,
    adapter_pick,
):
    length = tokens.shape[1]
    rows = length // CHUNKS
    chosen = adapter_pick[0, 0]
    state = jnp.stack([lax.axis_index("tensor").astype(jnp.int32), chosen])
    line = Line(state)
    gains = norm_gains.astype(F32)
    lead = jnp.swapaxes(lead_factors, 2, 3)
    merge = jnp.swapaxes(merge_factors, 1, 2)
    down = jnp.swapaxes(down_factors, 1, 2)
    cosine, sine = rope_tables(length)
    doc_column = doc_ids.reshape(length, 1)

    def cut(array, c):
        return array[c * rows : (c + 1) * rows]

    own_tokens = [cut(tokens[0], c) for c in range(CHUNKS)]
    token_parts = [spread(own, MODES["tok"][c]) for c, own in enumerate(own_tokens)]
    own_cots = [cut(cotangent[0], c) for c in range(CHUNKS)]
    cot_parts = [spread(own, MODES["cot"][c]) for c, own in enumerate(own_cots)]

    def project_chunk(c, after=()):
        return project(
            line,
            token_parts[c],
            gains,
            lead,
            query_key_value_matrix,
            head_factors,
            cut(cosine, c),
            cut(sine, c),
            after,
        )

    def attend_chunk(c, qkvs, after=()):
        return attend(
            line,
            qkvs,
            c,
            doc_column,
            doc_ids,
            keep_mask,
            output_matrix,
            merge,
            tail_factors,
            slabs,
            MODES["branch"][c],
            after,
        )

    def feed_chunk(c, parts, after=()):
        return feed_forward(
            line,
            parts,
            cot_parts[c],
            gains,
            lead,
            gate_up_matrix,
            down_matrix,
            unit_factors,
            down,
            tail_factors,
            (MODES["feed"][c], MODES["back"][c]),
            after,
        )

    def attend_back_chunk(c, parts, after=()):
        return attend_back(
            line,
            parts,
            qkvs[: c + 1],
            c,
            doc_column,
            doc_ids,
            keep_mask,
            attended[c],
            output_matrix,
            merge,
            tail_factors,
            after,
        )

    def project_back_chunk(c, query_grad, later, after=()):
        normed, mid, scale = saved[c]
        return project_back(
            line,
            query_grad,
            later,
            c,
            query_key_value_matrix,
            head_factors,
            lead,
            gains,
            normed,
            mid,
            scale,
            cut(cosine, c),
            cut(sine, c),
            slabs,
            MODES["last"][c],
            after,
        )

    adapters = lead_factors.shape[1]
    qkv0, *saved0 = project_chunk(0)
    attended0, *branch0 = attend_chunk(0, [qkv0])
    branch0 = SlabSum(line, branch0)
    qkv1, *saved1 = project_chunk(1)
    qkvs, saved = [qkv0, qkv1], [saved0, saved1]
    attended1, *branch1 = attend_chunk(1, qkvs, tuple(cot_parts[0][1:4]))
    attended = [attended0, attended1]
    branch1 = SlabSum(line, branch1)
    hidden0, rounded0 = branch0.finish(own_tokens[0], tuple(cot_parts[0][4:]))
    hidden_parts0 = spread(rounded0, MODES["hidden"][0])
    branch1.cross(tuple(cot_parts[1][1:4]))
    hidden1, rounded1 = branch1.finish(own_tokens[1], tuple(cot_parts[1][4:]))
    hidden_parts1 = spread(rounded1, MODES["hidden"][1])
    feed0, back0, unit_grads0 = feed_chunk(0, hidden_parts0)
    back0 = SlabSum(line, back0)
    feed1, back1, unit_grads1 = feed_chunk(1, hidden_parts1)
    back1 = SlabSum(line, back1)
    grad0, rounded0 = back0.finish(own_cots[0])
    grad_parts0 = spread(rounded0, MODES["grad"][0])
    back1.cross()
    grad1, rounded1 = back1.finish(own_cots[1])
    grad_parts1 = spread(rounded1, MODES["grad"][1])
    feed0_far, feed0_beside, feed1_far, feed1_beside = relay(line, (*feed0[:2], *feed1[:2]))
    feed0 = SlabSum(line, [feed0_far, feed0_beside, feed0[2]])
    query_grad0, key_grad0, value_grad0, *merge_grads0 = attend_back_chunk(0, grad_parts0)
    early = AdapterSums(
        line,
        list(zip(unit_grads0, unit_grads1))[:2],
        list(zip(unit_grads0, unit_grads1))[2:],
        adapters,
        slabs,
    )
    feed0.cross()
    feed1 = SlabSum(line, [feed1_far, feed1_beside, feed1[2]])
    query_grad1, key_grad1, value_grad1, *merge_grads1 = attend_back_chunk(1, grad_parts1)
    early.cross()
    feed1.cross()
    last1, *head_grads1 = project_back_chunk(1, query_grad1, [key_grad1, value_grad1])
    last1 = SlabSum(line, last1)
    early.join()
    _, out0 = feed0.finish(hidden0)
    last0, *head_grads0 = project_back_chunk(
        0, query_grad0, [key_grad0, value_grad0, key_grad1, value_grad1]
    )
    last0 = SlabSum(line, last0)
    (head0, lead0), (head1, lead1) = head_grads0, head_grads1
    (merge0, tail0), (merge1, tail1) = merge_grads0, merge_grads1
    late = AdapterSums(
        line,
        [(head0, head1), (merge0, merge1)],
        [(lead0, lead1), (tail0, tail1)],
        adapters,
        slabs,
    )
    layer_out = feed1.finish_after(hidden1, out0)
    late.cross()
    late.join()
    last0.cross()
    unit_all, down_all = early.combine()
    _, tokens_grad1 = last1.finish(grad1)
    head_all, merge_all = late.combine()
    _, tokens_grad0 = last0.finish(grad0)
    rank = lead_factors.shape[3]
    lead_all, tail_all = whole_width(line, early.parts, late.parts, adapters, rank)

    def ranked(array):
        return jnp.swapaxes(array.reshape(adapters, -1, rank, array.shape[-1]), 0, 1)

    return (
        layer_out[None],
        jnp.concatenate([tokens_grad0, tokens_grad1])[None],
        jnp.swapaxes(lead_all, 2, 3),
        ranked(head_all),
        ranked(unit_all),
        jnp.swapaxes(merge_all, 1, 2),
        jnp.swapaxes(down_all, 1, 2),
        tail_all,
    )


def solution(mesh):
    return jax.shard_map(
        functools.partial(on_device, mesh.shape["tensor"]),
        mesh=mesh,
        in_specs=(
            P("dp", None, "tensor"),
            P("dp", None, "tensor"),
            P(),
            P(None, None, "tensor"),
            P("tensor", None),
            P(None, None, "tensor"),
            P("tensor", None),
            P(),
            P(None, None, None, "tensor"),
            P(None, None, None, "tensor"),
            P(None, "tensor", None),
            P(None, "tensor", None),
            P(),
            P("dp", None),
            P("dp", None),
            P("dp", None),
        ),
        out_specs=(
            P("dp", None, "tensor"),
            P("dp", None, "tensor"),
            P(),
            P(None, None, None, "tensor"),
            P(None, None, None, "tensor"),
            P(None, "tensor", None),
            P(None, "tensor", None),
            P(),
        ),
        check_vma=False,
    )
```

time: 1750 us -> 833 us (0.48)
  waiting for transfers between devices: 1370 us -> 392 us
  Pallas kernels: 0 us -> 308 us
  matrix products: 242 us -> 0 us
  starting transfers between devices: 0.28 us -> 80.6 us
  other arithmetic: 71.8 us -> 6.13 us
    psum x5 -> x0, waiting for transfers between devices: 1270 us -> none  [the longest x1 540 us: on_device(): whole_feed = lax.psum(feedforward_portion, 'tensor')]
    ppermute x0 -> x48, waiting for transfers between devices: none -> 323 us  [the longest x7 84.1 us: cross(): far = lax.ppermute(far, 'tensor', ACROSS)]
    pallas_call x0 -> x33, Pallas kernels: none -> 308 us  [call(): pl.pallas_call(body, name=name, grid_spec=pltpu.PrefetchScalarGridSpec(nu...]
    dot_general x44 -> x0, matrix products: 242 us -> none  [the longest x1 23.2 us: on_device(): jnp.einsum('td,kdf->ktf', second_normalized, gate_up_matrix, preferred_el...]
    ppermute x0 -> x48, starting transfers between devices: none -> 80.2 us  [the longest x4 18.8 us: spread(): far = lax.ppermute(own, 'tensor', OVER)]
    all_gather x2 -> x8, waiting for transfers between devices: 98.2 us -> 67.7 us  [the longest x6 67.7 us: spread(): return [lax.all_gather(own, 'tensor', axis=0, tiled=False)]]
    reduce_sum x6 -> x0, other arithmetic: 26.4 us -> none  [the longest x2 12.7 us: norm_back(): jnp.mean(scaled * stream, axis=1, keepdims=True)]
    convert_element_type x4 -> x1, other arithmetic: 18.6 us -> 0.61 us  [on_device(): gains = norm_gains.astype(F32)]
  transfers between devices with their start and end apart: 7 -> 59, of which waited for: 7 -> 23; matrix products, arithmetic and copies ran while one was open for 8% -> 1% of each run, Pallas kernels for 0% -> 36%
where the time goes in v1:
time: 833 us; the launch traced here: 823 us
  waiting for transfers between devices  392 us (47%)
  Pallas kernels  308 us (37%)
  starting transfers between devices  80.6 us (10%)
  local copies, waits for them, and re-layouts  20.6 us (2%)
  between operations  15.9 us (2%)
    pallas_call x33, Pallas kernels, call(): pl.pallas_call(body, name=name, grid_spec=pltpu.PrefetchScalarGridSpec(nu...  308 us
    ppermute x7, waiting for transfers between devices, cross(): far = lax.ppermute(far, 'tensor', ACROSS)  84.1 us
    ppermute x4, waiting for transfers between devices, spread(): far = lax.ppermute(own, 'tensor', OVER)  77.5 us
    ppermute x7, waiting for transfers between devices, __init__(): self.received = lax.ppermute(parts[0], 'tensor', INWARD)  76.1 us
    all_gather x6, waiting for transfers between devices, spread(): return [lax.all_gather(own, 'tensor', axis=0, tiled=False)]  67.7 us
    ppermute x7, waiting for transfers between devices, cross(): beside = lax.ppermute(beside, 'tensor', BESIDE)  30.9 us
    ppermute x4, waiting for transfers between devices, spread(): lax.ppermute(far, 'tensor', OUTWARD)  23.8 us
    ppermute x4, starting transfers between devices, spread(): far = lax.ppermute(own, 'tensor', OVER)  18.8 us
  transfers between devices with their start and end apart: 59, of which 23 were waited for; matrix products, arithmetic and copies ran while one was open for 1% of the time, Pallas kernels for 36%

profile of v1, /device:TPU:0, one launch (start us, length us, event | category | flops | bytes accessed | tf_op | source)
XLA Modules:
  0.0 823.3 jit_solution(5557580617614083523)
XLA Ops:
  18.1 40.7 %all-gather.15.cloned.1.call-done.refs_1_ = bf16[4,512,512]{2,1,0:T(8,128)(2,1)} async-done(((bf16[1,512,512]{2,1,0:T(8,128)(2,1)}), bf16[4,512,512]{2,1,0:T(8,128)(2,1)}) %all-gather.15.cloned.1.call-update) | async-done | bytes 2097168 | tf_op jit(solution)/shard_map/all_gather | solution.py:69
  58.8 13.4 %project.2 = (bf16[3,512,512]{2,1,0:T(8,128)(2,1)}, bf16[512,2048]{1,0:T(8,128)(2,1)}, bf16[3,512,16]{2,1,0:T(8,128)(2,1)}, f32[512,1]{1,0:T(8,128)}) custom-call(s32[2]{0:T(128)} %pad_add_fusion.refs_0_, bf16[4,512,512]{2,1,0:T(8,128)(2,1)} %all-gather.15.cloned.1.call-done.refs_1_, f32[2,2048]{1,0:T(2,128)} %convert_element_type.3.refs_2_.refs_8_.refs_7_.refs_9_, ...), custom_call_target="tpu_custom_call" | custom-call | flops 1 | bytes 1 | tf_op jit(solution)/shard_map/project/pallas_call | solution.py:295
  72.2 14.5 %attend.2 = (bf16[512,512]{1,0:T(8,128)(2,1)}, bf16[4,512,512]{2,1,0:T(8,128)(2,1)}) custom-call(s32[2]{0:T(128)} %pad_add_fusion.refs_0_, bf16[3,512,512]{2,1,0:T(8,128)(2,1)} %get-tuple-element.110.refs_1_.refs_2_.refs_3_.refs_4_, bf16[3,512,512]{2,1,0:T(8,128)(2,1)} %get-tuple-element.110.refs_1_.refs_2_.refs_3_.refs_4_, ...), custom_call_target="tpu_custom_call" | custom-call | flops 1 | bytes 1 | tf_op jit(solution)/shard_map/attend/pallas_call | solution.py:295
  94.6 19.2 %collective-permute-done.2.refs_15_.refs_5_ = bf16[512,512]{1,0:T(8,128)(2,1)S(1)} collective-permute-done((bf16[512,512]{1,0:T(8,128)(2,1)S(1)}, bf16[512,512]{1,0:T(8,128)(2,1)S(1)}, u32[]{:S(2)}, u32[]{:S(2)}) %collective-permute-start.2) | collective-permute-done | bytes 524320 | tf_op jit(solution)/shard_map/ppermute | solution.py:72
  123.7 13.4 %project.3 = (bf16[3,512,512]{2,1,0:T(8,128)(2,1)}, bf16[512,2048]{1,0:T(8,128)(2,1)}, bf16[3,512,16]{2,1,0:T(8,128)(2,1)}, f32[512,1]{1,0:T(8,128)}) custom-call(s32[2]{0:T(128)} %pad_add_fusion.refs_0_, bf16[4,512,512]{2,1,0:T(8,128)(2,1)} %all-gather.17.cloned.1.call-done.refs_1_, f32[2,2048]{1,0:T(2,128)} %convert_element_type.3.refs_2_.refs_8_.refs_7_.refs_9_, ...), custom_call_target="tpu_custom_call" | custom-call | flops 1 | bytes 1 | tf_op jit(solution)/shard_map/project/pallas_call | solution.py:295
  137.9 17.1 %attend.3 = (bf16[512,512]{1,0:T(8,128)(2,1)}, bf16[2,512,512]{2,1,0:T(8,128)(2,1)}, bf16[512,512]{1,0:T(8,128)(2,1)}, bf16[512,512]{1,0:T(8,128)(2,1)}) custom-call(s32[2]{0:T(128)} %pad_add_fusion.refs_0_, bf16[3,512,512]{2,1,0:T(8,128)(2,1)} %get-tuple-element.110.refs_1_.refs_2_.refs_3_.refs_4_, ...), custom_call_target="tpu_custom_call" | custom-call | flops 1 | bytes 1 | tf_op jit(solution)/shard_map/attend/pallas_call | solution.py:295
  165.1 21.7 %collective-permute-done.4.refs_5_.refs_7_ = bf16[512,512]{1,0:T(8,128)(2,1)} collective-permute-done((bf16[512,512]{1,0:T(8,128)(2,1)S(1)}, bf16[512,512]{1,0:T(8,128)(2,1)}, u32[]{:S(2)}, u32[]{:S(2)}) %collective-permute-start.4) | collective-permute-done | bytes 524320 | tf_op jit(solution)/shard_map/ppermute | solution.py:79
  197.2 58.3 %collective-permute-done.8.refs_7_.refs_5_ = bf16[512,512]{1,0:T(8,128)(2,1)S(1)} collective-permute-done((bf16[512,512]{1,0:T(8,128)(2,1)S(1)}, bf16[512,512]{1,0:T(8,128)(2,1)S(1)}, u32[]{:S(2)}, u32[]{:S(2)}) %collective-permute-start.8) | collective-permute-done | bytes 524320 | tf_op jit(solution)/shard_map/ppermute | solution.py:72
  256.8 13.0 %collective-permute-done.6.refs_5_.refs_3_ = bf16[512,512]{1,0:T(8,128)(2,1)S(1)} collective-permute-done((bf16[512,512]{1,0:T(8,128)(2,1)S(1)}, bf16[512,512]{1,0:T(8,128)(2,1)S(1)}, u32[]{:S(2)}, u32[]{:S(2)}) %collective-permute-start.6) | collective-permute-done | bytes 524320 | tf_op jit(solution)/shard_map/ppermute | solution.py:70
  279.8 22.2 %collective-permute-done.11.refs_5_ = bf16[512,512]{1,0:T(8,128)(2,1)S(1)} collective-permute-done((bf16[512,512]{1,0:T(8,128)(2,1)}, bf16[512,512]{1,0:T(8,128)(2,1)S(1)}, u32[]{:S(2)}, u32[]{:S(2)}) %collective-permute-start.11) | collective-permute-done | bytes 524320 | tf_op jit(solution)/shard_map/ppermute | solution.py:241
  306.5 46.5 %feed_forward.2 = (bf16[2,512,512]{2,1,0:T(8,128)(2,1)}, bf16[512,512]{1,0:T(8,128)(2,1)}, bf16[512,512]{1,0:T(8,128)(2,1)}, bf16[4,512,512]{2,1,0:T(8,128)(2,1)...) custom-call(s32[2]{0:T(128)} %pad_add_fusion.refs_0_, ...), custom_call_target="tpu_custom_call" | custom-call | flops 1 | bytes 1 | tf_op jit(solution)/shard_map/feed_forward/pallas_call | solution.py:295
  353.2 47.3 %feed_forward.3 = (bf16[2,512,512]{2,1,0:T(8,128)(2,1)}, bf16[512,512]{1,0:T(8,128)(2,1)}, bf16[512,512]{1,0:T(8,128)(2,1)}, bf16[2,512,512]{2,1,0:T(8,128)(2,1)...) custom-call(s32[2]{0:T(128)} %pad_add_fusion.refs_0_, ...), custom_call_target="tpu_custom_call" | custom-call | flops 1 | bytes 1 | tf_op jit(solution)/shard_map/feed_forward/pallas_call | solution.py:295
  404.9 39.1 %collective-permute-done.14.refs_2_ = bf16[2,512,512]{2,1,0:T(8,128)(2,1)S(1)} collective-permute-done((bf16[2,512,512]{2,1,0:T(8,128)(2,1)}, bf16[2,512,512]{2,1,0:T(8,128)(2,1)S(1)}, u32[]{:S(2)}, u32[]{:S(2)}) %collective-permute-start.14) | collective-permute-done | bytes 1048608 | tf_op jit(solution)/shard_map/ppermute | solution.py:222
  452.7 19.5 %collective-permute-done.15.refs_3_ = bf16[512,512]{1,0:T(8,128)(2,1)S(1)} collective-permute-done((bf16[512,512]{1,0:T(8,128)(2,1)}, bf16[512,512]{1,0:T(8,128)(2,1)S(1)}, u32[]{:S(2)}, u32[]{:S(2)}) %collective-permute-start.15) | collective-permute-done | bytes 524320 | tf_op jit(solution)/shard_map/ppermute | solution.py:242
  472.2 10.7 %collective-permute-done.17.refs_5_ = bf16[512,512]{1,0:T(8,128)(2,1)S(1)} collective-permute-done((bf16[512,512]{1,0:T(8,128)(2,1)}, bf16[512,512]{1,0:T(8,128)(2,1)S(1)}, u32[]{:S(2)}, u32[]{:S(2)}) %collective-permute-start.17) | collective-permute-done | bytes 524320 | tf_op jit(solution)/shard_map/ppermute | solution.py:241
  494.2 19.8 %attend_back.2 = (f32[512,512]{1,0:T(8,128)}, f32[512,512]{1,0:T(8,128)}, f32[512,512]{1,0:T(8,128)}, f32[16,512]{1,0:T(8,128)}, f32[16,2048]{1,0:T(8,128)}) custom-call(s32[2]{0:T(128)} %pad_add_fusion.refs_0_, bf16[4,512,512]{2,1,0:T(8,128)(2,1)} %bitcast.48, bf16[3,512,512]{2,1,0:T(8,128)(2,1)} %get-tuple-element.110.refs_1_.refs_2_.refs_3_.refs_4_, ...), custom_call_target="tpu_custom_call" | custom-call | flops 1 | bytes 1 | tf_op jit(solution)/shard_map/attend_back/pallas_call | solution.py:295
  518.2 20.7 %collective-permute-done.18.refs_2_ = bf16[2,512,512]{2,1,0:T(8,128)(2,1)S(1)} collective-permute-done((bf16[2,512,512]{2,1,0:T(8,128)(2,1)}, bf16[2,512,512]{2,1,0:T(8,128)(2,1)S(1)}, u32[]{:S(2)}, u32[]{:S(2)}) %collective-permute-start.18) | collective-permute-done | bytes 1048608 | tf_op jit(solution)/shard_map/ppermute | solution.py:222
  543.4 18.4 %all-gather.25.cloned.1.call-done = bf16[2048,512]{1,0:T(8,128)(2,1)} async-done(((bf16[512,512]{1,0:T(8,128)(2,1)}), bf16[2048,512]{1,0:T(8,128)(2,1)}) %all-gather.25.cloned.1.call-update) | async-done | bytes 2097168 | tf_op jit(solution)/shard_map/all_gather | solution.py:69
  561.8 24.5 %attend_back.3 = (f32[512,512]{1,0:T(8,128)}, f32[1024,512]{1,0:T(8,128)}, f32[1024,512]{1,0:T(8,128)}, f32[16,512]{1,0:T(8,128)}, f32[16,2048]{1,0:T(8,128)}) custom-call(s32[2]{0:T(128)} %pad_add_fusion.refs_0_, bf16[4,512,512]{2,1,0:T(8,128)(2,1)} %bitcast.51, bf16[3,512,512]{2,1,0:T(8,128)(2,1)} %get-tuple-element.110.refs_1_.refs_2_.refs_3_.refs_4_, ...), custom_call_target="tpu_custom_call" | custom-call | flops 1 | bytes 1 | tf_op jit(solution)/shard_map/attend_back/pallas_call | solution.py:295
  598.5 16.4 %project_back.2 = (bf16[4,512,512]{2,1,0:T(8,128)(2,1)}, f32[3,16,512]{2,1,0:T(8,128)}, f32[3,16,2048]{2,1,0:T(8,128)}) custom-call(s32[2]{0:T(128)} %pad_add_fusion.refs_0_, f32[512,512]{1,0:T(8,128)} %get-tuple-element.163.refs_1_, f32[1024,512]{1,0:T(8,128)} %get-tuple-element.164.refs_2_.refs_4_, f32[1024,512]{1,0:T(8,128)} %get-tuple-element.165.refs_3_.refs_5_, ...), custom_call_target="tpu_custom_call" | custom-call | flops 1 | bytes 1 | tf_op jit(solution)/shard_map/project_back/pallas_call | solution.py:295
  637.8 13.6 %collective-permute-done.21.refs_5_ = bf16[512,512]{1,0:T(8,128)(2,1)S(1)} collective-permute-done((bf16[512,512]{1,0:T(8,128)(2,1)}, bf16[512,512]{1,0:T(8,128)(2,1)S(1)}, u32[]{:S(2)}, u32[]{:S(2)}) %collective-permute-start.21) | collective-permute-done | bytes 524320 | tf_op jit(solution)/shard_map/ppermute | solution.py:241
  656.0 17.2 %project_back.3 = (bf16[2,512,512]{2,1,0:T(8,128)(2,1)}, bf16[512,512]{1,0:T(8,128)(2,1)}, bf16[512,512]{1,0:T(8,128)(2,1)}, f32[3,16,512]{2,1,0:T(8,128)}, f32[3,16,2048]{2,1,0:T(8,128)}) custom-call(s32[2]{0:T(128)} %pad_add_fusion.refs_0_, f32[512,512]{1,0:T(8,128)} %get-tuple-element.176.refs_1_, f32[512,512]{1,0:T(8,128)} %get-tuple-element.177.refs_2_, ...), custom_call_target="tpu_custom_call" | custom-call | flops 1 | bytes 1 | tf_op jit(solution)/shard_map/project_back/pallas_call | solution.py:295
  677.2 25.9 %collective-permute-done.29.refs_6_ = bf16[512,512]{1,0:T(8,128)(2,1)S(1)} collective-permute-done((bf16[512,512]{1,0:T(8,128)(2,1)}, bf16[512,512]{1,0:T(8,128)(2,1)S(1)}, u32[]{:S(2)}, u32[]{:S(2)}) %collective-permute-start.29) | collective-permute-done | bytes 524320 | tf_op jit(solution)/shard_map/ppermute | solution.py:241
  725.6 16.2 %collective-permute-done.30.refs_2_ = bf16[2,512,512]{2,1,0:T(8,128)(2,1)S(1)} collective-permute-done((bf16[2,512,512]{2,1,0:T(8,128)(2,1)S(1)}, bf16[2,512,512]{2,1,0:T(8,128)(2,1)S(1)}, u32[]{:S(2)}, u32[]{:S(2)}) %collective-permute-start.30) | collective-permute-done | bytes 1048608 | tf_op jit(solution)/shard_map/ppermute | solution.py:222
  (251 shorter events, 238.1 us)
Async XLA Ops:
  7.2 51.6 %all-gather.15.cloned.1.call-start = ((), (), s32[]{:S(2)}) async-start(), calls=%async_computation.3 | async-start | bytes 2621440 | tf_op jit(solution)/shard_map/all_gather | solution.py:69
  9.9 113.9 %all-gather.17.cloned.1.call-start = ((), (), s32[]{:S(2)}) async-start(), calls=%async_computation.5 | async-start | bytes 2621440 | tf_op jit(solution)/shard_map/all_gather | solution.py:69
  10.6 176.2 %reduce-scatter.4.cloned.1.call-start = ((), (), s32[]{:S(2)}) async-start(), calls=%async_computation.4 | async-start | bytes 2621440 | tf_op jit(solution)/shard_map/reduce_scatter | solution.py:219
  86.7 219.8 %all-gather.19.cloned.1.call-start = ((), (), s32[]{:S(2)}) async-start(), calls=%async_computation.8 | async-start | bytes 2621440 | tf_op jit(solution)/shard_map/all_gather | solution.py:69
  93.2 43.9 %collective-permute-start = (bf16[512,512]{1,0:T(8,128)(2,1)S(1)}, bf16[512,512]{1,0:T(8,128)(2,1)S(1)}, u32[]{:S(2)}, u32[]{:S(2)}) collective-permute-start(bf16[512,512]{1,0:T(8,128)(2,1)S(1)} %get-tuple-element.213.refs_2_.refs_1_), channel_id=1, source_target_pairs={{0,1},{1,0},{2,3},{3,2},{4,5},{5,4},{6,7},{7,6},{8,9},{9,8},{10,11... | collective-permute-start | bytes 1572872 | tf_op jit(solution)/shard_map/ppermute | solution.py:70
  93.3 71.8 %collective-permute-start.3 = (bf16[512,512]{1,0:T(8,128)(2,1)S(1)}, bf16[512,512]{1,0:T(8,128)(2,1)S(1)}, u32[]{:S(2)}, u32[]{:S(2)}) collective-permute-start(bf16[512,512]{1,0:T(8,128)(2,1)S(1)} %collective-permute-done.1.refs_14_.refs_4_), channel_id=1, source_target_pairs={{1,0},{2,3},{5,4},{6,7},{9,8},{10,11},{13,12},{14,15},{17,16},{18,... | collective-permute-start | bytes 1572872 | tf_op jit(solution)/shard_map/ppermute | solution.py:78
  113.8 73.0 %collective-permute-start.4 = (bf16[512,512]{1,0:T(8,128)(2,1)S(1)}, bf16[512,512]{1,0:T(8,128)(2,1)}, u32[]{:S(2)}, u32[]{:S(2)}) collective-permute-start(bf16[512,512]{1,0:T(8,128)(2,1)S(1)} %collective-permute-done.2.refs_15_.refs_5_), channel_id=1, source_target_pairs={{1,0},{2,3},{5,4},{6,7},{9,8},{10,11},{13,12},{14,15},{17,16},{18,... | collective-permute-start | bytes 1572872 | tf_op jit(solution)/shard_map/ppermute | solution.py:79
  189.7 163.4 %all-gather.21.cloned.1.call-start = ((), (), s32[]{:S(2)}) async-start(), calls=%async_computation.9 | async-start | bytes 2621440 | tf_op jit(solution)/shard_map/all_gather | solution.py:69
  189.8 80.1 %collective-permute-start.5 = (bf16[2,512,512]{2,1,0:T(8,128)(2,1)}, bf16[2,512,512]{2,1,0:T(8,128)(2,1)}, u32[]{:S(2)}, u32[]{:S(2)}) collective-permute-start(bf16[2,512,512]{2,1,0:T(8,128)(2,1)} %get-tuple-element.118.refs_1_), channel_id=1, source_target_pairs={{0,1},{3,2},{4,5},{7,6},{8,9},{11,10},{12,13},{15,14},{16,17},{19,... | collective-permute-start | bytes 3145736 | tf_op jit(solution)/shard_map/ppermute | solution.py:222
  192.8 62.8 %collective-permute-start.8 = (bf16[512,512]{1,0:T(8,128)(2,1)S(1)}, bf16[512,512]{1,0:T(8,128)(2,1)S(1)}, u32[]{:S(2)}, u32[]{:S(2)}) collective-permute-start(bf16[512,512]{1,0:T(8,128)(2,1)S(1)} %get-tuple-element.212.refs_2_.refs_1_), channel_id=1, source_target_pairs={{0,2},{3,1},{4,6},{7,5},{8,10},{11,9},{12,14},{15,13},{16,18},{19,... | collective-permute-start | bytes 1572872 | tf_op jit(solution)/shard_map/ppermute | solution.py:72
  195.8 74.0 %collective-permute-start.6 = (bf16[512,512]{1,0:T(8,128)(2,1)S(1)}, bf16[512,512]{1,0:T(8,128)(2,1)S(1)}, u32[]{:S(2)}, u32[]{:S(2)}) collective-permute-start(bf16[512,512]{1,0:T(8,128)(2,1)S(1)} %get-tuple-element.212.refs_2_.refs_1_), channel_id=1, source_target_pairs={{0,1},{1,0},{2,3},{3,2},{4,5},{5,4},{6,7},{7,6},{8,9},{9,8},{10,11... | collective-permute-start | bytes 1572872 | tf_op jit(solution)/shard_map/ppermute | solution.py:70
  195.9 83.8 %collective-permute-start.12 = (bf16[512,512]{1,0:T(8,128)(2,1)S(1)}, bf16[512,512]{1,0:T(8,128)(2,1)S(1)}, u32[]{:S(2)}, u32[]{:S(2)}) collective-permute-start(bf16[512,512]{1,0:T(8,128)(2,1)S(1)} %collective-permute-done.7.refs_6_.refs_4_), channel_id=1, source_target_pairs={{1,0},{2,3},{5,4},{6,7},{9,8},{10,11},{13,12},{14,15},{17,16},{18,... | collective-permute-start | bytes 1572872 | tf_op jit(solution)/shard_map/ppermute | solution.py:78
  306.5 94.0 %reduce-scatter.6.cloned.1.call-start = ((), (), s32[]{:S(2)}) async-start(), calls=%async_computation.6 | async-start | bytes 2621440 | tf_op jit(solution)/shard_map/reduce_scatter | solution.py:219
  353.1 141.1 %all-gather.23.cloned.1.call-start = ((), (), s32[]{:S(2)}) async-start(), calls=%async_computation.10 | async-start | bytes 2621440 | tf_op jit(solution)/shard_map/all_gather | solution.py:69
  403.4 158.3 %all-gather.25.cloned.1.call-start = ((), (), s32[]{:S(2)}) async-start(), calls=%async_computation.11 | async-start | bytes 2621440 | tf_op jit(solution)/shard_map/all_gather | solution.py:69
  487.2 263.4 %all-gather.29.cloned.1.call-start = ((), (), s32[]{:S(2)}) async-start(), calls=%async_computation.13 | async-start | bytes 2359296 | tf_op jit(solution)/shard_map/all_gather | solution.py:1019
  491.4 47.5 %collective-permute-start.18 = (bf16[2,512,512]{2,1,0:T(8,128)(2,1)}, bf16[2,512,512]{2,1,0:T(8,128)(2,1)S(1)}, u32[]{:S(2)}, u32[]{:S(2)}) collective-permute-start(bf16[2,512,512]{2,1,0:T(8,128)(2,1)} %get-tuple-element.140.refs_1_), channel_id=1, source_target_pairs={{0,1},{3,2},{4,5},{7,6},{8,9},{11,10},{12,13},{15,14},{16,17},{19,... | collective-permute-start | bytes 3145736 | tf_op jit(solution)/shard_map/ppermute | solution.py:222
  492.8 101.1 %collective-permute-start.26 = (bf16[2,512,512]{2,1,0:T(8,128)(2,1)}, bf16[2,512,512]{2,1,0:T(8,128)(2,1)S(1)}, u32[]{:S(2)}, u32[]{:S(2)}) collective-permute-start(bf16[2,512,512]{2,1,0:T(8,128)(2,1)} %get-tuple-element.168.refs_1_), channel_id=1, source_target_pairs={{0,1},{3,2},{4,5},{7,6},{8,9},{11,10},{12,13},{15,14},{16,17},{19,... | collective-permute-start | bytes 3145736 | tf_op jit(solution)/shard_map/ppermute | solution.py:222
  516.9 69.3 %collective-permute-start.22 = (bf16[2,48,512]{2,1,0:T(8,128)(2,1)}, bf16[2,48,512]{2,1,0:T(8,128)(2,1)S(1)}, u32[]{:S(2)}, u32[]{:S(2)}) collective-permute-start(bf16[2,48,512]{2,1,0:T(8,128)(2,1)} %get-tuple-element.156.refs_1_), channel_id=1, source_target_pairs={{0,1},{3,2},{4,5},{7,6},{8,9},{11,10},{12,13},{15,14},{16,17},{19,... | collective-permute-start | bytes 294920 | tf_op jit(solution)/shard_map/ppermute | solution.py:222
  618.1 137.5 %reduce-scatter.8.cloned.1.call-start = ((), (), s32[]{:S(2)}) async-start(), calls=%async_computation.7 | async-start | bytes 2621440 | tf_op jit(solution)/shard_map/reduce_scatter | solution.py:219
  618.7 140.0 %all-gather.27.cloned.1.call-start = ((), (), s32[]{:S(2)}) async-start(), calls=%async_computation.12 | async-start | bytes 1327104 | tf_op jit(solution)/shard_map/all_gather | solution.py:1019
  625.7 51.6 %collective-permute-start.27 = (bf16[512,512]{1,0:T(8,128)(2,1)S(1)}, bf16[512,512]{1,0:T(8,128)(2,1)S(1)}, u32[]{:S(2)}, u32[]{:S(2)}) collective-permute-start(bf16[512,512]{1,0:T(8,128)(2,1)S(1)} %copy-done.19), channel_id=1, source_target_pairs={{0,1},{1,0},{2,3},{3,2},{4,5},{5,4},{6,7},{7,6},{8,9},{9,8},{10,11... | collective-permute-start | bytes 1572872 | tf_op jit(solution)/shard_map/ppermute | solution.py:242
  627.1 50.2 %collective-permute-start.28 = (bf16[512,512]{1,0:T(8,128)(2,1)}, bf16[512,512]{1,0:T(8,128)(2,1)S(1)}, u32[]{:S(2)}, u32[]{:S(2)}) collective-permute-start(bf16[512,512]{1,0:T(8,128)(2,1)} %get-tuple-element.174), channel_id=1, source_target_pairs={{1,2},{2,1},{5,6},{6,5},{9,10},{10,9},{13,14},{14,13},{17,18},{18,... | collective-permute-start | bytes 1572872 | tf_op jit(solution)/shard_map/ppermute | solution.py:240
  636.5 66.7 %collective-permute-start.29 = (bf16[512,512]{1,0:T(8,128)(2,1)}, bf16[512,512]{1,0:T(8,128)(2,1)S(1)}, u32[]{:S(2)}, u32[]{:S(2)}) collective-permute-start(bf16[512,512]{1,0:T(8,128)(2,1)} %get-tuple-element.175), channel_id=1, source_target_pairs={{1,3},{2,0},{5,7},{6,4},{9,11},{10,8},{13,15},{14,12},{17,19},{18,... | collective-permute-start | bytes 1572872 | tf_op jit(solution)/shard_map/ppermute | solution.py:241
  (85 other events, 1407.3 us)
Sparse Core Ops, SparseCore 0:
  10.2 48.6 all-gather.14
  61.0 62.7 all-gather.16
  126.0 57.6 reduce-scatter.3
  189.8 74.3 all-gather.18
  306.6 46.1 all-gather.20
  355.0 42.5 reduce-scatter.5
  403.6 68.2 all-gather.22
  487.3 74.3 all-gather.24
  618.2 30.3 all-gather.28
  650.7 54.0 reduce-scatter.7
  724.3 22.5 all-gather.26

commit v2 on v1

--- a/solution.py
+++ b/solution.py
@@ -16,17 +16,18 @@
 LONGEST_DOC = 512
 CHUNKS = 2
 MODES = {
-    "tok": ("stack", "stack"),
-    "cot": ("pair", "pair"),
-    "branch": ("stack", "pair"),
+    "tok": "stack",
+    "cot": "stack",
+    "branch": ("pair", "pair"),
     "hidden": ("stack", "stack"),
-    "feed": ("pair", "pair"),
+    "feed": ("pair", "stack"),
     "back": ("stack", "pair"),
     "grad": ("stack", "stack"),
-    "last": ("pair", "stack"),
+    "last": ("pair", "pair"),
 }
 SUB_ROWS = 256
-VMEM_LIMIT = 60 * 1024 * 1024
+LARGE_VMEM = 60 * 1024 * 1024
+SMALL_VMEM = 30 * 1024 * 1024
 
 BESIDE = [(0, 1), (1, 0), (2, 3), (3, 2)]
 MIDDLE = [(1, 2), (2, 1)]
@@ -84,12 +85,13 @@
     return pl.ds(pl.multiple_of(slab * width, width), width)
 
 
-def slab_copies(state, parts, target, sems):
+def slab_copies(state, parts, target, sems, first=0):
+    here = pl.ds(first, target.shape[0])
     width = parts[0].shape[-1]
     if len(parts) == 1:
         return [
             (None, pltpu.make_async_copy(
-                parts[0].at[j], target.at[:, j * width : (j + 1) * width], sems.at[j]
+                parts[0].at[j, here], target.at[:, j * width : (j + 1) * width], sems.at[j]
             ))
             for j in range(parts[0].shape[0])
         ]
@@ -104,7 +106,7 @@
         (jnp.logical_not(inner), parts[5], far),
     )):
         copies.append((condition, pltpu.make_async_copy(
-            part, target.at[:, slab_columns(slab, width)], sems.at[sem % 4 + 2 * (sem // 4)]
+            part.at[here], target.at[:, slab_columns(slab, width)], sems.at[sem % 4 + 2 * (sem // 4)]
         )))
     return copies
 
@@ -177,15 +179,15 @@
     rounded[...] = total.astype(BF16)
 
 
-def sum_after_kernel(count, state, first, *refs):
+def sum_beside_kernel(chunk, count, state, other, *refs):
     terms, joined = refs[:-1], refs[-1]
-    step = pl.program_id(0)
-
-    @pl.when(step < count)
+    here = pl.program_id(0) // count == chunk
+
+    @pl.when(jnp.logical_not(here))
     def _():
-        joined[...] = first[...]
-
-    @pl.when(step >= count)
+        joined[...] = other[...]
+
+    @pl.when(here)
     def _():
         total = terms[0][...].astype(F32)
         for term in terms[1:]:
@@ -199,7 +201,7 @@
         target[...] = source[...]
 
 
-def relay(line, parts):
+def relay(line, parts, after=()):
     return line.call(
         relay_kernel,
         "relay",
@@ -208,6 +210,7 @@
         [whole(x) for x in parts],
         tuple(jax.ShapeDtypeStruct(x.shape, x.dtype) for x in parts),
         tuple(out_whole(x.shape) for x in parts),
+        after=after,
     )
 
 
@@ -258,26 +261,31 @@
         )
 
 
-    def finish_after(self, base, first):
+    def finish_beside(self, base, other, chunk):
         rows, width = base.shape
         step = min(256, rows)
         count = rows // step
-        flat = pl.BlockSpec((step, width), lambda i, s: (jnp.maximum(i - count, 0), 0))
+
+        def rows_of(c):
+            return pl.BlockSpec(
+                (step, width), lambda i, s: (jnp.clip(i - c * count, 0, count - 1), 0)
+            )
+
         return self.line.call(
-            functools.partial(sum_after_kernel, count),
-            "sum_after",
+            functools.partial(sum_beside_kernel, chunk, count),
+            "sum_beside",
             (2 * count,),
-            (first, base, *self.terms),
-            [pl.BlockSpec((step, width), lambda i, s: (jnp.minimum(i, count - 1), 0))]
-            + [flat] * (1 + len(self.terms)),
+            (other, base, *self.terms),
+            [rows_of(1 - chunk)] + [rows_of(chunk)] * (1 + len(self.terms)),
             jax.ShapeDtypeStruct((2 * rows, width), BF16),
             pl.BlockSpec((step, width), lambda i, s: (i, 0)),
         )
 
 
-def params(grid_rank=1):
+def params(name):
     return pltpu.CompilerParams(
-        dimension_semantics=("arbitrary",) * grid_rank, vmem_limit_bytes=VMEM_LIMIT
+        dimension_semantics=("arbitrary",),
+        vmem_limit_bytes=LARGE_VMEM if name == "feed_forward" else SMALL_VMEM,
     )
 
 
@@ -303,7 +311,7 @@
                 scratch_shapes=list(scratch),
             ),
             out_shape=outs,
-            compiler_params=params(len(grid)),
+            compiler_params=params(name),
             cost_estimate=pl.CostEstimate(flops=1, bytes_accessed=1, transcendentals=0),
         )(self.state, *ins, *after)
         self.last = (jax.tree.leaves(results)[-1],)
@@ -329,7 +337,7 @@
     return jnp.concatenate(groups, axis=-1)
 
 
-def project_kernel(n_parts, state, *refs):
+def project_kernel(first_row, n_parts, state, *refs):
     parts, refs = refs[:n_parts], refs[n_parts:]
     gain, lead, weight, head, cosine, sine, qkv, normed, mid, scale, stream, sems = refs
     step = pl.program_id(0)
@@ -337,7 +345,7 @@
 
     @pl.when(step == 0)
     def _():
-        copies = slab_copies(state, parts, stream, sems)
+        copies = slab_copies(state, parts, stream, sems, first_row)
         start_copies(copies)
         wait_copies(copies)
         for first in range(0, stream.shape[0], SUB_ROWS):
@@ -364,13 +372,13 @@
             qkv[0, here, :] = projected.astype(BF16)
 
 
-def project(line, parts, gains, lead, weight, head, cosine, sine, after=()):
-    rows = parts[0].shape[-2]
+def project(line, parts, chunk, gains, lead, weight, head, cosine, sine, after=()):
+    rows = cosine.shape[0]
     full, width = weight.shape[1:]
     rank = lead.shape[2]
     slabs = full // parts[0].shape[-1]
     return line.call(
-        functools.partial(project_kernel, len(parts)),
+        functools.partial(project_kernel, chunk * rows, len(parts)),
         "project",
         (3,),
         (*parts, gains, lead, weight, head, cosine, sine),
@@ -512,7 +520,7 @@
     return outs
 
 
-def feed_kernel(n_parts, n_cots, n_feed, n_back, state, *refs):
+def feed_kernel(first_row, n_parts, n_cots, n_feed, n_back, state, *refs):
     parts, refs = refs[:n_parts], refs[n_parts:]
     cot_parts, refs = refs[:n_cots], refs[n_cots:]
     gain, lead, gate_w, up_w, down_w, unit, down, tail = refs[:8]
@@ -529,7 +537,7 @@
     @pl.when(step == 0)
     def _():
         copies = slab_copies(state, parts, stream, sems)
-        cot_copies = slab_copies(state, cot_parts, upstream, cot_sems)
+        cot_copies = slab_copies(state, cot_parts, upstream, cot_sems, first_row)
         start_copies(copies)
         start_copies(cot_copies)
         wait_copies(copies)
@@ -602,7 +610,7 @@
 
 
 def feed_forward(
-    line, parts, cot_parts, gains, lead, gate_up, down_w, unit, down, tail, modes, after=()
+    line, parts, cot_parts, chunk, gains, lead, gate_up, down_w, unit, down, tail, modes, after=()
 ):
     feed_mode, back_mode = modes
     rows, slab_width = parts[0].shape[-2:]
@@ -614,7 +622,7 @@
     back_shapes, back_specs = slab_outs(back_mode, slabs, rows, slab_width)
     outs = line.call(
         functools.partial(
-            feed_kernel, len(parts), len(cot_parts), len(feed_shapes), len(back_shapes)
+            feed_kernel, chunk * rows, len(parts), len(cot_parts), len(feed_shapes), len(back_shapes)
         ),
         "feed_forward",
         (units // block,),
@@ -792,92 +800,128 @@
     )
 
 
-def project_back_kernel(n_later, n_outs, state, *refs):
-    query_grad, refs = refs[0], refs[1:]
-    later, refs = refs[: 2 * n_later], refs[2 * n_later :]
-    weight, head, lead, gain, normed, mid, scale, cosine, sine = refs[:9]
-    outs, refs = refs[9 : 9 + n_outs], refs[9 + n_outs :]
-    head_grad, lead_grad, total, held = refs
+def head_back_kernel(state, *refs):
+    query_grads, key_grads, value_grads = refs[0:2], refs[2:4], refs[4:6]
+    normed, mids = refs[6:8], refs[8:10]
+    head, cosine, sine = refs[10:13]
+    gradients, backs, head_grad, lead_grad = refs[13:]
+    rows = query_grads[0].shape[0]
+    rank = head.shape[2]
+    head_terms = [jnp.zeros(head_grad.shape[1:], F32) for _ in range(3)]
+    lead_term = jnp.zeros((3 * rank, lead_grad.shape[2]), F32)
+    for c in range(2):
+        for first in range(0, rows, SUB_ROWS):
+            here = pl.ds(first, SUB_ROWS)
+            there = pl.ds(c * rows + first, SUB_ROWS)
+            key, value = key_grads[1][there, :], value_grads[1][there, :]
+            if c == 0:
+                key, value = key + key_grads[0][here, :], value + value_grads[0][here, :]
+            tables = cosine[there, :], sine[there, :], -1.0
+            turned = (
+                rope_groups(query_grads[c][here, :], *tables),
+                rope_groups(key, *tables),
+                value,
+            )
+            back = []
+            for j in range(3):
+                gradient = turned[j].astype(BF16)
+                gradients[j, there, :] = gradient
+                back.append((SCALING * dot_nt(gradient, head[j, 0])).astype(BF16))
+                backs[j, there, :] = back[j]
+                head_terms[j] += dot_tn(mids[c][j, here, :], gradient)
+            lead_term += dot_tn(jnp.concatenate(back, axis=1), normed[c][here, :])
+    for j in range(3):
+        head_grad[j] = SCALING * head_terms[j]
+        lead_grad[j] = lead_term[j * rank : (j + 1) * rank]
+
+
+def head_back(line, query_grads, key_grads, value_grads, saved, head, cosine, sine):
+    rows, width = query_grads[0].shape
+    full = saved[0][0].shape[1]
+    rank = head.shape[2]
+    ins = (
+        *query_grads,
+        *key_grads,
+        *value_grads,
+        *(normed for normed, _, _ in saved),
+        *(mid for _, mid, _ in saved),
+    )
+    shapes = (
+        ((3, 2 * rows, width), BF16),
+        ((3, 2 * rows, rank), BF16),
+        ((3, rank, width), F32),
+        ((3, rank, full), F32),
+    )
+    return line.call(
+        head_back_kernel,
+        "head_back",
+        (1,),
+        (*ins, head, cosine, sine),
+        [whole(x) for x in ins]
+        + [
+            pl.BlockSpec(
+                (3, 1, rank, width), lambda i, s: (0, s[1], 0, 0), pipeline_mode=pl.Buffered(1)
+            ),
+            whole(cosine),
+            whole(sine),
+        ],
+        tuple(jax.ShapeDtypeStruct(*shape) for shape in shapes),
+        tuple(out_whole(shape) for shape, _ in shapes),
+    )
+
+
+def project_back_kernel(state, gradient, back, weight, lead, gain, normed, scale, *refs):
+    outs, total = refs[:-1], refs[-1]
     step = pl.program_id(0)
-
-    @pl.when(step == 0)
-    def _():
-        total[...] = jnp.zeros_like(total)
-        held[...] = rope_groups(query_grad[...], cosine[...], sine[...], -1.0).astype(BF16)
-
-    def added(which):
-        gradient = later[which][...]
-        for other in range(1, n_later):
-            gradient += later[2 * other + which][...]
-        return gradient
-
-    @pl.when(step == 1)
-    def _():
-        held[...] = rope_groups(added(0), cosine[...], sine[...], -1.0).astype(BF16)
-
-    @pl.when(step == 2)
-    def _():
-        held[...] = added(1).astype(BF16)
-
-    gradient = held[...]
-    values = normed[...]
-    back = (SCALING * dot_nt(gradient, head[0, 0])).astype(BF16)
-    head_grad[0] = SCALING * dot_tn(mid[0], gradient)
-    lead_grad[0] = dot_tn(back, values)
-    total[...] += dot_nt(gradient, weight[0]) + dot(back, lead[0, 0])
+    for first in range(0, total.shape[0], SUB_ROWS):
+        here = pl.ds(first, SUB_ROWS)
+        term = dot_nt(gradient[0, here, :], weight[0]) + dot(back[0, here, :], lead[0, 0])
+
+        @pl.when(step == 0)
+        def _():
+            total[here, :] = term
+
+        @pl.when(step > 0)
+        def _():
+            total[here, :] += term
 
     @pl.when(step == pl.num_programs(0) - 1)
     def _():
-        r1 = scale[...]
-        rows = values.astype(F32)
-        inner = jnp.mean(total[...] * rows, axis=1, keepdims=True)
-        total[...] = r1 * (gain[0:1, :] * total[...] - rows / gain[0:1, :] * inner)
+        for first in range(0, total.shape[0], SUB_ROWS):
+            here = pl.ds(first, SUB_ROWS)
+            held, r1 = total[here, :], scale[here, :]
+            rows = normed[here, :].astype(F32)
+            inner = jnp.mean(held * rows, axis=1, keepdims=True)
+            total[here, :] = r1 * (gain[0:1, :] * held - rows / gain[0:1, :] * inner)
         write_slabs(state, outs, lambda columns: total[:, columns])
 
 
-def project_back(line, query_grad, later, chunk, weight, head, lead, gains, normed, mid, scale, cosine, sine, slabs, mode, after=()):
-    rows, width = query_grad.shape
-    full = weight.shape[1]
+def project_back(
+    line, gradients, backs, chunk, weight, lead, gains, normed, scale, slabs, mode, after
+):
+    rows, full = normed.shape
+    width = gradients.shape[2]
     rank = lead.shape[2]
-    ins, specs = [query_grad], [whole(query_grad)]
-    for array in later:
-        ins.append(array)
-        specs.append(
-            pl.BlockSpec((rows, width), lambda j, s: (chunk, 0), pipeline_mode=pl.Buffered(1))
-        )
-    ins += [weight, head, lead, gains, normed, mid, scale, cosine, sine]
-    specs += [
-        pl.BlockSpec((1, full, width), lambda j, s: (j, 0, 0)),
-        pl.BlockSpec((1, 1, rank, width), lambda j, s: (j, s[1], 0, 0)),
-        pl.BlockSpec((1, 1, rank, full), lambda j, s: (j, s[1], 0, 0)),
-        whole(gains),
-        whole(normed),
-        pl.BlockSpec((1, rows, rank), lambda j, s: (j, 0, 0)),
-        whole(scale),
-        whole(cosine),
-        whole(sine),
-    ]
     shapes, out_specs = slab_outs(mode, slabs, rows, full // slabs)
-    outs = line.call(
-        functools.partial(project_back_kernel, len(later) // 2, len(shapes)),
+    return line.call(
+        project_back_kernel,
         "project_back",
         (3,),
-        ins,
-        specs,
-        shapes
-        + (
-            jax.ShapeDtypeStruct((3, rank, width), F32),
-            jax.ShapeDtypeStruct((3, rank, full), F32),
-        ),
-        out_specs
-        + (
-            pl.BlockSpec((1, rank, width), lambda j, s: (j, 0, 0)),
-            pl.BlockSpec((1, rank, full), lambda j, s: (j, 0, 0)),
-        ),
-        [pltpu.VMEM((rows, full), F32), pltpu.VMEM((rows, width), BF16)],
+        (gradients, backs, weight, lead, gains, normed, scale),
+        [
+            pl.BlockSpec((1, rows, width), lambda j, s: (j, chunk, 0)),
+            pl.BlockSpec((1, rows, rank), lambda j, s: (j, chunk, 0)),
+            pl.BlockSpec((1, full, width), lambda j, s: (j, 0, 0)),
+            pl.BlockSpec((1, 1, rank, full), lambda j, s: (j, s[1], 0, 0)),
+            whole(gains),
+            whole(normed),
+            whole(scale),
+        ],
+        shapes,
+        out_specs,
+        [pltpu.VMEM((rows, full), F32)],
         after,
     )
-    return list(outs[:-2]), outs[-2], outs[-1]
 
 
 def rope_tables(length):
@@ -891,150 +935,174 @@
     )
 
 
-def wire_kernel(n_shared, n_pairs, state, *refs):
-    pairs, (far, beside, own, split, shared) = refs[: 2 * n_pairs], refs[2 * n_pairs :]
-    shared_at = split_at = 0
-    for p in range(n_pairs):
-        total = (pairs[2 * p][...] + pairs[2 * p + 1][...]).astype(BF16)
-        total = total.reshape(-1, total.shape[-1])
-        rows = total.shape[0]
-        if p < n_shared:
-            shared[shared_at : shared_at + rows, :] = total
-            shared_at += rows
-            continue
-        width = split.shape[1]
-        for first in range(0, total.shape[1], width):
-            split[split_at : split_at + rows, :] = total[:, first : first + width]
-            split_at += rows
+def wire_kernel(n_shared, state, *refs):
+    shared_terms, refs = refs[:n_shared], refs[n_shared:]
+    split_terms, refs = refs[:6], refs[6:]
+    (far, beside, own, split, shared) = refs
+    at = 0
+    for terms in (shared_terms[0:1], shared_terms[1:3], shared_terms[3:5], shared_terms[5:7]):
+        total = terms[0][...]
+        for term in terms[1:]:
+            total += term[...]
+        total = total.astype(BF16).reshape(-1, total.shape[-1])
+        shared[at : at + total.shape[0], :] = total
+        at += total.shape[0]
     write_slabs(state, (far, beside, own), lambda columns: shared[:, columns])
-    picked = jnp.full((split.shape[0] - split_at, split.shape[1]), state[1].astype(F32))
-    split[split_at:, :] = picked.astype(BF16)
-
-
-def join_kernel(state, own, beside, near, far, split, joined):
-    rows = own.shape[0]
-    total = own[...].astype(F32) + beside[...].astype(F32)
-    joined[:rows, :] = (total + near[...].astype(F32) + far[...].astype(F32)).astype(BF16)
+    unit0, unit1, down0, down1, head, merges = *split_terms[:5], split_terms[5]
+    rank, width = head.shape[1:]
+    for j in range(2):
+        split[j * rank : (j + 1) * rank, :] = (unit0[j] + unit1[j]).astype(BF16)
+    split[2 * rank : 3 * rank, :] = (down0[...] + down1[...]).astype(BF16)
+    for j in range(3):
+        split[3 * rank : 4 * rank, j * width : (j + 1) * width] = head[j].astype(BF16)
+    split[3 * rank : 4 * rank, 3 * width :] = (merges[0] + merges[1]).astype(BF16)
+    picked = jnp.full((rank, split.shape[1]), state[1].astype(F32))
+    split[4 * rank :, :] = picked.astype(BF16)
+
+
+def own_kernel(state, own, beside, near, far, total):
+    held = own[...].astype(F32) + beside[...].astype(F32)
+    total[...] = (held + near[...].astype(F32) + far[...].astype(F32)).astype(BF16)
+
+
+def join_kernel(n_parts, state, *refs):
+    parts, (split, joined, shared, sems) = refs[:n_parts], refs[n_parts:]
+    copies = slab_copies(state, parts, shared, sems)
+    start_copies(copies)
+    wait_copies(copies)
+    rows = shared.shape[0]
+    joined[:rows, :] = shared[...]
     joined[rows:, :] = split[...]
 
 
-def combine_kernel(n_shared, adapters, state, everyone, shared, *split):
-    count, rows, width = everyone.shape
-    for a in range(adapters):
-        total = jnp.zeros((rows - 16, width), F32)
+def combine_kernel(
+    adapters, width, state, everyone, picks, lead, tail, unit, down, head, merge, slots, held
+):
+    step = pl.program_id(0)
+    count = everyone.shape[0]
+
+    @pl.when(step == 0)
+    def _():
         for d in range(count):
-            here = everyone[d, rows - 16 :, :].astype(F32)[:1] == float(a)
-            total += jnp.where(here, everyone[d, : rows - 16, :].astype(F32), 0.0)
-        shared[a] = total[:n_shared].astype(BF16)
-        at = n_shared
-        for target in split:
-            height, full = target.shape[1:]
-            for first in range(0, full, width):
-                target[a, :, first : first + width] = total[at : at + height]
-                at += height
-
-
-def whole_width_kernel(state, *refs):
-    early, late, (lead, tail) = refs[:6], refs[6:12], refs[12:14]
-    early_whole, late_whole, early_sems, late_sems = refs[14:]
-    rank, adapters = lead.shape[2], lead.shape[1]
-    early_copies = slab_copies(state, early, early_whole, early_sems)
-    late_copies = slab_copies(state, late, late_whole, late_sems)
-    start_copies(early_copies)
-    start_copies(late_copies)
-    wait_copies(early_copies)
-    wait_copies(late_copies)
-    for held, leads, tails in ((late_whole, (0, 1, 2), 0), (early_whole, (3, 4), 1)):
-        height = held.shape[0] // adapters
+            slots[d] = jnp.max(picks[d].astype(F32)).astype(jnp.int32)
+
+    def add_into(target):
         for a in range(adapters):
-            rows = held[a * height : (a + 1) * height, :].astype(F32)
-            for i, j in enumerate(leads):
-                lead[j, a] = rows[i * rank : (i + 1) * rank]
-            tail[tails, a] = rows[len(leads) * rank :]
-
-
-def whole_width(line, early, late, adapters, rank):
-    width = early[0].shape[1]
-    full = 4 * width
-    return line.call(
-        whole_width_kernel,
-        "whole_width",
-        (1,),
-        (*early, *late),
-        [ANY] * 12,
-        (
-            jax.ShapeDtypeStruct((5, adapters, rank, full), F32),
-            jax.ShapeDtypeStruct((2, adapters, rank, full), F32),
-        ),
-        (out_whole((5, adapters, rank, full)), out_whole((2, adapters, rank, full))),
-        [
-            pltpu.VMEM((early[0].shape[0], full), BF16),
-            pltpu.VMEM((late[0].shape[0], full), BF16),
-            pltpu.SemaphoreType.DMA((4,)),
-            pltpu.SemaphoreType.DMA((4,)),
-        ],
-    )
+            target[a] = jnp.zeros(target.shape[1:], F32)
+        for d in range(count):
+            target[slots[d]] += everyone[d].astype(F32)
+
+    def write(first, blocks, target):
+        @pl.when((step >= first) & (step < first + blocks))
+        def _():
+            add_into(target.at[0])
+
+    write(0, 5, lead)
+    write(5, 2, tail)
+    write(7, 2, unit)
+    write(9, 1, down)
+
+    @pl.when(step == 10)
+    def _():
+        add_into(held)
+        for a in range(adapters):
+            for j in range(3):
+                head[j, a] = held[a, :, j * width : (j + 1) * width]
+            merge[a] = held[a, :, 3 * width :]
 
 
 class AdapterSums:
-    def __init__(self, line, split, shared, adapters, slabs):
-        full = shared[0][0].shape[-1]
+    def __init__(self, line, shared, split, slabs):
+        rank, full = shared[0].shape[1:]
         width = full // slabs
-        self.line, self.split = line, split
-        self.adapters, self.width = adapters, width
-        self.n_shared = sum(x.size // full for x, _ in shared)
-        n_split = sum(x.size // width for x, _ in split) + 16
-        arrays = [x for pair in shared + split for x in pair]
-        slab = (self.n_shared, width)
-        far, beside, self.own, self.sent = line.call(
-            functools.partial(wire_kernel, len(shared), len(shared) + len(split)),
+        self.line, self.rank, self.full, self.width = line, rank, full, width
+        slab = (7 * rank, width)
+        shapes = ((2, *slab), slab, slab, (5 * rank, full))
+        arrays = (*shared, *split)
+        far, beside, self.own, self.split = line.call(
+            functools.partial(wire_kernel, len(shared)),
             "wire",
             (1,),
             arrays,
             [whole(x) for x in arrays],
-            tuple(
-                jax.ShapeDtypeStruct(shape, BF16)
-                for shape in ((2, *slab), slab, slab, (n_split, width))
-            ),
-            tuple(out_whole(shape) for shape in ((2, *slab), slab, slab, (n_split, width))),
-            [pltpu.VMEM((self.n_shared, full), BF16)],
+            tuple(jax.ShapeDtypeStruct(shape, BF16) for shape in shapes),
+            tuple(out_whole(shape) for shape in shapes),
+            [pltpu.VMEM((7 * rank, full), BF16)],
         )
         self.slab_sum = SlabSum(line, (far, beside, self.own))
 
     def cross(self):
         self.slab_sum.cross()
 
+    def spread(self):
+        terms = self.slab_sum.terms
+        own = self.line.call(
+            own_kernel,
+            "own",
+            (1,),
+            terms,
+            [whole(x) for x in terms],
+            jax.ShapeDtypeStruct(self.own.shape, BF16),
+            out_whole(self.own.shape),
+        )
+        self.parts = spread(own, "pair")
+
     def join(self):
-        rows = self.own.shape[0] + self.sent.shape[0]
-        ins = (*self.slab_sum.terms, self.sent)
+        shape = (12 * self.rank, self.full)
         sent = self.line.call(
-            join_kernel,
+            functools.partial(join_kernel, len(self.parts)),
             "join",
             (1,),
-            ins,
-            [whole(x) for x in ins],
-            jax.ShapeDtypeStruct((rows, self.width), BF16),
-            out_whole((rows, self.width)),
+            (*self.parts, self.split),
+            [ANY] * len(self.parts) + [whole(self.split)],
+            jax.ShapeDtypeStruct(shape, BF16),
+            out_whole(shape),
+            [pltpu.VMEM((7 * self.rank, self.full), BF16), pltpu.SemaphoreType.DMA((4,))],
         )
         self.everyone = lax.all_gather(sent, "dp", axis=0, tiled=False)
 
-    def combine(self):
-        shapes = [(self.adapters, x.size // x.shape[-1], x.shape[-1]) for x, _ in self.split]
-        shared = (self.adapters, self.n_shared, self.width)
-        shared, *split = self.line.call(
-            functools.partial(combine_kernel, self.n_shared, self.adapters),
+    def combine(self, adapters):
+        count = self.everyone.shape[0]
+        rank, full, width = self.rank, self.full, self.width
+
+        def sums(first, blocks):
+            return pl.BlockSpec(
+                (1, adapters, rank, full),
+                lambda i, s: (jnp.clip(i - first, 0, blocks - 1), 0, 0, 0),
+            )
+
+        def shape(*dims):
+            return jax.ShapeDtypeStruct(dims, F32)
+
+        return self.line.call(
+            functools.partial(combine_kernel, adapters, width),
             "combine",
-            (1,),
-            (self.everyone,),
-            [whole(self.everyone)],
+            (11,),
+            (self.everyone, self.everyone),
+            [
+                pl.BlockSpec((count, rank, full), lambda i, s: (0, i, 0)),
+                pl.BlockSpec((count, rank, 128), lambda i, s: (0, 11, 0)),
+            ],
             (
-                jax.ShapeDtypeStruct(shared, BF16),
-                *(jax.ShapeDtypeStruct(shape, F32) for shape in shapes),
+                shape(5, adapters, rank, full),
+                shape(2, adapters, rank, full),
+                shape(2, adapters, rank, full),
+                shape(1, adapters, rank, full),
+                shape(3, adapters, rank, width),
+                shape(adapters, rank, width),
             ),
-            (out_whole(shared), *(out_whole(shape) for shape in shapes)),
+            (
+                sums(0, 5),
+                pl.BlockSpec(
+                    (1, adapters, rank, full), lambda i, s: (jnp.where(i < 6, 1, 0), 0, 0, 0)
+                ),
+                sums(7, 2),
+                sums(9, 1),
+                out_whole((3, adapters, rank, width)),
+                out_whole((adapters, rank, width)),
+            ),
+            [pltpu.SMEM((count,), jnp.int32), pltpu.VMEM((adapters, rank, full), F32)],
         )
-        self.parts = spread(shared.reshape(-1, self.width), "pair")
-        return split
 
 
 def on_device(
@@ -1072,14 +1140,15 @@
         return array[c * rows : (c + 1) * rows]
 
     own_tokens = [cut(tokens[0], c) for c in range(CHUNKS)]
-    token_parts = [spread(own, MODES["tok"][c]) for c, own in enumerate(own_tokens)]
+    token_parts = spread(tokens[0], MODES["tok"])
     own_cots = [cut(cotangent[0], c) for c in range(CHUNKS)]
-    cot_parts = [spread(own, MODES["cot"][c]) for c, own in enumerate(own_cots)]
+    cot_parts = spread(cotangent[0], MODES["cot"])
 
     def project_chunk(c, after=()):
         return project(
             line,
-            token_parts[c],
+            token_parts,
+            c,
             gains,
             lead,
             query_key_value_matrix,
@@ -1109,7 +1178,8 @@
         return feed_forward(
             line,
             parts,
-            cot_parts[c],
+            cot_parts,
+            c,
             gains,
             lead,
             gate_up_matrix,
@@ -1137,22 +1207,18 @@
             after,
         )
 
-    def project_back_chunk(c, query_grad, later, after=()):
-        normed, mid, scale = saved[c]
+    def project_back_chunk(c, after=()):
+        normed, _, scale = saved[c]
         return project_back(
             line,
-            query_grad,
-            later,
+            gradients,
+            backs,
             c,
             query_key_value_matrix,
-            head_factors,
             lead,
             gains,
             normed,
-            mid,
             scale,
-            cut(cosine, c),
-            cut(sine, c),
             slabs,
             MODES["last"][c],
             after,
@@ -1164,77 +1230,80 @@
     branch0 = SlabSum(line, branch0)
     qkv1, *saved1 = project_chunk(1)
     qkvs, saved = [qkv0, qkv1], [saved0, saved1]
-    attended1, *branch1 = attend_chunk(1, qkvs, tuple(cot_parts[0][1:4]))
+    branch0.cross()
+    attended1, *branch1 = attend_chunk(1, qkvs)
     attended = [attended0, attended1]
     branch1 = SlabSum(line, branch1)
-    hidden0, rounded0 = branch0.finish(own_tokens[0], tuple(cot_parts[0][4:]))
+    hidden0, rounded0 = branch0.finish(own_tokens[0])
     hidden_parts0 = spread(rounded0, MODES["hidden"][0])
-    branch1.cross(tuple(cot_parts[1][1:4]))
-    hidden1, rounded1 = branch1.finish(own_tokens[1], tuple(cot_parts[1][4:]))
+    branch1.cross()
+    hidden1, rounded1 = branch1.finish(own_tokens[1])
     hidden_parts1 = spread(rounded1, MODES["hidden"][1])
     feed0, back0, unit_grads0 = feed_chunk(0, hidden_parts0)
     back0 = SlabSum(line, back0)
+    feed0 = SlabSum(line, feed0)
     feed1, back1, unit_grads1 = feed_chunk(1, hidden_parts1)
     back1 = SlabSum(line, back1)
-    grad0, rounded0 = back0.finish(own_cots[0])
+    grad0, rounded0 = back0.finish(own_cots[0], (feed0.received,))
     grad_parts0 = spread(rounded0, MODES["grad"][0])
     back1.cross()
     grad1, rounded1 = back1.finish(own_cots[1])
     grad_parts1 = spread(rounded1, MODES["grad"][1])
-    feed0_far, feed0_beside, feed1_far, feed1_beside = relay(line, (*feed0[:2], *feed1[:2]))
-    feed0 = SlabSum(line, [feed0_far, feed0_beside, feed0[2]])
     query_grad0, key_grad0, value_grad0, *merge_grads0 = attend_back_chunk(0, grad_parts0)
-    early = AdapterSums(
+    feed0.cross()
+    feed1 = SlabSum(line, relay(line, feed1, (grad_parts1[0],)))
+    query_grad1, key_grad1, value_grad1, *merge_grads1 = attend_back_chunk(1, grad_parts1)
+    gradients, backs, head_grad, lead_grad = head_back(
         line,
-        list(zip(unit_grads0, unit_grads1))[:2],
-        list(zip(unit_grads0, unit_grads1))[2:],
-        adapters,
+        (query_grad0, query_grad1),
+        (key_grad0, key_grad1),
+        (value_grad0, value_grad1),
+        saved,
+        head_factors,
+        cosine,
+        sine,
+    )
+    sums = AdapterSums(
+        line,
+        (
+            lead_grad,
+            unit_grads0[2],
+            unit_grads1[2],
+            unit_grads0[3],
+            unit_grads1[3],
+            merge_grads0[1],
+            merge_grads1[1],
+        ),
+        (
+            unit_grads0[0],
+            unit_grads1[0],
+            unit_grads0[1],
+            unit_grads1[1],
+            head_grad,
+            jnp.stack([merge_grads0[0], merge_grads1[0]]),
+        ),
         slabs,
     )
-    feed0.cross()
-    feed1 = SlabSum(line, [feed1_far, feed1_beside, feed1[2]])
-    query_grad1, key_grad1, value_grad1, *merge_grads1 = attend_back_chunk(1, grad_parts1)
-    early.cross()
-    feed1.cross()
-    last1, *head_grads1 = project_back_chunk(1, query_grad1, [key_grad1, value_grad1])
-    last1 = SlabSum(line, last1)
-    early.join()
+    sums.cross()
+    sums.spread()
+    last1 = SlabSum(line, project_back_chunk(1, tuple(feed1.terms)))
+    sums.join()
+    last0 = SlabSum(line, project_back_chunk(0))
+    last1.cross()
+    last0.cross()
+    lead_all, tail_all, unit_all, down_all, head_all, merge_all = sums.combine(adapters)
     _, out0 = feed0.finish(hidden0)
-    last0, *head_grads0 = project_back_chunk(
-        0, query_grad0, [key_grad0, value_grad0, key_grad1, value_grad1]
-    )
-    last0 = SlabSum(line, last0)
-    (head0, lead0), (head1, lead1) = head_grads0, head_grads1
-    (merge0, tail0), (merge1, tail1) = merge_grads0, merge_grads1
-    late = AdapterSums(
-        line,
-        [(head0, head1), (merge0, merge1)],
-        [(lead0, lead1), (tail0, tail1)],
-        adapters,
-        slabs,
-    )
-    layer_out = feed1.finish_after(hidden1, out0)
-    late.cross()
-    late.join()
-    last0.cross()
-    unit_all, down_all = early.combine()
+    layer_out = feed1.finish_beside(hidden1, out0, 1)
     _, tokens_grad1 = last1.finish(grad1)
-    head_all, merge_all = late.combine()
-    _, tokens_grad0 = last0.finish(grad0)
-    rank = lead_factors.shape[3]
-    lead_all, tail_all = whole_width(line, early.parts, late.parts, adapters, rank)
-
-    def ranked(array):
-        return jnp.swapaxes(array.reshape(adapters, -1, rank, array.shape[-1]), 0, 1)
-
+    tokens_grad = last0.finish_beside(grad0, tokens_grad1, 0)
     return (
         layer_out[None],
-        jnp.concatenate([tokens_grad0, tokens_grad1])[None],
+        tokens_grad[None],
         jnp.swapaxes(lead_all, 2, 3),
-        ranked(head_all),
-        ranked(unit_all),
+        head_all,
+        unit_all,
         jnp.swapaxes(merge_all, 1, 2),
-        jnp.swapaxes(down_all, 1, 2),
+        jnp.swapaxes(down_all[0], 1, 2),
         tail_all,
     )
 

time: 833 us -> 747 us (0.90)
  Pallas kernels: 308 us -> 228 us
  local copies, waits for them, and re-layouts: 20.6 us -> 92.1 us
  waiting for transfers between devices: 392 us -> 330 us
  starting transfers between devices: 80.6 us -> 67.9 us
    pallas_call x33 -> x31, Pallas kernels: 308 us -> 228 us  [call(): pl.pallas_call(body, name=name, grid_spec=pltpu.PrefetchScalarGridSpec(nu...]
    ppermute x4 -> x1, waiting for transfers between devices: 77.5 us -> 0.97 us  [spread(): far = lax.ppermute(own, 'tensor', OVER)]
    unnamed x100 -> x284, local copies, waits for them, and re-layouts: 13.3 us -> 87.1 us
    ppermute x7, waiting for transfers between devices: 76.1 us -> 142 us  [__init__(): self.received = lax.ppermute(parts[0], 'tensor', INWARD)]
    ppermute x4 -> x1, waiting for transfers between devices: 23.8 us -> 0.01 us  [spread(): lax.ppermute(far, 'tensor', OUTWARD)]
    ppermute x7, waiting for transfers between devices: 30.9 us -> 7.36 us  [cross(): beside = lax.ppermute(beside, 'tensor', BESIDE)]
    all_gather x6, waiting for transfers between devices: 67.7 us -> 90.8 us  [spread(): return [lax.all_gather(own, 'tensor', axis=0, tiled=False)]]
    ppermute x4 -> x1, waiting for transfers between devices: 17.9 us -> 0.01 us  [spread(): lax.ppermute(near, 'tensor', OUTWARD)]
  transfers between devices with their start and end apart: 59 -> 42, of which waited for: 23 -> 18; matrix products, arithmetic and copies ran while one was open for 1% -> 1% of each run, Pallas kernels for 36% -> 30%
where the time goes in v2:
time: 747 us; the launch traced here: 737 us
  waiting for transfers between devices  330 us (44%)
  Pallas kernels  228 us (31%)
  local copies, waits for them, and re-layouts  92.1 us (12%)
  starting transfers between devices  67.9 us (9%)
  between operations  16.3 us (2%)
    pallas_call x31, Pallas kernels, call(): pl.pallas_call(body, name=name, grid_spec=pltpu.PrefetchScalarGridSpec(nu...  228 us
    ppermute x7, waiting for transfers between devices, __init__(): self.received = lax.ppermute(parts[0], 'tensor', INWARD)  142 us
    all_gather x6, waiting for transfers between devices, spread(): return [lax.all_gather(own, 'tensor', axis=0, tiled=False)]  90.8 us
    unnamed x284, local copies, waits for them, and re-layouts  87.1 us
    ppermute x7, waiting for transfers between devices, cross(): far = lax.ppermute(far, 'tensor', ACROSS)  78.8 us
    ppermute x7, starting transfers between devices, cross(): beside = lax.ppermute(beside, 'tensor', BESIDE)  29.6 us
    ppermute x7, starting transfers between devices, __init__(): self.received = lax.ppermute(parts[0], 'tensor', INWARD)  17.6 us
  transfers between devices with their start and end apart: 42, of which 18 were waited for; matrix products, arithmetic and copies ran while one was open for 1% of the time, Pallas kernels for 30%

profile of v2, /device:TPU:0, one launch (start us, length us, event | category | flops | bytes accessed | tf_op | source)
XLA Modules:
  0.0 737.3 jit_solution(14346543282685220857)
XLA Ops:
  15.1 78.0 %all-gather.13.cloned.1.call-done.refs_1_ = bf16[4,1024,512]{2,1,0:T(8,128)(2,1)} async-done(((bf16[1,1024,512]{2,1,0:T(8,128)(2,1)}), bf16[4,1024,512]{2,1,0:T(8,128)(2,1)}) %all-gather.13.cloned.1.call-update) | async-done | bytes 4194320 | tf_op jit(solution)/shard_map/all_gather | solution.py:70
  101.0 8.3 %project.2 = (bf16[3,512,512]{2,1,0:T(8,128)(2,1)S(1)}, bf16[512,2048]{1,0:T(8,128)(2,1)S(1)}, bf16[3,512,16]{2,1,0:T(8,128)(2,1)S(1)}, f32[512,1]{1,0:T(8,128)S(1)}) custom-call(s32[2]{0:T(128)S(1)} %pad_add_fusion.refs_0_, bf16[4,1024,512]{2,1,0:T(8,128)(2,1)S(1)} %copy-done.16, f32[2,2048]{1,0:T(2,128)S(1)} %convert_element_type.3.refs_2_.refs_3_.refs_5_, ...), custom_call_target="tpu_custom_call" | custom-call | flops 1 | bytes 1 | tf_op jit(solution)/shard_map/project/pallas_call | solution.py:303
  110.7 11.1 %attend.2 = (bf16[512,512]{1,0:T(8,128)(2,1)S(1)}, bf16[2,512,512]{2,1,0:T(8,128)(2,1)S(1)}, bf16[512,512]{1,0:T(8,128)(2,1)S(1)}, bf16[512,512]{1,0:T(8,128)(2,1)S(1)}) custom-call(s32[2]{0:T(128)S(1)} %pad_add_fusion.refs_0_, bf16[3,512,512]{2,1,0:T(8,128)(2,1)S(1)} %get-tuple-element.101.refs_1_.refs_2_.refs_3_.refs_4_, ...), custom_call_target="tpu_custom_call" | custom-call | flops 1 | bytes 1 | tf_op jit(solution)/shard_map/attend/pallas_call | solution.py:303
  127.0 8.3 %project.3 = (bf16[3,512,512]{2,1,0:T(8,128)(2,1)S(1)}, bf16[512,2048]{1,0:T(8,128)(2,1)S(1)}, bf16[3,512,16]{2,1,0:T(8,128)(2,1)S(1)}, f32[512,1]{1,0:T(8,128)S(1)}) custom-call(s32[2]{0:T(128)S(1)} %pad_add_fusion.refs_0_, bf16[4,1024,512]{2,1,0:T(8,128)(2,1)S(1)} %copy-done.17, f32[2,2048]{1,0:T(2,128)S(1)} %convert_element_type.3.refs_2_.refs_3_.refs_5_, ...), custom_call_target="tpu_custom_call" | custom-call | flops 1 | bytes 1 | tf_op jit(solution)/shard_map/project/pallas_call | solution.py:303
  135.4 34.2 %collective-permute-done.refs_2_ = bf16[2,512,512]{2,1,0:T(8,128)(2,1)S(1)} collective-permute-done((bf16[2,512,512]{2,1,0:T(8,128)(2,1)S(1)}, bf16[2,512,512]{2,1,0:T(8,128)(2,1)S(1)}, u32[]{:S(2)}, u32[]{:S(2)}) %collective-permute-start) | collective-permute-done | bytes 1048608 | tf_op jit(solution)/shard_map/ppermute | solution.py:225
  179.2 13.8 %attend.3 = (bf16[512,512]{1,0:T(8,128)(2,1)S(1)}, bf16[2,512,512]{2,1,0:T(8,128)(2,1)S(1)}, bf16[512,512]{1,0:T(8,128)(2,1)S(1)}, bf16[512,512]{1,0:T(8,128)(2,1)S(1)}) custom-call(s32[2]{0:T(128)S(1)} %pad_add_fusion.refs_0_, bf16[3,512,512]{2,1,0:T(8,128)(2,1)S(1)} %get-tuple-element.101.refs_1_.refs_2_.refs_3_.refs_4_, ...), custom_call_target="tpu_custom_call" | custom-call | flops 1 | bytes 1 | tf_op jit(solution)/shard_map/attend/pallas_call | solution.py:303
  194.8 15.3 %collective-permute-done.3.refs_5_ = bf16[512,512]{1,0:T(8,128)(2,1)S(1)} collective-permute-done((bf16[512,512]{1,0:T(8,128)(2,1)S(1)}, bf16[512,512]{1,0:T(8,128)(2,1)S(1)}, u32[]{:S(2)}, u32[]{:S(2)}) %collective-permute-start.3) | collective-permute-done | bytes 524320 | tf_op jit(solution)/shard_map/ppermute | solution.py:244
  214.3 41.1 %collective-permute-done.4.refs_2_ = bf16[2,512,512]{2,1,0:T(8,128)(2,1)S(1)} collective-permute-done((bf16[2,512,512]{2,1,0:T(8,128)(2,1)}, bf16[2,512,512]{2,1,0:T(8,128)(2,1)S(1)}, u32[]{:S(2)}, u32[]{:S(2)}) %collective-permute-start.4) | collective-permute-done | bytes 1048608 | tf_op jit(solution)/shard_map/ppermute | solution.py:225
  265.5 25.7 %collective-permute-done.7.refs_5_ = bf16[512,512]{1,0:T(8,128)(2,1)S(1)} collective-permute-done((bf16[512,512]{1,0:T(8,128)(2,1)S(1)}, bf16[512,512]{1,0:T(8,128)(2,1)S(1)}, u32[]{:S(2)}, u32[]{:S(2)}) %collective-permute-start.7) | collective-permute-done | bytes 524320 | tf_op jit(solution)/shard_map/ppermute | solution.py:244
  294.1 46.7 %feed_forward.2 = (bf16[2,512,512]{2,1,0:T(8,128)(2,1)}, bf16[512,512]{1,0:T(8,128)(2,1)}, bf16[512,512]{1,0:T(8,128)(2,1)}, bf16[4,512,512]{2,1,0:T(8,128)(2,1)...) custom-call(s32[2]{0:T(128)} %copy-done.121, ...), custom_call_target="tpu_custom_call" | custom-call | flops 1 | bytes 1 | tf_op jit(solution)/shard_map/feed_forward/pallas_call | solution.py:303
  345.6 47.6 %feed_forward.3 = (bf16[4,512,512]{2,1,0:T(8,128)(2,1)}, bf16[2,512,512]{2,1,0:T(8,128)(2,1)}, bf16[512,512]{1,0:T(8,128)(2,1)}, bf16[512,512]{1,0:T(8,128)(2,1)...) custom-call(s32[2]{0:T(128)} %copy-done.121, ...), custom_call_target="tpu_custom_call" | custom-call | flops 1 | bytes 1 | tf_op jit(solution)/shard_map/feed_forward/pallas_call | solution.py:303
  393.2 7.8 %reduce-scatter.3.cloned.1.call-done = bf16[1,512,512]{2,1,0:T(8,128)(2,1)} async-done(((bf16[4,512,512]{2,1,0:T(8,128)(2,1)}), bf16[1,512,512]{2,1,0:T(8,128)(2,1)}) %reduce-scatter.3.cloned.1.call-update) | async-done | bytes 524304 | tf_op jit(solution)/shard_map/reduce_scatter | solution.py:222
  408.1 39.5 %collective-permute-done.9.refs_2_ = bf16[2,512,512]{2,1,0:T(8,128)(2,1)S(1)} collective-permute-done((bf16[2,512,512]{2,1,0:T(8,128)(2,1)}, bf16[2,512,512]{2,1,0:T(8,128)(2,1)S(1)}, u32[]{:S(2)}, u32[]{:S(2)}) %collective-permute-start.9) | collective-permute-done | bytes 1048608 | tf_op jit(solution)/shard_map/ppermute | solution.py:225
  454.0 7.0 collective-permute-start.10
  460.9 26.9 %collective-permute-done.12.refs_5_ = bf16[512,512]{1,0:T(8,128)(2,1)S(1)} collective-permute-done((bf16[512,512]{1,0:T(8,128)(2,1)S(1)}, bf16[512,512]{1,0:T(8,128)(2,1)S(1)}, u32[]{:S(2)}, u32[]{:S(2)}) %collective-permute-start.12) | collective-permute-done | bytes 524320 | tf_op jit(solution)/shard_map/ppermute | solution.py:244
  498.2 16.2 %attend_back.2 = (f32[512,512]{1,0:T(8,128)S(1)}, f32[512,512]{1,0:T(8,128)S(1)}, f32[512,512]{1,0:T(8,128)S(1)}, f32[16,512]{1,0:T(8,128)S(1)}, f32[16,2048]{1,0:T(8,128)S(1)}) custom-call(s32[2]{0:T(128)S(1)} %copy-done.122, bf16[4,512,512]{2,1,0:T(8,128)(2,1)S(1)} %bitcast.42, bf16[3,512,512]{2,1,0:T(8,128)(2,1)S(1)} %get-tuple-element.101.refs_1_.refs_2_.refs_3_.refs_4_, ...), custom_call_target="tpu_custom_call" | custom-call | flops 1 | bytes 1 | tf_op jit(solution)/shard_map/attend_back/pallas_call | solution.py:303
  522.3 12.8 %all-gather.23.cloned.1.call-done = bf16[2048,512]{1,0:T(8,128)(2,1)} async-done(((bf16[512,512]{1,0:T(8,128)(2,1)}), bf16[2048,512]{1,0:T(8,128)(2,1)}) %all-gather.23.cloned.1.call-update) | async-done | bytes 2097168 | tf_op jit(solution)/shard_map/all_gather | solution.py:70
  549.5 21.2 %attend_back.3 = (f32[512,512]{1,0:T(8,128)S(1)}, f32[1024,512]{1,0:T(8,128)S(1)}, f32[1024,512]{1,0:T(8,128)S(1)}, f32[16,512]{1,0:T(8,128)S(1)}, f32[16,2048]{1,0:T(8,128)S(1)}) custom-call(s32[2]{0:T(128)S(1)} %copy-done.122, bf16[4,512,512]{2,1,0:T(8,128)(2,1)S(1)} %bitcast.40, ...), custom_call_target="tpu_custom_call" | custom-call | flops 1 | bytes 1 | tf_op jit(solution)/shard_map/attend_back/pallas_call | solution.py:303
  615.2 9.3 %project_back.2 = (bf16[2,512,512]{2,1,0:T(8,128)(2,1)S(1)}, bf16[512,512]{1,0:T(8,128)(2,1)S(1)}, bf16[512,512]{1,0:T(8,128)(2,1)S(1)}) custom-call(s32[2]{0:T(128)S(1)} %copy-done.122, bf16[3,1024,512]{2,1,0:T(8,128)(2,1)S(1)} %copy-done.23, bf16[3,1024,16]{2,1,0:T(8,128)(2,1)S(1)} %copy-done.41, bf16[3,2048,512]{2,1,0:T(8,128)(2,1)S(1)} %copy-done.2, ...), custom_call_target="tpu_custom_call" | custom-call | flops 1 | bytes 1 | tf_op jit(solution)/shard_map/project_back/pallas_call | solution.py:303
  629.7 7.6 %collective-permute-start.26 = (bf16[2,512,512]{2,1,0:T(8,128)(2,1)}, bf16[2,512,512]{2,1,0:T(8,128)(2,1)S(1)}, u32[]{:S(2)}, u32[]{:S(2)}) collective-permute-start(bf16[2,512,512]{2,1,0:T(8,128)(2,1)} %copy-done.83), channel_id=1, source_target_pairs={{0,1},{3,2},{4,5},{7,6},{8,9},{11,10},{12,13},{15,14},{16,17},{19,... | collective-permute-start | bytes 3145736 | tf_op jit(solution)/shard_map/ppermute | solution.py:225
  645.6 9.1 %project_back.3 = (bf16[2,512,512]{2,1,0:T(8,128)(2,1)S(1)}, bf16[512,512]{1,0:T(8,128)(2,1)S(1)}, bf16[512,512]{1,0:T(8,128)(2,1)S(1)}) custom-call(s32[2]{0:T(128)S(1)} %copy-done.122, bf16[3,1024,512]{2,1,0:T(8,128)(2,1)S(1)} %copy-done.24, bf16[3,1024,16]{2,1,0:T(8,128)(2,1)S(1)} %copy-done.42, bf16[3,2048,512]{2,1,0:T(8,128)(2,1)S(1)} %copy-done.3, ...), custom_call_target="tpu_custom_call" | custom-call | flops 1 | bytes 1 | tf_op jit(solution)/shard_map/project_back/pallas_call | solution.py:303
  663.6 19.9 %collective-permute-done.25.refs_2_ = bf16[2,512,512]{2,1,0:T(8,128)(2,1)S(1)} collective-permute-done((bf16[2,512,512]{2,1,0:T(8,128)(2,1)S(1)}, bf16[2,512,512]{2,1,0:T(8,128)(2,1)S(1)}, u32[]{:S(2)}, u32[]{:S(2)}) %collective-permute-start.25) | collective-permute-done | bytes 1048608 | tf_op jit(solution)/shard_map/ppermute | solution.py:225
  702.3 7.0 combine.1
  717.1 7.3 collective-permute-done.32.refs_6_
  (395 shorter events, 199.3 us)
Async XLA Ops:
  7.2 85.9 %all-gather.13.cloned.1.call-start = ((), (), s32[]{:S(2)}) async-start(), calls=%async_computation.2 | async-start | bytes 5242880 | tf_op jit(solution)/shard_map/all_gather | solution.py:70
  7.9 286.1 %all-gather.15.cloned.1.call-start = ((), (), s32[]{:S(2)}) async-start(), calls=%async_computation.3 | async-start | bytes 5242880 | tf_op jit(solution)/shard_map/all_gather | solution.py:70
  8.7 285.4 %all-gather.17.cloned.1.call-start = ((), (), s32[]{:S(2)}) async-start(), calls=%async_computation.6 | async-start | bytes 2621440 | tf_op jit(solution)/shard_map/all_gather | solution.py:70
  122.6 47.0 %collective-permute-start = (bf16[2,512,512]{2,1,0:T(8,128)(2,1)S(1)}, bf16[2,512,512]{2,1,0:T(8,128)(2,1)S(1)}, u32[]{:S(2)}, u32[]{:S(2)}) collective-permute-start(bf16[2,512,512]{2,1,0:T(8,128)(2,1)S(1)} %get-tuple-element.104.refs_1_), channel_id=1, source_target_pairs={{0,1},{3,2},{4,5},{7,6},{8,9},{11,10},{12,13},{15,14},{16,17},{19,... | collective-permute-start | bytes 3145736 | tf_op jit(solution)/shard_map/ppermute | solution.py:225
  171.3 38.9 %collective-permute-start.3 = (bf16[512,512]{1,0:T(8,128)(2,1)S(1)}, bf16[512,512]{1,0:T(8,128)(2,1)S(1)}, u32[]{:S(2)}, u32[]{:S(2)}) collective-permute-start(bf16[512,512]{1,0:T(8,128)(2,1)S(1)} %get-tuple-element.109), channel_id=1, source_target_pairs={{1,3},{2,0},{5,7},{6,4},{9,11},{10,8},{13,15},{14,12},{17,19},{18,... | collective-permute-start | bytes 1572872 | tf_op jit(solution)/shard_map/ppermute | solution.py:244
  172.6 37.6 %collective-permute-start.1 = (bf16[512,512]{1,0:T(8,128)(2,1)S(1)}, bf16[512,512]{1,0:T(8,128)(2,1)S(1)}, u32[]{:S(2)}, u32[]{:S(2)}) collective-permute-start(bf16[512,512]{1,0:T(8,128)(2,1)S(1)} %get-tuple-element.107.refs_12_), channel_id=1, source_target_pairs={{0,1},{1,0},{2,3},{3,2},{4,5},{5,4},{6,7},{7,6},{8,9},{9,8},{10,11... | collective-permute-start | bytes 1572872 | tf_op jit(solution)/shard_map/ppermute | solution.py:245
  212.9 132.7 %all-gather.19.cloned.1.call-start = ((), (), s32[]{:S(2)}) async-start(), calls=%async_computation.7 | async-start | bytes 2621440 | tf_op jit(solution)/shard_map/all_gather | solution.py:70
  213.0 42.5 %collective-permute-start.4 = (bf16[2,512,512]{2,1,0:T(8,128)(2,1)}, bf16[2,512,512]{2,1,0:T(8,128)(2,1)S(1)}, u32[]{:S(2)}, u32[]{:S(2)}) collective-permute-start(bf16[2,512,512]{2,1,0:T(8,128)(2,1)} %copy-done.85), channel_id=1, source_target_pairs={{0,1},{3,2},{4,5},{7,6},{8,9},{11,10},{12,13},{15,14},{16,17},{19,... | collective-permute-start | bytes 3145736 | tf_op jit(solution)/shard_map/ppermute | solution.py:225
  260.5 30.7 %collective-permute-start.7 = (bf16[512,512]{1,0:T(8,128)(2,1)S(1)}, bf16[512,512]{1,0:T(8,128)(2,1)S(1)}, u32[]{:S(2)}, u32[]{:S(2)}) collective-permute-start(bf16[512,512]{1,0:T(8,128)(2,1)S(1)} %get-tuple-element.118), channel_id=1, source_target_pairs={{1,3},{2,0},{5,7},{6,4},{9,11},{10,8},{13,15},{14,12},{17,19},{18,... | collective-permute-start | bytes 1572872 | tf_op jit(solution)/shard_map/ppermute | solution.py:244
  294.0 107.1 %reduce-scatter.3.cloned.1.call-start = ((), (), s32[]{:S(2)}) async-start(), calls=%async_computation.4 | async-start | bytes 2621440 | tf_op jit(solution)/shard_map/reduce_scatter | solution.py:222
  340.9 149.8 %all-gather.21.cloned.1.call-start = ((), (), s32[]{:S(2)}) async-start(), calls=%async_computation.8 | async-start | bytes 2621440 | tf_op jit(solution)/shard_map/all_gather | solution.py:70
  340.9 52.3 %collective-permute-start.8 = (bf16[2,512,512]{2,1,0:T(8,128)(2,1)}, bf16[2,512,512]{2,1,0:T(8,128)(2,1)}, u32[]{:S(2)}, u32[]{:S(2)}) collective-permute-start(bf16[2,512,512]{2,1,0:T(8,128)(2,1)} %get-tuple-element.121.refs_1_), channel_id=1, source_target_pairs={{0,1},{3,2},{4,5},{7,6},{8,9},{11,10},{12,13},{15,14},{16,17},{19,... | collective-permute-start | bytes 3145736 | tf_op jit(solution)/shard_map/ppermute | solution.py:225
  406.6 128.5 %all-gather.23.cloned.1.call-start = ((), (), s32[]{:S(2)}) async-start(), calls=%async_computation.9 | async-start | bytes 2621440 | tf_op jit(solution)/shard_map/all_gather | solution.py:70
  406.7 41.0 %collective-permute-start.9 = (bf16[2,512,512]{2,1,0:T(8,128)(2,1)}, bf16[2,512,512]{2,1,0:T(8,128)(2,1)S(1)}, u32[]{:S(2)}, u32[]{:S(2)}) collective-permute-start(bf16[2,512,512]{2,1,0:T(8,128)(2,1)} %get-tuple-element.129.refs_1_), channel_id=1, source_target_pairs={{0,1},{3,2},{4,5},{7,6},{8,9},{11,10},{12,13},{15,14},{16,17},{19,... | collective-permute-start | bytes 3145736 | tf_op jit(solution)/shard_map/ppermute | solution.py:225
  452.7 35.1 %collective-permute-start.12 = (bf16[512,512]{1,0:T(8,128)(2,1)S(1)}, bf16[512,512]{1,0:T(8,128)(2,1)S(1)}, u32[]{:S(2)}, u32[]{:S(2)}) collective-permute-start(bf16[512,512]{1,0:T(8,128)(2,1)S(1)} %get-tuple-element.133), channel_id=1, source_target_pairs={{1,3},{2,0},{5,7},{6,4},{9,11},{10,8},{13,15},{14,12},{17,19},{18,... | collective-permute-start | bytes 1572872 | tf_op jit(solution)/shard_map/ppermute | solution.py:244
  454.0 33.8 %collective-permute-start.10 = (bf16[512,512]{1,0:T(8,128)(2,1)S(1)}, bf16[512,512]{1,0:T(8,128)(2,1)S(1)}, u32[]{:S(2)}, u32[]{:S(2)}) collective-permute-start(bf16[512,512]{1,0:T(8,128)(2,1)S(1)} %get-tuple-element.131.refs_6_), channel_id=1, source_target_pairs={{0,1},{1,0},{2,3},{3,2},{4,5},{5,4},{6,7},{7,6},{8,9},{9,8},{10,11... | collective-permute-start | bytes 1572872 | tf_op jit(solution)/shard_map/ppermute | solution.py:245
  490.6 116.8 %reduce-scatter.5.cloned.1.call-start = ((), (), s32[]{:S(2)}) async-start(), calls=%async_computation.5 | async-start | bytes 2621440 | tf_op jit(solution)/shard_map/reduce_scatter | solution.py:222
  541.4 158.1 %all-gather.25.cloned.1.call-start = ((), (), s32[]{:S(2)}) async-start(), calls=%async_computation.10 | async-start | bytes 7077888 | tf_op jit(solution)/shard_map/all_gather | solution.py:1062
  629.7 31.4 %collective-permute-start.26 = (bf16[2,512,512]{2,1,0:T(8,128)(2,1)}, bf16[2,512,512]{2,1,0:T(8,128)(2,1)S(1)}, u32[]{:S(2)}, u32[]{:S(2)}) collective-permute-start(bf16[2,512,512]{2,1,0:T(8,128)(2,1)} %copy-done.83), channel_id=1, source_target_pairs={{0,1},{3,2},{4,5},{7,6},{8,9},{11,10},{12,13},{15,14},{16,17},{19,... | collective-permute-start | bytes 3145736 | tf_op jit(solution)/shard_map/ppermute | solution.py:225
  656.1 31.7 %collective-permute-start.14 = (bf16[512,512]{1,0:T(8,128)(2,1)S(1)}, bf16[512,512]{1,0:T(8,128)(2,1)S(1)}, u32[]{:S(2)}, u32[]{:S(2)}) collective-permute-start(bf16[512,512]{1,0:T(8,128)(2,1)S(1)} %copy-done.139), channel_id=1, source_target_pairs={{1,2},{2,1},{5,6},{6,5},{9,10},{10,9},{13,14},{14,13},{17,18},{18,... | collective-permute-start | bytes 1572872 | tf_op jit(solution)/shard_map/ppermute | solution.py:243
  656.8 37.9 %collective-permute-start.13 = (bf16[512,512]{1,0:T(8,128)(2,1)S(1)}, bf16[512,512]{1,0:T(8,128)(2,1)S(1)}, u32[]{:S(2)}, u32[]{:S(2)}) collective-permute-start(bf16[512,512]{1,0:T(8,128)(2,1)S(1)} %copy-done.120), channel_id=1, source_target_pairs={{0,1},{1,0},{2,3},{3,2},{4,5},{5,4},{6,7},{7,6},{8,9},{9,8},{10,11... | collective-permute-start | bytes 1572872 | tf_op jit(solution)/shard_map/ppermute | solution.py:245
  657.7 31.4 %collective-permute-start.15 = (bf16[512,512]{1,0:T(8,128)(2,1)S(1)}, bf16[512,512]{1,0:T(8,128)(2,1)S(1)}, u32[]{:S(2)}, u32[]{:S(2)}) collective-permute-start(bf16[512,512]{1,0:T(8,128)(2,1)S(1)} %copy-done.137), channel_id=1, source_target_pairs={{1,3},{2,0},{5,7},{6,4},{9,11},{10,8},{13,15},{14,12},{17,19},{18,... | collective-permute-start | bytes 1572872 | tf_op jit(solution)/shard_map/ppermute | solution.py:244
  662.9 33.1 %collective-permute-start.28 = (bf16[512,512]{1,0:T(8,128)(2,1)S(1)}, bf16[512,512]{1,0:T(8,128)(2,1)S(1)}, u32[]{:S(2)}, u32[]{:S(2)}) collective-permute-start(bf16[512,512]{1,0:T(8,128)(2,1)S(1)} %get-tuple-element.183), channel_id=1, source_target_pairs={{1,2},{2,1},{5,6},{6,5},{9,10},{10,9},{13,14},{14,13},{17,18},{18,... | collective-permute-start | bytes 1572872 | tf_op jit(solution)/shard_map/ppermute | solution.py:243
  696.1 30.8 %collective-permute-start.30 = (bf16[512,512]{1,0:T(8,128)(2,1)S(1)}, bf16[512,512]{1,0:T(8,128)(2,1)}, u32[]{:S(2)}, u32[]{:S(2)}) collective-permute-start(bf16[512,512]{1,0:T(8,128)(2,1)S(1)} %get-tuple-element.178.refs_3_), channel_id=1, source_target_pairs={{0,1},{1,0},{2,3},{3,2},{4,5},{5,4},{6,7},{7,6},{8,9},{9,8},{10,11... | collective-permute-start | bytes 1572872 | tf_op jit(solution)/shard_map/ppermute | solution.py:245
  (160 other events, 2098.6 us)
Sparse Core Ops, SparseCore 0:
  9.6 83.4 all-gather.12
  94.7 108.7 all-gather.14
  213.0 64.5 all-gather.16
  294.1 45.9 all-gather.18
  342.8 58.2 reduce-scatter.2
  406.7 63.7 all-gather.20
  490.7 44.3 all-gather.22
  541.5 42.6 reduce-scatter.4
  629.9 48.7 all-gather.24

commit v3 on v2

--- a/solution.py
+++ b/solution.py
@@ -28,6 +28,7 @@
 SUB_ROWS = 256
 LARGE_VMEM = 60 * 1024 * 1024
 SMALL_VMEM = 30 * 1024 * 1024
+LARGE = ("feed_forward", "attend_back", "project_back")
 
 BESIDE = [(0, 1), (1, 0), (2, 3), (3, 2)]
 MIDDLE = [(1, 2), (2, 1)]
@@ -285,7 +286,7 @@
 def params(name):
     return pltpu.CompilerParams(
         dimension_semantics=("arbitrary",),
-        vmem_limit_bytes=LARGE_VMEM if name == "feed_forward" else SMALL_VMEM,
+        vmem_limit_bytes=LARGE_VMEM if name in LARGE else SMALL_VMEM,
     )
 
 

time: 747 us -> 736 us (0.985)
  local copies, waits for them, and re-layouts: 92.1 us -> 56.5 us
  Pallas kernels: 228 us -> 248 us
  waiting for transfers between devices: 330 us -> 339 us
    unnamed x284 -> x226, local copies, waits for them, and re-layouts: 87.1 us -> 52.5 us
    pallas_call x31, Pallas kernels: 228 us -> 248 us  [call(): pl.pallas_call(body, name=name, grid_spec=pltpu.PrefetchScalarGridSpec(nu...]
  transfers between devices with their start and end apart: 42 -> 42, of which waited for: 18 -> 18; matrix products, arithmetic and copies ran while one was open for 1% -> 1% of each run, Pallas kernels for 30% -> 33%
where the time goes in v3:
time: 736 us; the launch traced here: 727 us
  waiting for transfers between devices  339 us (46%)
  Pallas kernels  248 us (34%)
  starting transfers between devices  64.8 us (9%)
  local copies, waits for them, and re-layouts  56.5 us (8%)
  between operations  16 us (2%)
    pallas_call x31, Pallas kernels, call(): pl.pallas_call(body, name=name, grid_spec=pltpu.PrefetchScalarGridSpec(nu...  248 us
    ppermute x7, waiting for transfers between devices, __init__(): self.received = lax.ppermute(parts[0], 'tensor', INWARD)  143 us
    all_gather x6, waiting for transfers between devices, spread(): return [lax.all_gather(own, 'tensor', axis=0, tiled=False)]  96.7 us
    ppermute x7, waiting for transfers between devices, cross(): far = lax.ppermute(far, 'tensor', ACROSS)  78.1 us
    unnamed x226, local copies, waits for them, and re-layouts  52.5 us
    ppermute x7, starting transfers between devices, cross(): beside = lax.ppermute(beside, 'tensor', BESIDE)  27.6 us
    ppermute x7, starting transfers between devices, __init__(): self.received = lax.ppermute(parts[0], 'tensor', INWARD)  15.6 us
  transfers between devices with their start and end apart: 42, of which 18 were waited for; matrix products, arithmetic and copies ran while one was open for 1% of the time, Pallas kernels for 33%

profile of v3, /device:TPU:0, one launch (start us, length us, event | category | flops | bytes accessed | tf_op | source)
XLA Modules:
  0.0 727.2 jit_solution(6560084350576613210)
XLA Ops:
  15.1 78.0 %all-gather.13.cloned.1.call-done.refs_1_ = bf16[4,1024,512]{2,1,0:T(8,128)(2,1)} async-done(((bf16[1,1024,512]{2,1,0:T(8,128)(2,1)}), bf16[4,1024,512]{2,1,0:T(8,128)(2,1)}) %all-gather.13.cloned.1.call-update) | async-done | bytes 4194320 | tf_op jit(solution)/shard_map/all_gather | solution.py:71
  101.0 8.4 %project.2 = (bf16[3,512,512]{2,1,0:T(8,128)(2,1)S(1)}, bf16[512,2048]{1,0:T(8,128)(2,1)S(1)}, bf16[3,512,16]{2,1,0:T(8,128)(2,1)S(1)}, f32[512,1]{1,0:T(8,128)S(1)}) custom-call(s32[2]{0:T(128)S(1)} %pad_add_fusion.refs_0_, bf16[4,1024,512]{2,1,0:T(8,128)(2,1)S(1)} %copy-done.9, f32[2,2048]{1,0:T(2,128)S(1)} %convert_element_type.3.refs_2_.refs_3_.refs_5_, ...), custom_call_target="tpu_custom_call" | custom-call | flops 1 | bytes 1 | tf_op jit(solution)/shard_map/project/pallas_call | solution.py:304
  111.5 11.1 %attend.2 = (bf16[512,512]{1,0:T(8,128)(2,1)S(1)}, bf16[2,512,512]{2,1,0:T(8,128)(2,1)S(1)}, bf16[512,512]{1,0:T(8,128)(2,1)S(1)}, bf16[512,512]{1,0:T(8,128)(2,1)S(1)}) custom-call(s32[2]{0:T(128)S(1)} %pad_add_fusion.refs_0_, bf16[3,512,512]{2,1,0:T(8,128)(2,1)S(1)} %get-tuple-element.101.refs_1_.refs_2_.refs_3_.refs_4_, ...), custom_call_target="tpu_custom_call" | custom-call | flops 1 | bytes 1 | tf_op jit(solution)/shard_map/attend/pallas_call | solution.py:304
  127.9 8.4 %project.3 = (bf16[3,512,512]{2,1,0:T(8,128)(2,1)S(1)}, bf16[512,2048]{1,0:T(8,128)(2,1)S(1)}, bf16[3,512,16]{2,1,0:T(8,128)(2,1)S(1)}, f32[512,1]{1,0:T(8,128)S(1)}) custom-call(s32[2]{0:T(128)S(1)} %pad_add_fusion.refs_0_, bf16[4,1024,512]{2,1,0:T(8,128)(2,1)S(1)} %copy-done.10, f32[2,2048]{1,0:T(2,128)S(1)} %convert_element_type.3.refs_2_.refs_3_.refs_5_, ...), custom_call_target="tpu_custom_call" | custom-call | flops 1 | bytes 1 | tf_op jit(solution)/shard_map/project/pallas_call | solution.py:304
  137.0 33.3 %collective-permute-done.refs_2_ = bf16[2,512,512]{2,1,0:T(8,128)(2,1)S(1)} collective-permute-done((bf16[2,512,512]{2,1,0:T(8,128)(2,1)S(1)}, bf16[2,512,512]{2,1,0:T(8,128)(2,1)S(1)}, u32[]{:S(2)}, u32[]{:S(2)}) %collective-permute-start) | collective-permute-done | bytes 1048608 | tf_op jit(solution)/shard_map/ppermute | solution.py:226
  173.4 5.8 collective-permute-start.1
  180.0 13.8 %attend.3 = (bf16[512,512]{1,0:T(8,128)(2,1)S(1)}, bf16[2,512,512]{2,1,0:T(8,128)(2,1)S(1)}, bf16[512,512]{1,0:T(8,128)(2,1)S(1)}, bf16[512,512]{1,0:T(8,128)(2,1)S(1)}) custom-call(s32[2]{0:T(128)S(1)} %pad_add_fusion.refs_0_, bf16[3,512,512]{2,1,0:T(8,128)(2,1)S(1)} %get-tuple-element.101.refs_1_.refs_2_.refs_3_.refs_4_, ...), custom_call_target="tpu_custom_call" | custom-call | flops 1 | bytes 1 | tf_op jit(solution)/shard_map/attend/pallas_call | solution.py:304
  194.7 15.5 %collective-permute-done.3.refs_5_ = bf16[512,512]{1,0:T(8,128)(2,1)S(1)} collective-permute-done((bf16[512,512]{1,0:T(8,128)(2,1)S(1)}, bf16[512,512]{1,0:T(8,128)(2,1)S(1)}, u32[]{:S(2)}, u32[]{:S(2)}) %collective-permute-start.3) | collective-permute-done | bytes 524320 | tf_op jit(solution)/shard_map/ppermute | solution.py:245
  214.3 41.2 %collective-permute-done.4.refs_2_ = bf16[2,512,512]{2,1,0:T(8,128)(2,1)S(1)} collective-permute-done((bf16[2,512,512]{2,1,0:T(8,128)(2,1)}, bf16[2,512,512]{2,1,0:T(8,128)(2,1)S(1)}, u32[]{:S(2)}, u32[]{:S(2)}) %collective-permute-start.4) | collective-permute-done | bytes 1048608 | tf_op jit(solution)/shard_map/ppermute | solution.py:226
  263.4 27.6 %collective-permute-done.7.refs_5_ = bf16[512,512]{1,0:T(8,128)(2,1)S(1)} collective-permute-done((bf16[512,512]{1,0:T(8,128)(2,1)S(1)}, bf16[512,512]{1,0:T(8,128)(2,1)S(1)}, u32[]{:S(2)}, u32[]{:S(2)}) %collective-permute-start.7) | collective-permute-done | bytes 524320 | tf_op jit(solution)/shard_map/ppermute | solution.py:245
  293.8 47.1 %feed_forward.2 = (bf16[2,512,512]{2,1,0:T(8,128)(2,1)}, bf16[512,512]{1,0:T(8,128)(2,1)}, bf16[512,512]{1,0:T(8,128)(2,1)}, bf16[4,512,512]{2,1,0:T(8,128)(2,1)...) custom-call(s32[2]{0:T(128)} %copy-done.89, ...), custom_call_target="tpu_custom_call" | custom-call | flops 1 | bytes 1 | tf_op jit(solution)/shard_map/feed_forward/pallas_call | solution.py:304
  344.8 47.6 %feed_forward.3 = (bf16[4,512,512]{2,1,0:T(8,128)(2,1)}, bf16[2,512,512]{2,1,0:T(8,128)(2,1)}, bf16[512,512]{1,0:T(8,128)(2,1)}, bf16[512,512]{1,0:T(8,128)(2,1)...) custom-call(s32[2]{0:T(128)} %copy-done.89, ...), custom_call_target="tpu_custom_call" | custom-call | flops 1 | bytes 1 | tf_op jit(solution)/shard_map/feed_forward/pallas_call | solution.py:304
  392.4 8.5 %reduce-scatter.3.cloned.1.call-done = bf16[1,512,512]{2,1,0:T(8,128)(2,1)} async-done(((bf16[4,512,512]{2,1,0:T(8,128)(2,1)}), bf16[1,512,512]{2,1,0:T(8,128)(2,1)}) %reduce-scatter.3.cloned.1.call-update) | async-done | bytes 524304 | tf_op jit(solution)/shard_map/reduce_scatter | solution.py:223
  407.7 39.1 %collective-permute-done.9.refs_2_ = bf16[2,512,512]{2,1,0:T(8,128)(2,1)S(1)} collective-permute-done((bf16[2,512,512]{2,1,0:T(8,128)(2,1)S(1)}, bf16[2,512,512]{2,1,0:T(8,128)(2,1)S(1)}, u32[]{:S(2)}, u32[]{:S(2)}) %collective-permute-start.9) | collective-permute-done | bytes 1048608 | tf_op jit(solution)/shard_map/ppermute | solution.py:226
  456.6 29.8 %collective-permute-done.12.refs_5_ = bf16[512,512]{1,0:T(8,128)(2,1)S(1)} collective-permute-done((bf16[512,512]{1,0:T(8,128)(2,1)S(1)}, bf16[512,512]{1,0:T(8,128)(2,1)S(1)}, u32[]{:S(2)}, u32[]{:S(2)}) %collective-permute-start.12) | collective-permute-done | bytes 524320 | tf_op jit(solution)/shard_map/ppermute | solution.py:245
  489.2 19.9 %attend_back.2 = (f32[512,512]{1,0:T(8,128)}, f32[512,512]{1,0:T(8,128)}, f32[512,512]{1,0:T(8,128)}, f32[16,512]{1,0:T(8,128)}, f32[16,2048]{1,0:T(8,128)}) custom-call(s32[2]{0:T(128)} %copy-done.89, bf16[4,512,512]{2,1,0:T(8,128)(2,1)} %bitcast.52, bf16[3,512,512]{2,1,0:T(8,128)(2,1)} %copy-done, bf16[3,512,512]{2,1,0:T(8,128)(2,1)} %copy-done, ...), custom_call_target="tpu_custom_call" | custom-call | flops 1 | bytes 1 | tf_op jit(solution)/shard_map/attend_back/pallas_call | solution.py:304
  514.7 18.7 %all-gather.23.cloned.1.call-done = bf16[2048,512]{1,0:T(8,128)(2,1)} async-done(((bf16[512,512]{1,0:T(8,128)(2,1)}), bf16[2048,512]{1,0:T(8,128)(2,1)}) %all-gather.23.cloned.1.call-update) | async-done | bytes 2097168 | tf_op jit(solution)/shard_map/all_gather | solution.py:71
  538.2 24.9 %attend_back.3 = (f32[512,512]{1,0:T(8,128)}, f32[1024,512]{1,0:T(8,128)}, f32[1024,512]{1,0:T(8,128)}, f32[16,512]{1,0:T(8,128)}, f32[16,2048]{1,0:T(8,128)}) custom-call(s32[2]{0:T(128)} %copy-done.89, bf16[4,512,512]{2,1,0:T(8,128)(2,1)} %bitcast.39, bf16[3,512,512]{2,1,0:T(8,128)(2,1)} %copy-done, bf16[3,512,512]{2,1,0:T(8,128)(2,1)} %copy-done, ...), custom_call_target="tpu_custom_call" | custom-call | flops 1 | bytes 1 | tf_op jit(solution)/shard_map/attend_back/pallas_call | solution.py:304
  606.7 13.3 %project_back.2 = (bf16[2,512,512]{2,1,0:T(8,128)(2,1)}, bf16[512,512]{1,0:T(8,128)(2,1)}, bf16[512,512]{1,0:T(8,128)(2,1)}) custom-call(s32[2]{0:T(128)} %copy-done.89, bf16[3,1024,512]{2,1,0:T(8,128)(2,1)} %copy-done.13, bf16[3,1024,16]{2,1,0:T(8,128)(2,1)} %copy-done.24, bf16[3,2048,512]{2,1,0:T(8,128)(2,1)} %refs_3_.3, ...), custom_call_target="tpu_custom_call" | custom-call | flops 1 | bytes 1 | tf_op jit(solution)/shard_map/project_back/pallas_call | solution.py:304
  623.6 5.9 collective-permute-start.26
  629.6 13.5 %project_back.3 = (bf16[2,512,512]{2,1,0:T(8,128)(2,1)}, bf16[512,512]{1,0:T(8,128)(2,1)}, bf16[512,512]{1,0:T(8,128)(2,1)}) custom-call(s32[2]{0:T(128)} %copy-done.89, bf16[3,1024,512]{2,1,0:T(8,128)(2,1)} %copy-done.13, bf16[3,1024,16]{2,1,0:T(8,128)(2,1)} %copy-done.24, bf16[3,2048,512]{2,1,0:T(8,128)(2,1)} %refs_3_.3, ...), custom_call_target="tpu_custom_call" | custom-call | flops 1 | bytes 1 | tf_op jit(solution)/shard_map/project_back/pallas_call | solution.py:304
  647.2 5.9 collective-permute-done.26.refs_2_
  656.6 19.1 %collective-permute-done.25.refs_2_ = bf16[2,512,512]{2,1,0:T(8,128)(2,1)S(1)} collective-permute-done((bf16[2,512,512]{2,1,0:T(8,128)(2,1)}, bf16[2,512,512]{2,1,0:T(8,128)(2,1)S(1)}, u32[]{:S(2)}, u32[]{:S(2)}) %collective-permute-start.25) | collective-permute-done | bytes 1048608 | tf_op jit(solution)/shard_map/ppermute | solution.py:226
  694.5 7.0 combine.1
  (337 shorter events, 167.9 us)
Async XLA Ops:
  7.2 85.9 %all-gather.13.cloned.1.call-start = ((), (), s32[]{:S(2)}) async-start(), calls=%async_computation.2 | async-start | bytes 5242880 | tf_op jit(solution)/shard_map/all_gather | solution.py:71
  7.9 285.9 %all-gather.15.cloned.1.call-start = ((), (), s32[]{:S(2)}) async-start(), calls=%async_computation.3 | async-start | bytes 5242880 | tf_op jit(solution)/shard_map/all_gather | solution.py:71
  8.7 285.1 %all-gather.17.cloned.1.call-start = ((), (), s32[]{:S(2)}) async-start(), calls=%async_computation.6 | async-start | bytes 2621440 | tf_op jit(solution)/shard_map/all_gather | solution.py:71
  123.4 47.0 %collective-permute-start = (bf16[2,512,512]{2,1,0:T(8,128)(2,1)S(1)}, bf16[2,512,512]{2,1,0:T(8,128)(2,1)S(1)}, u32[]{:S(2)}, u32[]{:S(2)}) collective-permute-start(bf16[2,512,512]{2,1,0:T(8,128)(2,1)S(1)} %get-tuple-element.104.refs_1_), channel_id=1, source_target_pairs={{0,1},{3,2},{4,5},{7,6},{8,9},{11,10},{12,13},{15,14},{16,17},{19,... | collective-permute-start | bytes 3145736 | tf_op jit(solution)/shard_map/ppermute | solution.py:226
  172.1 38.1 %collective-permute-start.3 = (bf16[512,512]{1,0:T(8,128)(2,1)S(1)}, bf16[512,512]{1,0:T(8,128)(2,1)S(1)}, u32[]{:S(2)}, u32[]{:S(2)}) collective-permute-start(bf16[512,512]{1,0:T(8,128)(2,1)S(1)} %get-tuple-element.109), channel_id=1, source_target_pairs={{1,3},{2,0},{5,7},{6,4},{9,11},{10,8},{13,15},{14,12},{17,19},{18,... | collective-permute-start | bytes 1572872 | tf_op jit(solution)/shard_map/ppermute | solution.py:245
  173.4 36.8 %collective-permute-start.1 = (bf16[512,512]{1,0:T(8,128)(2,1)S(1)}, bf16[512,512]{1,0:T(8,128)(2,1)S(1)}, u32[]{:S(2)}, u32[]{:S(2)}) collective-permute-start(bf16[512,512]{1,0:T(8,128)(2,1)S(1)} %get-tuple-element.107.refs_12_), channel_id=1, source_target_pairs={{0,1},{1,0},{2,3},{3,2},{4,5},{5,4},{6,7},{7,6},{8,9},{9,8},{10,11... | collective-permute-start | bytes 1572872 | tf_op jit(solution)/shard_map/ppermute | solution.py:246
  212.8 132.0 %all-gather.19.cloned.1.call-start = ((), (), s32[]{:S(2)}) async-start(), calls=%async_computation.7 | async-start | bytes 2621440 | tf_op jit(solution)/shard_map/all_gather | solution.py:71
  212.8 42.7 %collective-permute-start.4 = (bf16[2,512,512]{2,1,0:T(8,128)(2,1)}, bf16[2,512,512]{2,1,0:T(8,128)(2,1)S(1)}, u32[]{:S(2)}, u32[]{:S(2)}) collective-permute-start(bf16[2,512,512]{2,1,0:T(8,128)(2,1)} %copy-done.53), channel_id=1, source_target_pairs={{0,1},{3,2},{4,5},{7,6},{8,9},{11,10},{12,13},{15,14},{16,17},{19,... | collective-permute-start | bytes 3145736 | tf_op jit(solution)/shard_map/ppermute | solution.py:226
  258.4 32.6 %collective-permute-start.7 = (bf16[512,512]{1,0:T(8,128)(2,1)S(1)}, bf16[512,512]{1,0:T(8,128)(2,1)S(1)}, u32[]{:S(2)}, u32[]{:S(2)}) collective-permute-start(bf16[512,512]{1,0:T(8,128)(2,1)S(1)} %get-tuple-element.118), channel_id=1, source_target_pairs={{1,3},{2,0},{5,7},{6,4},{9,11},{10,8},{13,15},{14,12},{17,19},{18,... | collective-permute-start | bytes 1572872 | tf_op jit(solution)/shard_map/ppermute | solution.py:245
  259.7 31.3 %collective-permute-start.5 = (bf16[512,512]{1,0:T(8,128)(2,1)S(1)}, bf16[512,512]{1,0:T(8,128)(2,1)S(1)}, u32[]{:S(2)}, u32[]{:S(2)}) collective-permute-start(bf16[512,512]{1,0:T(8,128)(2,1)S(1)} %get-tuple-element.116.refs_6_), channel_id=1, source_target_pairs={{0,1},{1,0},{2,3},{3,2},{4,5},{5,4},{6,7},{7,6},{8,9},{9,8},{10,11... | collective-permute-start | bytes 1572872 | tf_op jit(solution)/shard_map/ppermute | solution.py:246
  293.7 107.2 %reduce-scatter.3.cloned.1.call-start = ((), (), s32[]{:S(2)}) async-start(), calls=%async_computation.4 | async-start | bytes 2621440 | tf_op jit(solution)/shard_map/reduce_scatter | solution.py:223
  340.9 148.3 %all-gather.21.cloned.1.call-start = ((), (), s32[]{:S(2)}) async-start(), calls=%async_computation.8 | async-start | bytes 2621440 | tf_op jit(solution)/shard_map/all_gather | solution.py:71
  342.1 50.3 %collective-permute-start.8 = (bf16[2,512,512]{2,1,0:T(8,128)(2,1)S(1)}, bf16[2,512,512]{2,1,0:T(8,128)(2,1)S(1)}, u32[]{:S(2)}, u32[]{:S(2)}) collective-permute-start(bf16[2,512,512]{2,1,0:T(8,128)(2,1)S(1)} %copy-done.49), channel_id=1, source_target_pairs={{0,1},{3,2},{4,5},{7,6},{8,9},{11,10},{12,13},{15,14},{16,17},{19,... | collective-permute-start | bytes 3145736 | tf_op jit(solution)/shard_map/ppermute | solution.py:226
  405.4 128.0 %all-gather.23.cloned.1.call-start = ((), (), s32[]{:S(2)}) async-start(), calls=%async_computation.9 | async-start | bytes 2621440 | tf_op jit(solution)/shard_map/all_gather | solution.py:71
  405.4 41.4 %collective-permute-start.9 = (bf16[2,512,512]{2,1,0:T(8,128)(2,1)S(1)}, bf16[2,512,512]{2,1,0:T(8,128)(2,1)S(1)}, u32[]{:S(2)}, u32[]{:S(2)}) collective-permute-start(bf16[2,512,512]{2,1,0:T(8,128)(2,1)S(1)} %copy-done.55), channel_id=1, source_target_pairs={{0,1},{3,2},{4,5},{7,6},{8,9},{11,10},{12,13},{15,14},{16,17},{19,... | collective-permute-start | bytes 3145736 | tf_op jit(solution)/shard_map/ppermute | solution.py:226
  449.6 36.9 %collective-permute-start.12 = (bf16[512,512]{1,0:T(8,128)(2,1)S(1)}, bf16[512,512]{1,0:T(8,128)(2,1)S(1)}, u32[]{:S(2)}, u32[]{:S(2)}) collective-permute-start(bf16[512,512]{1,0:T(8,128)(2,1)S(1)} %get-tuple-element.133), channel_id=1, source_target_pairs={{1,3},{2,0},{5,7},{6,4},{9,11},{10,8},{13,15},{14,12},{17,19},{18,... | collective-permute-start | bytes 1572872 | tf_op jit(solution)/shard_map/ppermute | solution.py:245
  450.9 35.6 %collective-permute-start.10 = (bf16[512,512]{1,0:T(8,128)(2,1)S(1)}, bf16[512,512]{1,0:T(8,128)(2,1)S(1)}, u32[]{:S(2)}, u32[]{:S(2)}) collective-permute-start(bf16[512,512]{1,0:T(8,128)(2,1)S(1)} %get-tuple-element.131.refs_6_), channel_id=1, source_target_pairs={{0,1},{1,0},{2,3},{3,2},{4,5},{5,4},{6,7},{7,6},{8,9},{9,8},{10,11... | collective-permute-start | bytes 1572872 | tf_op jit(solution)/shard_map/ppermute | solution.py:246
  489.1 117.6 %reduce-scatter.5.cloned.1.call-start = ((), (), s32[]{:S(2)}) async-start(), calls=%async_computation.5 | async-start | bytes 2621440 | tf_op jit(solution)/shard_map/reduce_scatter | solution.py:223
  538.0 153.7 %all-gather.25.cloned.1.call-start = ((), (), s32[]{:S(2)}) async-start(), calls=%async_computation.10 | async-start | bytes 7077888 | tf_op jit(solution)/shard_map/all_gather | solution.py:1063
  643.1 32.6 %collective-permute-start.25 = (bf16[2,512,512]{2,1,0:T(8,128)(2,1)}, bf16[2,512,512]{2,1,0:T(8,128)(2,1)S(1)}, u32[]{:S(2)}, u32[]{:S(2)}) collective-permute-start(bf16[2,512,512]{2,1,0:T(8,128)(2,1)} %get-tuple-element.172.refs_1_), channel_id=1, source_target_pairs={{0,1},{3,2},{4,5},{7,6},{8,9},{11,10},{12,13},{15,14},{16,17},{19,... | collective-permute-start | bytes 3145736 | tf_op jit(solution)/shard_map/ppermute | solution.py:226
  644.4 35.4 %collective-permute-start.14 = (bf16[512,512]{1,0:T(8,128)(2,1)}, bf16[512,512]{1,0:T(8,128)(2,1)S(1)}, u32[]{:S(2)}, u32[]{:S(2)}) collective-permute-start(bf16[512,512]{1,0:T(8,128)(2,1)} %get-tuple-element.137), channel_id=1, source_target_pairs={{1,2},{2,1},{5,6},{6,5},{9,10},{10,9},{13,14},{14,13},{17,18},{18,... | collective-permute-start | bytes 1572872 | tf_op jit(solution)/shard_map/ppermute | solution.py:244
  645.1 41.8 %collective-permute-start.13 = (bf16[512,512]{1,0:T(8,128)(2,1)}, bf16[512,512]{1,0:T(8,128)(2,1)S(1)}, u32[]{:S(2)}, u32[]{:S(2)}) collective-permute-start(bf16[512,512]{1,0:T(8,128)(2,1)} %copy-done.87), channel_id=1, source_target_pairs={{0,1},{1,0},{2,3},{3,2},{4,5},{5,4},{6,7},{7,6},{8,9},{9,8},{10,11... | collective-permute-start | bytes 1572872 | tf_op jit(solution)/shard_map/ppermute | solution.py:246
  645.9 35.2 %collective-permute-start.15 = (bf16[512,512]{1,0:T(8,128)(2,1)}, bf16[512,512]{1,0:T(8,128)(2,1)S(1)}, u32[]{:S(2)}, u32[]{:S(2)}) collective-permute-start(bf16[512,512]{1,0:T(8,128)(2,1)} %copy-done.108), channel_id=1, source_target_pairs={{1,3},{2,0},{5,7},{6,4},{9,11},{10,8},{13,15},{14,12},{17,19},{18,... | collective-permute-start | bytes 1572872 | tf_op jit(solution)/shard_map/ppermute | solution.py:245
  655.9 32.3 %collective-permute-start.28 = (bf16[512,512]{1,0:T(8,128)(2,1)S(1)}, bf16[512,512]{1,0:T(8,128)(2,1)S(1)}, u32[]{:S(2)}, u32[]{:S(2)}) collective-permute-start(bf16[512,512]{1,0:T(8,128)(2,1)S(1)} %get-tuple-element.183), channel_id=1, source_target_pairs={{1,2},{2,1},{5,6},{6,5},{9,10},{10,9},{13,14},{14,13},{17,18},{18,... | collective-permute-start | bytes 1572872 | tf_op jit(solution)/shard_map/ppermute | solution.py:244
  (131 other events, 2197.0 us)
Sparse Core Ops, SparseCore 0:
  9.6 83.4 all-gather.12
  94.7 108.7 all-gather.14
  212.9 66.6 all-gather.16
  293.8 45.4 all-gather.18
  342.1 58.8 reduce-scatter.2
  405.5 67.5 all-gather.20
  489.2 44.1 all-gather.22
  538.2 42.5 reduce-scatter.4
  623.7 47.0 all-gather.24
